TPU v7x, 32 devices: a whole 2x2x4 slice. The times are simulated.
32 devices in a mesh: gx: 8 (over y, x, core), gy: 4 (over z).
Axes of the slice: x: 2, y: 2, z: 4, core: 2. Of those that a mesh axis runs over, the one named last changes fastest.
Arguments:
- offsets: float32 [3, 32, 32, 256], P(None, 'gx', 'gy'), may hold values from -0.5 to 0.5
- strengths: float32 [3, 32, 32, 256], P(None, 'gx', 'gy'), may hold values from -6 to 6
- counts: int32 [32, 32, 2], P('gx', 'gy'), may hold values from 64 to 128, as said below
- check_inverse: float32 [121, 121], replicated, may hold values from -1 to 1
Outputs:
- field: float32 [12, 32, 32, 256], P(None, 'gx', 'gy')
Inputs may be any that keep to these rules, and one draw needn't show every extreme that they name: `counts`: A leaf's live particles fill its first slots; in each block of 4 x 8 x 2 leaves that one device holds, one leaf is full.
All inputs are finite; a program needn't handle non-finite values.
Results may differ from a plain program's by a relative error of at most 0.0003.
Values sent between devices are 32-bit elements; how exact they have to be, the bound alone decides.
No kernel may reach another device: no remote copies, remote signals or barrier semaphores. Data moves between devices by JAX's collectives and lax.ppermute only.
A program may use at most 192 MiB of HBM per device.

v0:
```python
import math

import jax
import jax.numpy as jnp
from jax import lax
from jax.sharding import PartitionSpec as P

SMOOTH2 = 0.01
STRENGTH_SCALE = 0.03
GOLDEN = math.pi * (3.0 - math.sqrt(5.0))
HIGHEST = lax.Precision.HIGHEST


def extended(cells, sides, width):
    for axis, dim in sides:
        count = lax.axis_size(axis)
        ends = count - 1
        head = lax.slice_in_dim(cells, 0, width, axis=dim)
        tail = lax.slice_in_dim(cells, cells.shape[dim] - width, cells.shape[dim], axis=dim)
        cells = jnp.concatenate(
            [
                lax.ppermute(tail, axis, [(i, (i + 1) % count) for i in range(ends)]),
                cells,
                lax.ppermute(head, axis, [((i + 1) % count, i) for i in range(ends)]),
            ],
            axis=dim,
        )
    return cells


def sphere_points(amount):
    counter = jnp.arange(amount).astype(jnp.float32)
    height = 1.0 - (2.0 * counter + 1.0) / amount
    radius = jnp.sqrt(jnp.maximum(1.0 - height * height, 0.0))
    azimuth = counter * GOLDEN
    return jnp.stack([radius * jnp.cos(azimuth), radius * jnp.sin(azimuth), height])


def kernel_of(vector):
    return lax.rsqrt(jnp.sum(vector * vector, axis=0) + SMOOTH2)


def translation(displacement, target_radius, source_radius, points):
    offset = jnp.array(displacement, dtype=jnp.float32)
    vector = (
        offset[:, None, None]
        + target_radius * points[:, :, None]
        - source_radius * points[:, None, :]
    )
    return kernel_of(vector)


def child_tables(points, target_radius, source_radius, direction):
    tables = []
    for corner_x in range(2):
        for corner_y in range(2):
            for corner_z in range(2):
                displacement = [
                    direction * (corner_x - 0.5),
                    direction * (corner_y - 0.5),
                    direction * (corner_z - 0.5),
                ]
                tables.append(translation(displacement, target_radius, source_radius, points))
    return jnp.stack(tables)


def parent_near(counter, displacement):
    return (jnp.abs((counter + displacement) // 2 - counter // 2) <= 1).astype(jnp.float32)


def apply_inverse(matrix, operand):
    return jnp.dot(matrix, operand.reshape(operand.shape[0], -1), precision=HIGHEST).reshape(
        operand.shape
    )


def top_block(charges, source_x, source_y, target_x, target_y, within):
    gap_x = target_x[:, None] - source_x[None, :]
    gap_y = target_y[:, None] - source_y[None, :]
    distant_mask = ((jnp.abs(gap_x) >= 2) | (jnp.abs(gap_y) >= 2)).astype(jnp.float32)
    along_x = 1.8 * within[0][:, None, :, None] + 2.0 * gap_x.astype(jnp.float32)[None, :, None, :]
    along_y = 1.8 * within[1][:, None, :, None] + 2.0 * gap_y.astype(jnp.float32)[None, :, None, :]
    along_z = 1.8 * within[2][:, None, :, None]
    weight = (
        lax.rsqrt(along_x * along_x + along_y * along_y + along_z * along_z + SMOOTH2)
        * distant_mask[None, :, None, :]
    )
    return jnp.einsum("ktmb,mcb->kct", weight, charges, precision=HIGHEST)


def accumulate(potential, gradient, vector, weighted, inverse):
    cubed = weighted * inverse[None] * inverse[None]
    potential = potential + jnp.sum(weighted, axis=-1)
    parts = [jnp.sum(vector[axis_number][None] * cubed, axis=-1) for axis_number in range(3)]
    gradient = gradient - jnp.stack(parts, axis=1)
    return (potential, gradient)


def evaluate(target, local_eq, source_places, source_charge, points):
    shape = target.shape[1:]
    potential = jnp.zeros((3,) + shape, jnp.float32)
    gradient = jnp.zeros((3, 3) + shape, jnp.float32)

    def one_shift(index, carry):
        shift_x = index // 9 - 1
        shift_y = index // 3 % 3 - 1
        shift_z = index % 3 - 1
        zero = jnp.zeros((), jnp.int32)
        start = (zero, shift_x + 1, shift_y + 1, shift_z + 1, zero)
        source = lax.dynamic_slice(source_places, start, (3,) + shape)
        weight = lax.dynamic_slice(source_charge, start, (3,) + shape)
        offset = jnp.stack([shift_x, shift_y, shift_z]).astype(jnp.float32)
        vector = (
            target[..., :, None] - source[..., None, :] - offset[:, None, None, None, None, None]
        )
        inverse = kernel_of(vector)
        weighted = inverse[None] * weight[..., None, :]
        return accumulate(carry[0], carry[1], vector, weighted, inverse)

    potential, gradient = lax.fori_loop(0, 27, one_shift, (potential, gradient))
    vector = target[..., None] - 1.5 * points[:, None, None, None, None, :]
    inverse = kernel_of(vector)
    weighted = inverse[None] * jnp.moveaxis(local_eq, 0, -1)[..., None, :]
    potential, gradient = accumulate(potential, gradient, vector, weighted, inverse)
    return jnp.concatenate([potential, gradient.reshape((9,) + shape)], axis=0)


def body(offsets, strengths, counts, check_inverse):
    size_x, size_y, depth = counts.shape
    slots_per = offsets.shape[3] // depth
    expansion = check_inverse.shape[0]
    half_x = size_x // 2
    half_y = size_y // 2
    top_boxes = half_x * half_y
    points = sphere_points(expansion)
    within = points[:, :, None] - points[:, None, :]
    slot_index = jnp.arange(slots_per)
    living = (slot_index[None, None, None, :] < counts[:, :, :, None]).astype(jnp.float32)
    places = offsets.reshape(3, size_x, size_y, depth, slots_per)
    charge = STRENGTH_SCALE * strengths.reshape(3, size_x, size_y, depth, slots_per) * living[None]
    vector = 1.5 * points[:, :, None, None, None, None] - places[:, None]
    upward = jnp.einsum("kxyzp,cxyzp->kcxyz", kernel_of(vector), charge, precision=HIGHEST)
    leaf_charges = 0.5 * apply_inverse(check_inverse, upward)
    grouped = (
        leaf_charges.reshape(expansion, 3, half_x, 2, half_y, 2, 2)
        .transpose(3, 5, 6, 0, 1, 2, 4)
        .reshape(8, expansion, 3 * top_boxes)
    )
    top_check = jnp.einsum(
        "ckm,cmt->kt", child_tables(points, 3.0, 0.9, -1.0), grouped, precision=HIGHEST
    )
    top_charges = apply_inverse(check_inverse, top_check.reshape(expansion, 3, top_boxes))
    lanes_y = lax.axis_size("gy")
    column_index = jnp.arange(top_boxes)
    my_x = lax.axis_index("gx") * half_x + column_index // half_y
    my_y = lax.axis_index("gy") * half_y + column_index % half_y
    running = jnp.zeros((expansion, 3, top_boxes), jnp.float32)
    shard_part = lax.all_gather(top_charges, ("gx", "gy"), axis=2, tiled=True)
    amount = shard_part.shape[2]
    block_size = math.gcd(amount, 16)
    flat = jnp.arange(amount)
    device = flat // top_boxes
    inside = flat % top_boxes
    source_x = device // lanes_y * half_x + inside // half_y
    source_y = device % lanes_y * half_y + inside % half_y
    pieces = jnp.moveaxis(shard_part.reshape(expansion, 3, amount // block_size, block_size), 2, 0)

    def advance(carry, element):
        return (carry + top_block(element[0], element[1], element[2], my_x, my_y, within), None)

    running, unused = lax.scan(
        advance,
        running,
        (pieces, source_x.reshape(-1, block_size), source_y.reshape(-1, block_size)),
    )
    top_local = apply_inverse(check_inverse, running)
    spread = jnp.einsum(
        "ckm,mt->ckt",
        child_tables(points, 0.9, 3.0, 1.0),
        top_local.reshape(expansion, -1),
        precision=HIGHEST,
    )
    inherited = (
        spread.reshape(2, 2, 2, expansion, 3, half_x, half_y)
        .transpose(3, 4, 5, 0, 6, 1, 2)
        .reshape(expansion, 3, size_x, size_y, depth)
    )
    border = extended(leaf_charges, (("gx", 2), ("gy", 3)), 3)
    border = jnp.pad(border, ((0, 0), (0, 0), (0, 0), (0, 0), (1, 1)))
    local_x = jnp.arange(size_x)
    local_y = jnp.arange(size_y)
    distant = jnp.zeros((expansion, 3 * size_x * size_y * depth), jnp.float32)
    for shift_x in range(-3, 4):
        tables = []
        sources = []
        for shift_y in range(-3, 4):
            if abs(shift_x) < 2 and abs(shift_y) < 2:
                continue
            parent_mask = (
                parent_near(local_x, shift_x)[:, None, None]
                * parent_near(local_y, shift_y)[None, :, None]
            )
            for shift_z in range(-1, 2):
                tables.append(translation([-shift_x, -shift_y, -shift_z], 0.9, 0.9, points))
                source = (
                    border[
                        :,
                        :,
                        3 + shift_x : 3 + shift_x + size_x,
                        3 + shift_y : 3 + shift_y + size_y,
                        1 + shift_z : 1 + shift_z + depth,
                    ]
                    * parent_mask
                )
                sources.append(source.reshape(expansion, -1))
        distant = distant + jnp.dot(
            jnp.concatenate(tables, axis=1), jnp.concatenate(sources, axis=0), precision=HIGHEST
        )
    leaf_down = distant.reshape(expansion, 3, size_x, size_y, depth) + inherited
    leaf_local = 0.5 * apply_inverse(check_inverse, leaf_down)
    stacked = jnp.concatenate(
        [offsets, charge.reshape(3, size_x, size_y, depth * slots_per)], axis=0
    )
    neighbours = extended(stacked, (("gx", 1), ("gy", 2)), 1)
    neighbours = jnp.pad(
        neighbours.reshape(6, size_x + 2, size_y + 2, depth, slots_per),
        ((0, 0), (0, 0), (0, 0), (1, 1), (0, 0)),
    )
    result_field = (
        evaluate(places, leaf_local, neighbours[:3], neighbours[3:], points) * living[None]
    )
    return result_field.reshape(12, size_x, size_y, depth * slots_per)


def solution(mesh):
    return jax.shard_map(
        body,
        mesh=mesh,
        in_specs=(P(None, "gx", "gy", None), P(None, "gx", "gy", None), P("gx", "gy", None), P()),
        out_specs=P(None, "gx", "gy", None),
        check_vma=False,
    )
```

profile of v0, /device:TPU:0, one launch (start us, length us, event | category | flops | bytes accessed | tf_op | source)
XLA Modules:
  0.0 1393.3 jit_solution(9604315068000600718)
XLA Ops:
  121.2 73.0 %all_gather.3 = f32[121,3,256]{0,2,1:T(8,128)S(1)} all-gather(f32[121,3,8]{0,2,1:T(8,128)S(1)} %convolution_bitcast_fusion.1), channel_id=1, replica_groups=mesh['gx'=8,'gy'=4] {'gx','gy'}, dimensions={2}, use_global_device_ids=true | all-gather | bytes 383328 | tf_op jit(solution)/shard_map/all_gather | solution.py:158
  194.6 149.9 %while.33 = (s32[]{:T(128)}, f32[121,3,8]{0,1,2:T(4,128)S(1)}, f32[16,121,3,16]{1,2,3,0:T(4,128)S(1)}, f32[3,121,121]{2,1,0:T(8,128)S(1)}, s32[16,16]{1,0:T(8,12...) while((s32[]{:T(128)}, f32[121,3,8]{0,1,2:T(4,128)S(1)}, ...), condition=%wide.region_146.147_spmd.clone, body=%wide.region_145.146_spmd.clone.sunk | while | flops 82524392 | bytes 623415 | solution.py:171
  393.3 936.2 %while.32 = (s32[]{:T(128)}, f32[3,4,8,2,128]{4,3,2,1,0:T(2,128)S(1)}, f32[3,3,4,8,2,128]{5,4,3,2,0,1:T(2,128)S(1)}, f32[3,4,8,256]{3,2,1,0:T(8,128)S(1)}, f32[3...) while((s32[]{:T(128)}, ...), condition=%wide.region_6.0_spmd.clone, body=%wide.region_0.6_spmd.clone.sunk | while | flops 44286000 | bytes 103121512 | solution.py:120
  412.7 14.8 %fusion.136 = (f32[3,4,8,2,128]{4,3,2,1,0:T(2,128)S(1)}, f32[3,4,8,2,128]{4,3,2,1,0:T(2,128)S(1)}, f32[3,4,8,2,128]{4,3,2,1,0:T(2,128)S(1)}, f32[3,4,8,2,128]{4,3,2,1,0:T(2,128)S(1)}) fusion(f32[4,8,2,128,128]{4,3,2,1,0:T(8,128)S(1)} %copy-done.2, f32[4,8,2,128,128]{4,3,2,1,0:T(8,128)S(1)} %add_rsqrt_fusion.124, ...), kind=kLoop, calls=%fused_computation.8.clone.1 | loop fusion | flops 31358976 | bytes 17268736 | tf_op jit(solution)/shard_map/while/body/eval_jaxpr/reduce_sum | solution.py:94
  447.4 14.8 %fusion.136 = (f32[3,4,8,2,128]{4,3,2,1,0:T(2,128)S(1)}, f32[3,4,8,2,128]{4,3,2,1,0:T(2,128)S(1)}, f32[3,4,8,2,128]{4,3,2,1,0:T(2,128)S(1)}, f32[3,4,8,2,128]{4,3,2,1,0:T(2,128)S(1)}) fusion(f32[4,8,2,128,128]{4,3,2,1,0:T(8,128)S(1)} %copy-done.2, f32[4,8,2,128,128]{4,3,2,1,0:T(8,128)S(1)} %add_rsqrt_fusion.124, ...), kind=kLoop, calls=%fused_computation.8.clone.1 | loop fusion | flops 31358976 | bytes 17268736 | tf_op jit(solution)/shard_map/while/body/eval_jaxpr/reduce_sum | solution.py:94
  482.1 14.8 %fusion.136 = (f32[3,4,8,2,128]{4,3,2,1,0:T(2,128)S(1)}, f32[3,4,8,2,128]{4,3,2,1,0:T(2,128)S(1)}, f32[3,4,8,2,128]{4,3,2,1,0:T(2,128)S(1)}, f32[3,4,8,2,128]{4,3,2,1,0:T(2,128)S(1)}) fusion(f32[4,8,2,128,128]{4,3,2,1,0:T(8,128)S(1)} %copy-done.2, f32[4,8,2,128,128]{4,3,2,1,0:T(8,128)S(1)} %add_rsqrt_fusion.124, ...), kind=kLoop, calls=%fused_computation.8.clone.1 | loop fusion | flops 31358976 | bytes 17268736 | tf_op jit(solution)/shard_map/while/body/eval_jaxpr/reduce_sum | solution.py:94
  516.8 14.8 %fusion.136 = (f32[3,4,8,2,128]{4,3,2,1,0:T(2,128)S(1)}, f32[3,4,8,2,128]{4,3,2,1,0:T(2,128)S(1)}, f32[3,4,8,2,128]{4,3,2,1,0:T(2,128)S(1)}, f32[3,4,8,2,128]{4,3,2,1,0:T(2,128)S(1)}) fusion(f32[4,8,2,128,128]{4,3,2,1,0:T(8,128)S(1)} %copy-done.2, f32[4,8,2,128,128]{4,3,2,1,0:T(8,128)S(1)} %add_rsqrt_fusion.124, ...), kind=kLoop, calls=%fused_computation.8.clone.1 | loop fusion | flops 31358976 | bytes 17268736 | tf_op jit(solution)/shard_map/while/body/eval_jaxpr/reduce_sum | solution.py:94
  551.4 14.8 %fusion.136 = (f32[3,4,8,2,128]{4,3,2,1,0:T(2,128)S(1)}, f32[3,4,8,2,128]{4,3,2,1,0:T(2,128)S(1)}, f32[3,4,8,2,128]{4,3,2,1,0:T(2,128)S(1)}, f32[3,4,8,2,128]{4,3,2,1,0:T(2,128)S(1)}) fusion(f32[4,8,2,128,128]{4,3,2,1,0:T(8,128)S(1)} %copy-done.2, f32[4,8,2,128,128]{4,3,2,1,0:T(8,128)S(1)} %add_rsqrt_fusion.124, ...), kind=kLoop, calls=%fused_computation.8.clone.1 | loop fusion | flops 31358976 | bytes 17268736 | tf_op jit(solution)/shard_map/while/body/eval_jaxpr/reduce_sum | solution.py:94
  586.1 14.8 %fusion.136 = (f32[3,4,8,2,128]{4,3,2,1,0:T(2,128)S(1)}, f32[3,4,8,2,128]{4,3,2,1,0:T(2,128)S(1)}, f32[3,4,8,2,128]{4,3,2,1,0:T(2,128)S(1)}, f32[3,4,8,2,128]{4,3,2,1,0:T(2,128)S(1)}) fusion(f32[4,8,2,128,128]{4,3,2,1,0:T(8,128)S(1)} %copy-done.2, f32[4,8,2,128,128]{4,3,2,1,0:T(8,128)S(1)} %add_rsqrt_fusion.124, ...), kind=kLoop, calls=%fused_computation.8.clone.1 | loop fusion | flops 31358976 | bytes 17268736 | tf_op jit(solution)/shard_map/while/body/eval_jaxpr/reduce_sum | solution.py:94
  620.8 14.8 %fusion.136 = (f32[3,4,8,2,128]{4,3,2,1,0:T(2,128)S(1)}, f32[3,4,8,2,128]{4,3,2,1,0:T(2,128)S(1)}, f32[3,4,8,2,128]{4,3,2,1,0:T(2,128)S(1)}, f32[3,4,8,2,128]{4,3,2,1,0:T(2,128)S(1)}) fusion(f32[4,8,2,128,128]{4,3,2,1,0:T(8,128)S(1)} %copy-done.2, f32[4,8,2,128,128]{4,3,2,1,0:T(8,128)S(1)} %add_rsqrt_fusion.124, ...), kind=kLoop, calls=%fused_computation.8.clone.1 | loop fusion | flops 31358976 | bytes 17268736 | tf_op jit(solution)/shard_map/while/body/eval_jaxpr/reduce_sum | solution.py:94
  655.4 14.8 %fusion.136 = (f32[3,4,8,2,128]{4,3,2,1,0:T(2,128)S(1)}, f32[3,4,8,2,128]{4,3,2,1,0:T(2,128)S(1)}, f32[3,4,8,2,128]{4,3,2,1,0:T(2,128)S(1)}, f32[3,4,8,2,128]{4,3,2,1,0:T(2,128)S(1)}) fusion(f32[4,8,2,128,128]{4,3,2,1,0:T(8,128)S(1)} %copy-done.2, f32[4,8,2,128,128]{4,3,2,1,0:T(8,128)S(1)} %add_rsqrt_fusion.124, ...), kind=kLoop, calls=%fused_computation.8.clone.1 | loop fusion | flops 31358976 | bytes 17268736 | tf_op jit(solution)/shard_map/while/body/eval_jaxpr/reduce_sum | solution.py:94
  690.1 14.8 %fusion.136 = (f32[3,4,8,2,128]{4,3,2,1,0:T(2,128)S(1)}, f32[3,4,8,2,128]{4,3,2,1,0:T(2,128)S(1)}, f32[3,4,8,2,128]{4,3,2,1,0:T(2,128)S(1)}, f32[3,4,8,2,128]{4,3,2,1,0:T(2,128)S(1)}) fusion(f32[4,8,2,128,128]{4,3,2,1,0:T(8,128)S(1)} %copy-done.2, f32[4,8,2,128,128]{4,3,2,1,0:T(8,128)S(1)} %add_rsqrt_fusion.124, ...), kind=kLoop, calls=%fused_computation.8.clone.1 | loop fusion | flops 31358976 | bytes 17268736 | tf_op jit(solution)/shard_map/while/body/eval_jaxpr/reduce_sum | solution.py:94
  724.8 14.8 %fusion.136 = (f32[3,4,8,2,128]{4,3,2,1,0:T(2,128)S(1)}, f32[3,4,8,2,128]{4,3,2,1,0:T(2,128)S(1)}, f32[3,4,8,2,128]{4,3,2,1,0:T(2,128)S(1)}, f32[3,4,8,2,128]{4,3,2,1,0:T(2,128)S(1)}) fusion(f32[4,8,2,128,128]{4,3,2,1,0:T(8,128)S(1)} %copy-done.2, f32[4,8,2,128,128]{4,3,2,1,0:T(8,128)S(1)} %add_rsqrt_fusion.124, ...), kind=kLoop, calls=%fused_computation.8.clone.1 | loop fusion | flops 31358976 | bytes 17268736 | tf_op jit(solution)/shard_map/while/body/eval_jaxpr/reduce_sum | solution.py:94
  759.4 14.8 %fusion.136 = (f32[3,4,8,2,128]{4,3,2,1,0:T(2,128)S(1)}, f32[3,4,8,2,128]{4,3,2,1,0:T(2,128)S(1)}, f32[3,4,8,2,128]{4,3,2,1,0:T(2,128)S(1)}, f32[3,4,8,2,128]{4,3,2,1,0:T(2,128)S(1)}) fusion(f32[4,8,2,128,128]{4,3,2,1,0:T(8,128)S(1)} %copy-done.2, f32[4,8,2,128,128]{4,3,2,1,0:T(8,128)S(1)} %add_rsqrt_fusion.124, ...), kind=kLoop, calls=%fused_computation.8.clone.1 | loop fusion | flops 31358976 | bytes 17268736 | tf_op jit(solution)/shard_map/while/body/eval_jaxpr/reduce_sum | solution.py:94
  794.1 14.8 %fusion.136 = (f32[3,4,8,2,128]{4,3,2,1,0:T(2,128)S(1)}, f32[3,4,8,2,128]{4,3,2,1,0:T(2,128)S(1)}, f32[3,4,8,2,128]{4,3,2,1,0:T(2,128)S(1)}, f32[3,4,8,2,128]{4,3,2,1,0:T(2,128)S(1)}) fusion(f32[4,8,2,128,128]{4,3,2,1,0:T(8,128)S(1)} %copy-done.2, f32[4,8,2,128,128]{4,3,2,1,0:T(8,128)S(1)} %add_rsqrt_fusion.124, ...), kind=kLoop, calls=%fused_computation.8.clone.1 | loop fusion | flops 31358976 | bytes 17268736 | tf_op jit(solution)/shard_map/while/body/eval_jaxpr/reduce_sum | solution.py:94
  828.8 14.8 %fusion.136 = (f32[3,4,8,2,128]{4,3,2,1,0:T(2,128)S(1)}, f32[3,4,8,2,128]{4,3,2,1,0:T(2,128)S(1)}, f32[3,4,8,2,128]{4,3,2,1,0:T(2,128)S(1)}, f32[3,4,8,2,128]{4,3,2,1,0:T(2,128)S(1)}) fusion(f32[4,8,2,128,128]{4,3,2,1,0:T(8,128)S(1)} %copy-done.2, f32[4,8,2,128,128]{4,3,2,1,0:T(8,128)S(1)} %add_rsqrt_fusion.124, ...), kind=kLoop, calls=%fused_computation.8.clone.1 | loop fusion | flops 31358976 | bytes 17268736 | tf_op jit(solution)/shard_map/while/body/eval_jaxpr/reduce_sum | solution.py:94
  863.5 14.8 %fusion.136 = (f32[3,4,8,2,128]{4,3,2,1,0:T(2,128)S(1)}, f32[3,4,8,2,128]{4,3,2,1,0:T(2,128)S(1)}, f32[3,4,8,2,128]{4,3,2,1,0:T(2,128)S(1)}, f32[3,4,8,2,128]{4,3,2,1,0:T(2,128)S(1)}) fusion(f32[4,8,2,128,128]{4,3,2,1,0:T(8,128)S(1)} %copy-done.2, f32[4,8,2,128,128]{4,3,2,1,0:T(8,128)S(1)} %add_rsqrt_fusion.124, ...), kind=kLoop, calls=%fused_computation.8.clone.1 | loop fusion | flops 31358976 | bytes 17268736 | tf_op jit(solution)/shard_map/while/body/eval_jaxpr/reduce_sum | solution.py:94
  898.1 14.8 %fusion.136 = (f32[3,4,8,2,128]{4,3,2,1,0:T(2,128)S(1)}, f32[3,4,8,2,128]{4,3,2,1,0:T(2,128)S(1)}, f32[3,4,8,2,128]{4,3,2,1,0:T(2,128)S(1)}, f32[3,4,8,2,128]{4,3,2,1,0:T(2,128)S(1)}) fusion(f32[4,8,2,128,128]{4,3,2,1,0:T(8,128)S(1)} %copy-done.2, f32[4,8,2,128,128]{4,3,2,1,0:T(8,128)S(1)} %add_rsqrt_fusion.124, ...), kind=kLoop, calls=%fused_computation.8.clone.1 | loop fusion | flops 31358976 | bytes 17268736 | tf_op jit(solution)/shard_map/while/body/eval_jaxpr/reduce_sum | solution.py:94
  932.8 14.8 %fusion.136 = (f32[3,4,8,2,128]{4,3,2,1,0:T(2,128)S(1)}, f32[3,4,8,2,128]{4,3,2,1,0:T(2,128)S(1)}, f32[3,4,8,2,128]{4,3,2,1,0:T(2,128)S(1)}, f32[3,4,8,2,128]{4,3,2,1,0:T(2,128)S(1)}) fusion(f32[4,8,2,128,128]{4,3,2,1,0:T(8,128)S(1)} %copy-done.2, f32[4,8,2,128,128]{4,3,2,1,0:T(8,128)S(1)} %add_rsqrt_fusion.124, ...), kind=kLoop, calls=%fused_computation.8.clone.1 | loop fusion | flops 31358976 | bytes 17268736 | tf_op jit(solution)/shard_map/while/body/eval_jaxpr/reduce_sum | solution.py:94
  967.5 14.8 %fusion.136 = (f32[3,4,8,2,128]{4,3,2,1,0:T(2,128)S(1)}, f32[3,4,8,2,128]{4,3,2,1,0:T(2,128)S(1)}, f32[3,4,8,2,128]{4,3,2,1,0:T(2,128)S(1)}, f32[3,4,8,2,128]{4,3,2,1,0:T(2,128)S(1)}) fusion(f32[4,8,2,128,128]{4,3,2,1,0:T(8,128)S(1)} %copy-done.2, f32[4,8,2,128,128]{4,3,2,1,0:T(8,128)S(1)} %add_rsqrt_fusion.124, ...), kind=kLoop, calls=%fused_computation.8.clone.1 | loop fusion | flops 31358976 | bytes 17268736 | tf_op jit(solution)/shard_map/while/body/eval_jaxpr/reduce_sum | solution.py:94
  1002.1 14.8 %fusion.136 = (f32[3,4,8,2,128]{4,3,2,1,0:T(2,128)S(1)}, f32[3,4,8,2,128]{4,3,2,1,0:T(2,128)S(1)}, f32[3,4,8,2,128]{4,3,2,1,0:T(2,128)S(1)}, f32[3,4,8,2,128]{4,3,2,1,0:T(2,128)S(1)}) fusion(f32[4,8,2,128,128]{4,3,2,1,0:T(8,128)S(1)} %copy-done.2, f32[4,8,2,128,128]{4,3,2,1,0:T(8,128)S(1)} %add_rsqrt_fusion.124, ...), kind=kLoop, calls=%fused_computation.8.clone.1 | loop fusion | flops 31358976 | bytes 17268736 | tf_op jit(solution)/shard_map/while/body/eval_jaxpr/reduce_sum | solution.py:94
  1106.1 14.8 %fusion.136 = (f32[3,4,8,2,128]{4,3,2,1,0:T(2,128)S(1)}, f32[3,4,8,2,128]{4,3,2,1,0:T(2,128)S(1)}, f32[3,4,8,2,128]{4,3,2,1,0:T(2,128)S(1)}, f32[3,4,8,2,128]{4,3,2,1,0:T(2,128)S(1)}) fusion(f32[4,8,2,128,128]{4,3,2,1,0:T(8,128)S(1)} %copy-done.2, f32[4,8,2,128,128]{4,3,2,1,0:T(8,128)S(1)} %add_rsqrt_fusion.124, ...), kind=kLoop, calls=%fused_computation.8.clone.1 | loop fusion | flops 31358976 | bytes 17268736 | tf_op jit(solution)/shard_map/while/body/eval_jaxpr/reduce_sum | solution.py:94
  1210.1 14.8 %fusion.136 = (f32[3,4,8,2,128]{4,3,2,1,0:T(2,128)S(1)}, f32[3,4,8,2,128]{4,3,2,1,0:T(2,128)S(1)}, f32[3,4,8,2,128]{4,3,2,1,0:T(2,128)S(1)}, f32[3,4,8,2,128]{4,3,2,1,0:T(2,128)S(1)}) fusion(f32[4,8,2,128,128]{4,3,2,1,0:T(8,128)S(1)} %copy-done.2, f32[4,8,2,128,128]{4,3,2,1,0:T(8,128)S(1)} %add_rsqrt_fusion.124, ...), kind=kLoop, calls=%fused_computation.8.clone.1 | loop fusion | flops 31358976 | bytes 17268736 | tf_op jit(solution)/shard_map/while/body/eval_jaxpr/reduce_sum | solution.py:94
  1314.2 14.8 %fusion.136 = (f32[3,4,8,2,128]{4,3,2,1,0:T(2,128)S(1)}, f32[3,4,8,2,128]{4,3,2,1,0:T(2,128)S(1)}, f32[3,4,8,2,128]{4,3,2,1,0:T(2,128)S(1)}, f32[3,4,8,2,128]{4,3,2,1,0:T(2,128)S(1)}) fusion(f32[4,8,2,128,128]{4,3,2,1,0:T(8,128)S(1)} %copy-done.2, f32[4,8,2,128,128]{4,3,2,1,0:T(8,128)S(1)} %add_rsqrt_fusion.124, ...), kind=kLoop, calls=%fused_computation.8.clone.1 | loop fusion | flops 31358976 | bytes 17268736 | tf_op jit(solution)/shard_map/while/body/eval_jaxpr/reduce_sum | solution.py:94
  (1094 shorter events, 1000.8 us)
Async XLA Ops:
  17.4 367.5 %collective-permute-start.4 = (f32[121,3,3,8,2]{0,4,3,2,1:T(2,128)}, f32[121,3,3,8,2]{0,4,3,2,1:T(2,128)S(1)}, u32[]{:S(2)}, u32[]{:S(2)}) collective-permute-start(f32[121,3,3,8,2]{0,4,3,2,1:T(2,128)} %get-tuple-element.764), channel_id=1, source_target_pairs={{0,4},{4,8},{8,12},{12,16},{16,20},{20,24},{24,28},{1,5},{5,9},{9,... | collective-permute-start | bytes 209096 | tf_op jit(solution)/shard_map/ppermute | solution.py:22
  19.8 365.2 %collective-permute-start.5 = (f32[121,3,3,8,2]{0,4,3,2,1:T(2,128)}, f32[121,3,3,8,2]{0,4,3,2,1:T(2,128)S(1)}, u32[]{:S(2)}, u32[]{:S(2)}) collective-permute-start(f32[121,3,3,8,2]{0,4,3,2,1:T(2,128)} %get-tuple-element.765), channel_id=1, source_target_pairs={{4,0},{8,4},{12,8},{16,12},{20,16},{24,20},{28,24},{5,1},{9,5},{13... | collective-permute-start | bytes 209096 | tf_op jit(solution)/shard_map/ppermute | solution.py:24
  21.9 359.5 %collective-permute-start = (f32[6,1,8,256]{3,2,1,0:T(8,128)}, f32[6,1,8,256]{3,2,1,0:T(8,128)}, u32[]{:S(2)}, u32[]{:S(2)}) collective-permute-start(f32[6,1,8,256]{3,2,1,0:T(8,128)} %get-tuple-element.754), channel_id=1, source_target_pairs={{0,4},{4,8},{8,12},{12,16},{16,20},{20,24},{24,28},{1,5},{5,9},{9,... | collective-permute-start | bytes 147464 | tf_op jit(solution)/shard_map/ppermute | solution.py:22
  27.6 353.8 %collective-permute-start.1 = (f32[6,1,8,256]{3,2,1,0:T(8,128)}, f32[6,1,8,256]{3,2,1,0:T(8,128)}, u32[]{:S(2)}, u32[]{:S(2)}) collective-permute-start(f32[6,1,8,256]{3,2,1,0:T(8,128)} %get-tuple-element.755), channel_id=1, source_target_pairs={{4,0},{8,4},{12,8},{16,12},{20,16},{24,20},{28,24},{5,1},{9,5},{13... | collective-permute-start | bytes 147464 | tf_op jit(solution)/shard_map/ppermute | solution.py:24
  54.8 31.2 %copy-start.152 = (f32[3]{0:T(128)S(1)}, f32[3]{0:T(128)}, u32[]{:S(2)}) copy-start(f32[3]{0:T(128)} %constant.1069.clone) | copy-start | bytes 40
  54.8 31.2 %copy-start.153 = (f32[3]{0:T(128)S(1)}, f32[3]{0:T(128)}, u32[]{:S(2)}) copy-start(f32[3]{0:T(128)} %constant.1070.clone) | copy-start | bytes 40
  194.6 150.2 %copy-start.81 = (f32[3,121]{1,0:T(4,128)S(1)}, f32[3,121]{1,0:T(4,128)}, u32[]{:S(2)}) copy-start(f32[3,121]{1,0:T(4,128)} %get-tuple-element.771) | copy-start | bytes 4360
  194.6 150.8 %copy-start.17 = (f32[121,121]{1,0:T(8,128)S(1)}, f32[121,121]{1,0:T(8,128)}, u32[]{:S(2)}) copy-start(f32[121,121]{1,0:T(8,128)} %get-tuple-element.437) | copy-start | bytes 175696
  194.6 150.8 %copy-start.16 = (f32[121,121]{1,0:T(8,128)S(1)}, f32[121,121]{1,0:T(8,128)}, u32[]{:S(2)}) copy-start(f32[121,121]{1,0:T(8,128)} %get-tuple-element.454) | copy-start | bytes 175696
  194.6 150.8 %copy-start.15 = (f32[121,121]{1,0:T(8,128)S(1)}, f32[121,121]{1,0:T(8,128)}, u32[]{:S(2)}) copy-start(f32[121,121]{1,0:T(8,128)} %get-tuple-element.453) | copy-start | bytes 175696
  194.6 150.8 %copy-start.14 = (f32[121,121]{1,0:T(8,128)S(1)}, f32[121,121]{1,0:T(8,128)}, u32[]{:S(2)}) copy-start(f32[121,121]{1,0:T(8,128)} %get-tuple-element.452) | copy-start | bytes 175696
  194.6 151.5 %copy-start.13 = (f32[121,121]{1,0:T(8,128)S(1)}, f32[121,121]{1,0:T(8,128)}, u32[]{:S(2)}) copy-start(f32[121,121]{1,0:T(8,128)} %get-tuple-element.451) | copy-start | bytes 175696
  194.6 156.3 %copy-start.19 = (f32[121,121]{1,0:T(8,128)S(1)}, f32[121,121]{1,0:T(8,128)}, u32[]{:S(2)}) copy-start(f32[121,121]{1,0:T(8,128)} %get-tuple-element.457) | copy-start | bytes 175696
  194.6 156.9 %copy-start.18 = (f32[121,121]{1,0:T(8,128)S(1)}, f32[121,121]{1,0:T(8,128)}, u32[]{:S(2)}) copy-start(f32[121,121]{1,0:T(8,128)} %get-tuple-element.456) | copy-start | bytes 175696
  382.3 9.5 collective-permute-start.2
  383.6 8.2 collective-permute-start.3
  385.1 944.7 %collective-permute-start.6 = (f32[121,3,10,3,2]{0,4,3,2,1:T(2,128)S(1)}, f32[121,3,10,3,2]{0,4,3,2,1:T(2,128)S(1)}, u32[]{:S(2)}, u32[]{:S(2)}) collective-permute-start(f32[121,3,10,3,2]{0,4,3,2,1:T(2,128)S(1)} %get-tuple-element.752), channel_id=1, source_target_pairs={{0,1},{1,2},{2,3},{4,5},{5,6},{6,7},{8,9},{9,10},{10,11},{12,13},{... | collective-permute-start | bytes 261368 | tf_op jit(solution)/shard_map/ppermute | solution.py:22
  389.6 940.1 %collective-permute-start.7 = (f32[121,3,10,3,2]{0,4,3,2,1:T(2,128)S(1)}, f32[121,3,10,3,2]{0,4,3,2,1:T(2,128)S(1)}, u32[]{:S(2)}, u32[]{:S(2)}) collective-permute-start(f32[121,3,10,3,2]{0,4,3,2,1:T(2,128)S(1)} %get-tuple-element.753), channel_id=1, source_target_pairs={{1,0},{2,1},{3,2},{5,4},{6,5},{7,6},{9,8},{10,9},{11,10},{13,12},{... | collective-permute-start | bytes 261368 | tf_op jit(solution)/shard_map/ppermute | solution.py:24
  393.3 936.9 %copy-start.73 = (f32[4,8]{1,0:T(4,128)S(1)}, f32[4,8]{1,0:T(4,128)}, u32[]{:S(2)}) copy-start(f32[4,8]{1,0:T(4,128)} %get-tuple-element.911) | copy-start | bytes 388
  393.3 936.9 %copy-start.74 = (f32[4,8]{1,0:T(4,128)S(1)}, f32[4,8]{1,0:T(4,128)}, u32[]{:S(2)}) copy-start(f32[4,8]{1,0:T(4,128)} %get-tuple-element.918) | copy-start | bytes 388
  393.3 936.9 %copy-start.75 = (f32[4,8]{1,0:T(4,128)S(1)}, f32[4,8]{1,0:T(4,128)}, u32[]{:S(2)}) copy-start(f32[4,8]{1,0:T(4,128)} %get-tuple-element.920) | copy-start | bytes 388
  393.3 936.9 %copy-start.76 = (f32[4,8]{1,0:T(4,128)S(1)}, f32[4,8]{1,0:T(4,128)}, u32[]{:S(2)}) copy-start(f32[4,8]{1,0:T(4,128)} %get-tuple-element.936) | copy-start | bytes 388
  393.3 936.9 %copy-start.77 = (f32[4,8]{1,0:T(4,128)S(1)}, f32[4,8]{1,0:T(4,128)}, u32[]{:S(2)}) copy-start(f32[4,8]{1,0:T(4,128)} %get-tuple-element.939) | copy-start | bytes 388
  393.3 936.9 %copy-start.91 = (f32[8]{0:T(128)S(1)}, f32[8]{0:T(128)}, u32[]{:S(2)}) copy-start(f32[8]{0:T(128)} %get-tuple-element.950) | copy-start | bytes 100
  (224 other events, 2360.2 us)
where the time goes:
time: 1400 us; the launch traced here: 1390 us
  other arithmetic  729 us (52%)
  local copies, waits for them, and re-layouts  384 us (27%)
  matrix products  179 us (13%)
  blocking collectives  73 us (5%)
  starting transfers between devices  19.3 us (1%)
    reduce_sum x27, other arithmetic, accumulate(): jnp.sum(vector[axis_number][None] * cubed, axis=-1)  400 us
    mul x28, local copies, waits for them, and re-layouts, accumulate(): vector[axis_number][None] * cubed  269 us
    reduce_sum x37, other arithmetic, kernel_of(): return lax.rsqrt(jnp.sum(vector * vector, axis=0) + SMOOTH2)  175 us
    dot_general x16, matrix products, top_block(): return jnp.einsum('ktmb,mcb->kct', weight, charges, precision=HIGHEST)  145 us
    rsqrt x149, other arithmetic, kernel_of(): return lax.rsqrt(jnp.sum(vector * vector, axis=0) + SMOOTH2)  82.5 us
    while x108, local copies, waits for them, and re-layouts  78.7 us
    all_gather x1, blocking collectives, body(): shard_part = lax.all_gather(top_charges, ('gx', 'gy'), axis=2, tiled=True)  73 us
  transfers between devices with their start and end apart: 8, of which 0 were waited for; matrix products, arithmetic and copies ran while one was open for 81% of the time, Pallas kernels for 0%

commit v1 on v0

v1 whole, which is shorter than its diff:
```python
import functools
import math

import jax
import jax.numpy as jnp
import numpy as np
from jax import lax
from jax.experimental import pallas as pl
from jax.experimental.pallas import tpu as pltpu
from jax.sharding import PartitionSpec as P

SMOOTH2 = 0.01
STRENGTH_SCALE = 0.03
LANES = 128
F32 = jnp.float32
BF16 = jnp.bfloat16
HIGHEST = lax.Precision.HIGHEST


def sphere_points(amount):
    counter = np.arange(amount, dtype=np.float32)
    height = (1.0 - (2.0 * counter + 1.0) / np.float32(amount)).astype(np.float32)
    radius = np.sqrt(np.maximum(1.0 - height * height, 0.0)).astype(np.float32)
    azimuth = counter * np.float32(math.pi * (3.0 - math.sqrt(5.0)))
    points = np.zeros((3, LANES), np.float32)
    points[:, :amount] = np.stack([radius * np.cos(azimuth), radius * np.sin(azimuth), height])
    return points


def split(value):
    high = value.astype(BF16)
    return high, (value - high.astype(F32)).astype(BF16)


def bdot(left, right):
    return jnp.dot(left, right, preferred_element_type=F32)


def dot_nt(left, right):
    return lax.dot_general(
        left, right, (((1,), (1,)), ((), ())), precision=HIGHEST, preferred_element_type=F32
    )


def two_terms(high, low):
    return jnp.concatenate(
        [
            jnp.concatenate([high, high], axis=1),
            jnp.concatenate([low, jnp.zeros_like(low)], axis=1),
        ],
        axis=0,
    )


def cubes(dx, dy, dz):
    inverse = lax.rsqrt(dx * dx + dy * dy + dz * dz + SMOOTH2)
    return inverse * inverse * inverse


def up_kernel(size_x, size_y, pack_ref, rows_ref, cols_ref, inverse_ref, leaf_ref, top_ref, check):
    point = [rows_ref[j : j + 1, :] for j in range(3)]

    def column(index, carry):
        i = index // size_y
        j = index % size_y
        row = [pack_ref[c, i, pl.ds(j, 1), :] for c in range(6)]
        for half in range(2):
            lanes = slice(half * LANES, (half + 1) * LANES)
            delta = []
            for axis in range(3):
                source = jnp.broadcast_to(row[axis][:, lanes], (LANES, LANES)).T
                delta.append(1.5 * point[axis] - source)
            kernel = lax.rsqrt(
                delta[0] * delta[0] + delta[1] * delta[1] + delta[2] * delta[2] + SMOOTH2
            )
            charge = jnp.concatenate(
                [row[3 + c][:, lanes] for c in range(3)] + [jnp.zeros((5, LANES), F32)], axis=0
            )
            c_high, c_low = split(charge)
            k_high, k_low = split(kernel)
            total = bdot(
                two_terms(
                    jnp.concatenate([c_high, c_low], axis=0),
                    jnp.zeros((16, LANES), BF16),
                )[:16],
                jnp.concatenate([k_high, k_low], axis=0),
            )
            total = total[:8] + total[8:]
            for c in range(3):
                check[half, c, i, pl.ds(j, 1), :] = total[c : c + 1]
        return carry

    lax.fori_loop(0, size_x * size_y, column, 0)
    matrix = inverse_ref[...]
    rows = 6 * size_x * size_y
    charges = 0.5 * dot_nt(check[...].reshape(rows, LANES), matrix)
    leaf_ref[...] = charges.reshape(2, 3, size_x, size_y, LANES)
    half_x = size_x // 2
    half_y = size_y // 2
    total = jnp.zeros((3 * half_x * half_y, LANES), F32)
    for a in range(2):
        for b in range(2):
            for e in range(2):
                shift = (a - 0.5, b - 0.5, e - 0.5)
                delta = [
                    3.0 * point[axis] - shift[axis] - 0.9 * cols_ref[axis] for axis in range(3)
                ]
                table = lax.rsqrt(
                    delta[0] * delta[0] + delta[1] * delta[1] + delta[2] * delta[2] + SMOOTH2
                )
                pieces = [
                    leaf_ref[e, c, 2 * x + a, pl.ds(b, half_y, stride=2), :]
                    for c in range(3)
                    for x in range(half_x)
                ]
                total = total + jnp.dot(
                    jnp.concatenate(pieces, axis=0),
                    table,
                    precision=HIGHEST,
                    preferred_element_type=F32,
                )
    top_ref[...] = dot_nt(total, matrix)


def near_kernel(size_x, size_y, ext_ref, out_ref, spread, moments):
    ext_y = size_y + 2
    lane = lax.broadcasted_iota(jnp.int32, (1, 2 * LANES), 1)
    lift = jnp.where(lane < LANES, -0.5, 0.5).astype(F32)

    def prepare(index, carry):
        i = index // ext_y
        j = index % ext_y
        row = [ext_ref[c, i, pl.ds(j, 1), :] for c in range(6)]
        x, y, z = row[0], row[1], row[2] + lift
        for axis, value in enumerate((x, y, z)):
            for half in range(2):
                lanes = slice(half * LANES, (half + 1) * LANES)
                spread[index, axis, lanes, :] = jnp.broadcast_to(
                    value[:, lanes], (LANES, LANES)
                ).T
        zero = jnp.zeros_like(x)
        one = jnp.ones_like(x)

        def weighted(factors):
            return jnp.concatenate(
                [factor * row[3 + c] for factor in factors for c in range(3)] + [zero], axis=0
            )

        moments[index, 0] = weighted([one, x, y, z, x * x + y * y + z * z])
        moments[index, 1] = weighted([zero, one, zero, zero, 2.0 * x])
        moments[index, 2] = weighted([zero, zero, one, zero, 2.0 * y])
        moments[index, 3] = weighted([zero, zero, zero, zero, one])
        return carry

    lax.fori_loop(0, (size_x + 2) * ext_y, prepare, 0)

    def target(index, carry):
        i = index // size_y
        j = index % size_y
        row = [ext_ref[c, i + 1, pl.ds(j + 1, 1), :] for c in range(3)]
        total = jnp.zeros((32, 2 * LANES), F32)
        for shift_x in (-1, 0, 1):
            for shift_y in (-1, 0, 1):
                source = (i + 1 + shift_x) * ext_y + j + 1 + shift_y
                weight = moments[source, 0]
                if shift_x:
                    weight = weight + float(shift_x) * moments[source, 1]
                if shift_y:
                    weight = weight + float(shift_y) * moments[source, 2]
                if shift_x or shift_y:
                    weight = weight + float(shift_x**2 + shift_y**2) * moments[source, 3]
                w_high, w_low = split(weight)
                place = [row[0] - float(shift_x), row[1] - float(shift_y), row[2] + lift]
                for half in range(2):
                    part = slice(half * LANES, (half + 1) * LANES)
                    highs = []
                    lows = []
                    for side in range(2):
                        lanes = slice(side * LANES, (side + 1) * LANES)
                        delta = [
                            place[axis][:, lanes] - spread[source, axis, part, :]
                            for axis in range(3)
                        ]
                        high, low = split(cubes(*delta))
                        highs.append(high)
                        lows.append(low)
                    total = total + bdot(
                        two_terms(w_high[:, part], w_low[:, part]),
                        jnp.concatenate(
                            [jnp.concatenate(highs, axis=1), jnp.concatenate(lows, axis=1)],
                            axis=0,
                        ),
                    )
        out_ref[index] = total[:16] + total[16:]
        return carry

    lax.fori_loop(0, size_x * size_y, target, 0)


def far_kernel(
    size_x,
    size_y,
    tops_x,
    tops_y,
    scalar_ref,
    shift_ref,
    counts_ref,
    leaf_ref,
    tops_ref,
    near_ref,
    pack_ref,
    rows_ref,
    cols_ref,
    pattern_ref,
    inverse_ref,
    out_ref,
    base,
    windows,
    down,
    top_down,
    local,
):
    half_x = size_x // 2
    half_y = size_y // 2
    group = half_x * 4
    across = tops_x + half_x - 1
    along = tops_y + half_y - 1
    point = [rows_ref[j : j + 1, :] for j in range(3)]
    for axis in range(3):
        base[axis] = point[axis] - cols_ref[axis]

    windows[...] = jnp.zeros_like(windows)

    def place(index, carry):
        i = index // tops_y
        j = index % tops_y
        device = (i // half_x) * (tops_y // half_y) + j // half_y
        inside = (i % half_x) * half_y + j % half_y
        for c in range(3):
            row = tops_ref[device, pl.ds(c * half_x * half_y + inside, 1), :]
            for x in range(half_x):
                windows[
                    i + half_x - 1 - x, pl.ds((j + half_y - 1) * group + x * 4 + c, 1), :
                ] = row
        return carry

    lax.fori_loop(0, tops_x * tops_y, place, 0)
    first_x = scalar_ref[0]
    first_y = scalar_ref[1]
    top_down[...] = jnp.zeros_like(top_down)

    def top_row(wx, carry):
        gap_x = first_x - (wx - (half_x - 1))
        dx = 1.8 * base[0] + 2.0 * gap_x.astype(F32)
        dz = 1.8 * base[2]
        squares = dx * dx + dz * dz + SMOOTH2

        def top_step(wy, inner):
            gap_y = first_y - (wy - (half_y - 1))
            distant = (jnp.abs(gap_x) >= 2) | (jnp.abs(gap_y) >= 2)
            dy = 1.8 * base[1] + 2.0 * gap_y.astype(F32)
            table = lax.rsqrt(squares + dy * dy)
            t_high, t_low = split(table)
            rows = windows[wx, pl.ds(wy * group, half_y * group), :]
            rows = jnp.where(distant, rows, 0.0)
            r_high, r_low = split(rows)
            both = bdot(jnp.concatenate([r_high, r_low], axis=0), t_high)
            top_down[...] += both[: half_y * group] + both[half_y * group :] + bdot(r_high, t_low)
            return inner

        return lax.fori_loop(0, along, top_step, carry)

    lax.fori_loop(0, across, top_row, 0)
    matrix = inverse_ref[...]
    top_local = dot_nt(top_down[...], matrix)

    down[...] = jnp.zeros_like(down)
    odd_y = lax.broadcasted_iota(jnp.int32, (size_y, LANES), 0) % 2

    def leaf_step(step, carry):
        shift_x = shift_ref[2 * step]
        shift_y = shift_ref[2 * step + 1]
        dx = 0.9 * base[0] - shift_x.astype(F32)
        dy = 0.9 * base[1] - shift_y.astype(F32)
        flat = dx * dx + dy * dy + SMOOTH2
        tables = []
        for shift_z in (-1, 0, 1):
            dz = 0.9 * base[2] - float(shift_z)
            tables.append(split(lax.rsqrt(flat + dz * dz)))
        wide = [
            jnp.concatenate(
                [
                    jnp.concatenate([tables[1][t], tables[0][t]], axis=1),
                    jnp.concatenate([tables[2][t], tables[1][t]], axis=1),
                ],
                axis=0,
            )
            for t in range(2)
        ]
        near_y = jnp.where(
            ((shift_y > -3) | (odd_y == 1)) & ((shift_y < 3) | (odd_y == 0)), 1.0, 0.0
        )
        highs = []
        lows = []
        for depth in range(2):
            pieces = []
            for c in range(3):
                for x in range(size_x):
                    near_x = (shift_x > -3) if x % 2 == 0 else (shift_x < 3)
                    pieces.append(
                        leaf_ref[depth, c, x + 3 + shift_x, pl.ds(3 + shift_y, size_y), :]
                        * jnp.where(near_x, near_y, 0.0)
                    )
            high, low = split(jnp.concatenate(pieces, axis=0))
            highs.append(high)
            lows.append(low)
        high = jnp.concatenate(highs, axis=1)
        low = jnp.concatenate(lows, axis=1)
        down[...] += bdot(high, wide[0]) + bdot(low, wide[0]) + bdot(high, wide[1])
        return carry

    lax.fori_loop(0, shift_ref.shape[0] // 2, leaf_step, 0)

    for a in range(2):
        for b in range(2):
            for e in range(2):
                offset = (a - 0.5, b - 0.5, e - 0.5)
                delta = [
                    offset[axis] + 0.9 * point[axis] - 3.0 * cols_ref[axis] for axis in range(3)
                ]
                table = lax.rsqrt(
                    delta[0] * delta[0] + delta[1] * delta[1] + delta[2] * delta[2] + SMOOTH2
                )
                inherited = jnp.dot(
                    top_local, table, precision=HIGHEST, preferred_element_type=F32
                )
                for y in range(half_y):
                    for x in range(half_x):
                        for c in range(3):
                            row = (c * size_x + 2 * x + a) * size_y + 2 * y + b
                            down[row : row + 1, e * LANES : (e + 1) * LANES] += inherited[
                                y * group + x * 4 + c : y * group + x * 4 + c + 1
                            ]
    for e in range(2):
        part = 0.5 * dot_nt(down[:, e * LANES : (e + 1) * LANES], matrix)
        local[e] = part.reshape(3, size_x, size_y, LANES)

    lane = lax.broadcasted_iota(jnp.int32, (1, LANES), 1)

    def column(index, carry):
        i = index // size_y
        j = index % size_y
        row = [pack_ref[c, i, pl.ds(j, 1), :] for c in range(3)]
        results = []
        for half in range(2):
            lanes = slice(half * LANES, (half + 1) * LANES)
            place = [row[axis][:, lanes] for axis in range(3)]
            delta = [place[axis] - 1.5 * cols_ref[axis] for axis in range(3)]
            high, low = split(cubes(*delta))
            charge = jnp.concatenate(
                [local[half, c, i, pl.ds(j, 1), :] for c in range(3)], axis=0
            )
            weight = pattern_ref[half] * jnp.concatenate(
                [charge] * 5 + [jnp.zeros((1, LANES), F32)], axis=0
            )
            total = bdot(two_terms(*split(weight)), jnp.concatenate([high, low], axis=0))
            total = total[:16] + total[16:] + near_ref[index, :, lanes]
            place[2] = place[2] + (half - 0.5)
            living = jnp.where(lane < counts_ref[2 * index + half], 1.0, 0.0)
            square = (
                place[0] * place[0] + place[1] * place[1] + place[2] * place[2] + SMOOTH2
            )
            potential = (
                square * total[0:3]
                - 2.0
                * (place[0] * total[3:6] + place[1] * total[6:9] + place[2] * total[9:12])
                + total[12:15]
            ) * living
            slopes = [
                (total[3 + 3 * axis : 6 + 3 * axis] - place[axis] * total[0:3]) * living
                for axis in range(3)
            ]
            results.append((potential, slopes))
        potential = jnp.concatenate([results[0][0], results[1][0]], axis=1)
        slopes = [
            jnp.concatenate([results[0][1][axis], results[1][1][axis]], axis=1)
            for axis in range(3)
        ]
        for c in range(3):
            out_ref[c, i, pl.ds(j, 1), :] = potential[c : c + 1]
            for axis in range(3):
                out_ref[3 + 3 * c + axis, i, pl.ds(j, 1), :] = slopes[axis][c : c + 1]
        return carry

    lax.fori_loop(0, size_x * size_y, column, 0)


def extended(cells, sides):
    for axis, dim, width in sides:
        count = lax.axis_size(axis)
        head = lax.slice_in_dim(cells, 0, width, axis=dim)
        tail = lax.slice_in_dim(cells, cells.shape[dim] - width, cells.shape[dim], axis=dim)
        cells = jnp.concatenate(
            [
                lax.ppermute(tail, axis, [(i, i + 1) for i in range(count - 1)]),
                cells,
                lax.ppermute(head, axis, [(i + 1, i) for i in range(count - 1)]),
            ],
            axis=dim,
        )
    return cells


def body(offsets, strengths, counts, check_inverse):
    size_x, size_y, depth = counts.shape
    expansion = check_inverse.shape[0]
    half_x = size_x // 2
    half_y = size_y // 2
    lanes_x = lax.axis_size("gx")
    lanes_y = lax.axis_size("gy")
    tops_x = lanes_x * half_x
    tops_y = lanes_y * half_y
    points = sphere_points(expansion)
    rows = jnp.asarray(np.concatenate([points, np.zeros((5, LANES), np.float32)], axis=0))
    cols = jnp.asarray(np.repeat(points[:, :, None], LANES, axis=2))
    patterns = np.zeros((2, 16, LANES), np.float32)
    for half in range(2):
        lifted = (1.5 * points).astype(np.float32)
        lifted[2] += half - 0.5
        factors = [np.ones(LANES), *lifted, np.sum(lifted.astype(np.float64) ** 2, axis=0)]
        for k in range(5):
            patterns[half, 3 * k : 3 * k + 3, :] = factors[k]
    patterns = jnp.asarray(patterns)
    pad = LANES - expansion
    matrix = jnp.pad(check_inverse, ((0, pad), (0, pad)))
    slot = jnp.arange(LANES)
    living = (slot < counts[:, :, :, None]).astype(F32).reshape(1, size_x, size_y, depth * LANES)
    pack = jnp.concatenate([offsets, STRENGTH_SCALE * strengths * living], axis=0)

    params = pltpu.CompilerParams(vmem_limit_bytes=58 * 2**20)
    leaf_charges, top_charges = pl.pallas_call(
        functools.partial(up_kernel, size_x, size_y),
        out_shape=(
            jax.ShapeDtypeStruct((2, 3, size_x, size_y, LANES), F32),
            jax.ShapeDtypeStruct((3 * half_x * half_y, LANES), F32),
        ),
        scratch_shapes=[pltpu.VMEM((2, 3, size_x, size_y, LANES), F32)],
        compiler_params=params,
        cost_estimate=pl.CostEstimate(flops=10**9, bytes_accessed=10**6, transcendentals=0),
        name="up",
    )(pack, rows, cols, matrix)

    neighbours = extended(pack, (("gx", 1, 1), ("gy", 2, 1)))
    border = extended(leaf_charges, (("gx", 2, 3), ("gy", 3, 3)))
    gathered = lax.all_gather(top_charges, ("gx", "gy"), axis=0)

    near = pl.pallas_call(
        functools.partial(near_kernel, size_x, size_y),
        out_shape=jax.ShapeDtypeStruct((size_x * size_y, 16, 2 * LANES), F32),
        scratch_shapes=[
            pltpu.VMEM(((size_x + 2) * (size_y + 2), 3, 2 * LANES, LANES), F32),
            pltpu.VMEM(((size_x + 2) * (size_y + 2), 4, 16, 2 * LANES), F32),
        ],
        compiler_params=params,
        cost_estimate=pl.CostEstimate(flops=4 * 10**10, bytes_accessed=10**6, transcendentals=0),
        name="near",
    )(neighbours)

    shifts = np.array(
        [
            (x, y)
            for x in range(-3, 4)
            for y in range(-3, 4)
            if abs(x) >= 2 or abs(y) >= 2
        ],
        np.int32,
    ).reshape(-1)
    first = jnp.stack([lax.axis_index("gx") * half_x, lax.axis_index("gy") * half_y])
    across = tops_x + half_x - 1
    along = tops_y + 2 * half_y - 2
    smem = pl.BlockSpec(memory_space=pltpu.SMEM)
    vmem = pl.BlockSpec(memory_space=pltpu.VMEM)
    return pl.pallas_call(
        functools.partial(far_kernel, size_x, size_y, tops_x, tops_y),
        out_shape=jax.ShapeDtypeStruct((12, size_x, size_y, depth * LANES), F32),
        in_specs=[smem] * 3 + [vmem] * 8,
        out_specs=vmem,
        scratch_shapes=[
            pltpu.VMEM((3, LANES, LANES), F32),
            pltpu.VMEM((across, along * half_x * 4, LANES), F32),
            pltpu.VMEM((3 * size_x * size_y, 2 * LANES), F32),
            pltpu.VMEM((half_y * half_x * 4, LANES), F32),
            pltpu.VMEM((2, 3, size_x, size_y, LANES), F32),
        ],
        compiler_params=params,
        cost_estimate=pl.CostEstimate(flops=10**10, bytes_accessed=10**6, transcendentals=0),
        name="far",
    )(
        first.astype(jnp.int32),
        jnp.asarray(shifts),
        counts.reshape(-1),
        border,
        gathered,
        near,
        pack,
        rows,
        cols,
        patterns,
        matrix,
    )


def solution(mesh):
    return jax.shard_map(
        body,
        mesh=mesh,
        in_specs=(P(None, "gx", "gy", None), P(None, "gx", "gy", None), P("gx", "gy", None), P()),
        out_specs=P(None, "gx", "gy", None),
        check_vma=False,
    )
```

time: 1400 us -> 250 us (0.18)
  other arithmetic: 729 us -> 4.91 us
  local copies, waits for them, and re-layouts: 384 us -> 2.42 us
  matrix products: 179 us -> 0 us
  Pallas kernels: 0 us -> 144 us
    reduce_sum x65 -> x0, other arithmetic: 584 us -> none  [the longest x27 400 us: accumulate(): jnp.sum(vector[axis_number][None] * cubed, axis=-1)]
    mul x29 -> x0, local copies, waits for them, and re-layouts: 269 us -> none  [the longest x28 269 us: accumulate(): vector[axis_number][None] * cubed]
    dot_general x30 -> x0, matrix products: 179 us -> none  [the longest x16 145 us: top_block(): return jnp.einsum('ktmb,mcb->kct', weight, charges, precision=HIGHEST)]
    pallas_call x0 -> x3, Pallas kernels: none -> 144 us  [the longest x1 76.9 us: body(): pl.pallas_call(functools.partial(far_kernel, size_x, size_y, tops_x, tops...]
    rsqrt x149 -> x0, other arithmetic: 82.5 us -> none  [kernel_of(): return lax.rsqrt(jnp.sum(vector * vector, axis=0) + SMOOTH2)]
    while x108 -> x0, local copies, waits for them, and re-layouts: 78.7 us -> none
    concatenate x14 -> x1, local copies, waits for them, and re-layouts: 27.4 us -> 0.01 us  [extended(): jnp.concatenate([lax.ppermute(tail, axis, [(i, i + 1) for i in range(coun...]
    mul x66 -> x2, other arithmetic: 21.2 us -> 1.7 us  [body(): STRENGTH_SCALE * strengths * living]
  transfers between devices with their start and end apart: 8 -> 8, of which waited for: 0 -> 0; matrix products, arithmetic and copies ran while one was open for 81% -> 2% of each run, Pallas kernels for 0% -> 27%
where the time goes in v1:
time: 250 us; the launch traced here: 248 us
  Pallas kernels  144 us (58%)
  blocking collectives  76.5 us (31%)
  starting transfers between devices  19.4 us (8%)
  other arithmetic  4.91 us (2%)
    pallas_call x1, Pallas kernels, body(): pl.pallas_call(functools.partial(far_kernel, size_x, size_y, tops_x, tops...  76.9 us
    all_gather x1, blocking collectives, body(): gathered = lax.all_gather(top_charges, ('gx', 'gy'), axis=0)  76.5 us
    pallas_call x1, Pallas kernels, body(): pl.pallas_call(functools.partial(near_kernel, size_x, size_y), out_shape=...  54.8 us
    ppermute x4, starting transfers between devices, extended(): lax.ppermute(tail, axis, [(i, i + 1) for i in range(count - 1)])  14.1 us
    pallas_call x1, Pallas kernels, body(): pl.pallas_call(functools.partial(up_kernel, size_x, size_y), out_shape=(j...  12.7 us
    ppermute x4, starting transfers between devices, extended(): lax.ppermute(head, axis, [(i + 1, i) for i in range(count - 1)])  5.3 us
  transfers between devices with their start and end apart: 8, of which 0 were waited for; matrix products, arithmetic and copies ran while one was open for 2% of the time, Pallas kernels for 27%

profile of v1, /device:TPU:0, one launch (start us, length us, event | category | flops | bytes accessed | tf_op | source)
XLA Modules:
  0.0 247.7 jit_solution(7748255467016075683)
XLA Ops:
  0.0 0.8 fusion.2
  0.8 0.9 broadcast_multiply_fusion
  1.7 2.4 collective-permute-start.4
  4.1 1.4 collective-permute-start.5
  5.6 0.7 pad_maximum_fusion.2.pack_ref
  6.2 0.6 pad.4.inverse_ref
  6.9 12.7 %up.1 = (f32[2,3,4,8,128]{4,3,2,1,0:T(8,128)}, f32[24,128]{1,0:T(8,128)}) custom-call(f32[6,4,8,256]{3,2,1,0:T(8,128)} %pad_maximum_fusion.2.pack_ref, f32[8,128]{1,0:T(8,128)} %constant.27.clone.rows_ref, f32[3,128,128]{2,1,0:T(8,128)} %constant.28.clone.cols_ref, f32[128,128]{1,0:T(8,128)} %pad.4.inverse_ref), custom_call_target="tpu_custom_call" | custom-call | flops 1000000000 | bytes 1000000 | tf_op jit(solution)/shard_map/up/pallas_call | solution.py:441
  19.5 1.0 fusion.4
  20.5 1.3 collective-permute-start.1
  21.8 5.8 %collective-permute-start = (f32[2,3,3,8,128]{4,3,2,1,0:T(8,128)S(1)}, f32[2,3,3,8,128]{4,3,2,1,0:T(8,128)S(1)}, u32[]{:S(2)}, u32[]{:S(2)}) collective-permute-start(f32[2,3,3,8,128]{4,3,2,1,0:T(8,128)S(1)} %get-tuple-element.16), channel_id=1, source_target_pairs={{0,4},{4,8},{8,12},{12,16},{16,20},{20,24},{24,28},{1,5},{5,9},{9,... | collective-permute-start | bytes 221192 | tf_op jit(solution)/shard_map/ppermute | solution.py:405
  27.6 76.5 %all-gather = f32[768,128]{1,0:T(8,128)} all-gather(f32[24,128]{1,0:T(8,128)S(1)} %copy-done.4), channel_id=2, replica_groups=mesh['gx'=8,'gy'=4] {'gx','gy'}, dimensions={0}, use_global_device_ids=true | all-gather | bytes 405504 | tf_op jit(solution)/shard_map/all_gather | solution.py:455
  104.1 0.7 pad_add_fusion.scalar_ref
  104.7 0.0 copy-done.3
  104.8 0.1 copy.10
  104.9 0.6 reshape.14.counts_ref
  105.5 0.0 copy-start.1
  105.5 1.4 collective-permute-start.6
  107.0 1.3 collective-permute-start.7
  108.4 4.6 %collective-permute-start.2 = (f32[2,3,10,3,128]{4,3,2,1,0:T(4,128)S(1)}, f32[2,3,10,3,128]{4,3,2,1,0:T(4,128)S(1)}, u32[]{:S(2)}, u32[]{:S(2)}) collective-permute-start(f32[2,3,10,3,128]{4,3,2,1,0:T(4,128)S(1)} %get-tuple-element.11), channel_id=1, source_target_pairs={{0,1},{1,2},{2,3},{4,5},{5,6},{6,7},{8,9},{9,10},{10,11},{12,13},{... | collective-permute-start | bytes 276488 | tf_op jit(solution)/shard_map/ppermute | solution.py:405
  113.0 1.3 collective-permute-start.3
  114.3 0.9 pad_maximum_fusion.ext_ref
  115.2 54.8 %near.1.near_ref = f32[32,16,256]{2,1,0:T(8,128)} custom-call(f32[6,6,10,256]{3,2,1,0:T(8,128)} %pad_maximum_fusion.ext_ref), custom_call_target="tpu_custom_call" | custom-call | flops 40000000000 | bytes 1000000 | tf_op jit(solution)/shard_map/near/pallas_call | solution.py:457
  170.0 0.9 pad_maximum_fusion.1.leaf_ref
  170.9 76.9 %far.1 = f32[12,4,8,256]{3,2,1,0:T(8,128)} custom-call(s32[2]{0:T(128)} %pad_add_fusion.scalar_ref, s32[80]{0:T(128)} %constant.30.clone.shift_ref, s32[64]{0:T(128)} %reshape.14.counts_ref, f32[2,3,10,14,128]{4,3,2,1,0:T(8,128)} %pad_maximum_fusion.1.leaf_ref, f32[32,24,128]{2,1,0:T(8,128)} %bitcast.9, f32[32,16,256]{2,1,0:T(8,128)} %near.1.near_ref, ...), custom_call_target="tpu_custom_call" | custom-call | flops 10000000000 | bytes 1000000 | tf_op jit(solution)/shard_map/far/pallas_call | solution.py:483
  (23 shorter events, 0.2 us)
Async XLA Ops:
  0.8 1.0 copy-start
  1.7 103.7 %collective-permute-start.4 = (f32[6,1,8,256]{3,2,1,0:T(8,128)S(1)}, f32[6,1,8,256]{3,2,1,0:T(8,128)S(1)}, u32[]{:S(2)}, u32[]{:S(2)}) collective-permute-start(f32[6,1,8,256]{3,2,1,0:T(8,128)S(1)} %get-tuple-element.13), channel_id=1, source_target_pairs={{0,4},{4,8},{8,12},{12,16},{16,20},{20,24},{24,28},{1,5},{5,9},{9,... | collective-permute-start | bytes 147464 | tf_op jit(solution)/shard_map/ppermute | solution.py:405
  4.1 2.1 copy-start.2
  4.1 101.4 %collective-permute-start.5 = (f32[6,1,8,256]{3,2,1,0:T(8,128)S(1)}, f32[6,1,8,256]{3,2,1,0:T(8,128)S(1)}, u32[]{:S(2)}, u32[]{:S(2)}) collective-permute-start(f32[6,1,8,256]{3,2,1,0:T(8,128)S(1)} %get-tuple-element.14), channel_id=1, source_target_pairs={{4,0},{8,4},{12,8},{16,12},{20,16},{24,20},{28,24},{5,1},{9,5},{13... | collective-permute-start | bytes 147464 | tf_op jit(solution)/shard_map/ppermute | solution.py:407
  20.5 7.1 %copy-start.4 = (f32[24,128]{1,0:T(8,128)S(1)}, f32[24,128]{1,0:T(8,128)}, u32[]{:S(2)}) copy-start(f32[24,128]{1,0:T(8,128)} %get-tuple-element.8) | copy-start | bytes 36868
  20.5 87.8 %collective-permute-start.1 = (f32[2,3,3,8,128]{4,3,2,1,0:T(8,128)S(1)}, f32[2,3,3,8,128]{4,3,2,1,0:T(8,128)S(1)}, u32[]{:S(2)}, u32[]{:S(2)}) collective-permute-start(f32[2,3,3,8,128]{4,3,2,1,0:T(8,128)S(1)} %get-tuple-element.15), channel_id=1, source_target_pairs={{4,0},{8,4},{12,8},{16,12},{20,16},{24,20},{28,24},{5,1},{9,5},{13... | collective-permute-start | bytes 221192 | tf_op jit(solution)/shard_map/ppermute | solution.py:407
  21.8 86.5 %collective-permute-start = (f32[2,3,3,8,128]{4,3,2,1,0:T(8,128)S(1)}, f32[2,3,3,8,128]{4,3,2,1,0:T(8,128)S(1)}, u32[]{:S(2)}, u32[]{:S(2)}) collective-permute-start(f32[2,3,3,8,128]{4,3,2,1,0:T(8,128)S(1)} %get-tuple-element.16), channel_id=1, source_target_pairs={{0,4},{4,8},{8,12},{12,16},{16,20},{20,24},{24,28},{1,5},{5,9},{9,... | collective-permute-start | bytes 221192 | tf_op jit(solution)/shard_map/ppermute | solution.py:405
  104.1 0.7 copy-start.3
  105.5 2.8 %copy-start.1 = (f32[2,3,4,8,128]{4,3,2,1,0:T(8,128)S(1)}, f32[2,3,4,8,128]{4,3,2,1,0:T(8,128)}, u32[]{:S(2)}) copy-start(f32[2,3,4,8,128]{4,3,2,1,0:T(8,128)} %get-tuple-element.7) | copy-start | bytes 294916
  105.5 8.7 %collective-permute-start.6 = (f32[6,6,1,256]{3,2,1,0:T(1,128)S(1)}, f32[6,6,1,256]{3,2,1,0:T(1,128)S(1)}, u32[]{:S(2)}, u32[]{:S(2)}) collective-permute-start(f32[6,6,1,256]{3,2,1,0:T(1,128)S(1)} %get-tuple-element.9), channel_id=1, source_target_pairs={{0,1},{1,2},{2,3},{4,5},{5,6},{6,7},{8,9},{9,10},{10,11},{12,13},{... | collective-permute-start | bytes 110600 | tf_op jit(solution)/shard_map/ppermute | solution.py:405
  107.0 7.3 %collective-permute-start.7 = (f32[6,6,1,256]{3,2,1,0:T(1,128)S(1)}, f32[6,6,1,256]{3,2,1,0:T(1,128)S(1)}, u32[]{:S(2)}, u32[]{:S(2)}) collective-permute-start(f32[6,6,1,256]{3,2,1,0:T(1,128)S(1)} %get-tuple-element.10), channel_id=1, source_target_pairs={{1,0},{2,1},{3,2},{5,4},{6,5},{7,6},{9,8},{10,9},{11,10},{13,12},{... | collective-permute-start | bytes 110600 | tf_op jit(solution)/shard_map/ppermute | solution.py:407
  108.4 61.6 %collective-permute-start.2 = (f32[2,3,10,3,128]{4,3,2,1,0:T(4,128)S(1)}, f32[2,3,10,3,128]{4,3,2,1,0:T(4,128)S(1)}, u32[]{:S(2)}, u32[]{:S(2)}) collective-permute-start(f32[2,3,10,3,128]{4,3,2,1,0:T(4,128)S(1)} %get-tuple-element.11), channel_id=1, source_target_pairs={{0,1},{1,2},{2,3},{4,5},{5,6},{6,7},{8,9},{9,10},{10,11},{12,13},{... | collective-permute-start | bytes 276488 | tf_op jit(solution)/shard_map/ppermute | solution.py:405
  113.0 57.0 %collective-permute-start.3 = (f32[2,3,10,3,128]{4,3,2,1,0:T(4,128)S(1)}, f32[2,3,10,3,128]{4,3,2,1,0:T(4,128)S(1)}, u32[]{:S(2)}, u32[]{:S(2)}) collective-permute-start(f32[2,3,10,3,128]{4,3,2,1,0:T(4,128)S(1)} %get-tuple-element.12), channel_id=1, source_target_pairs={{1,0},{2,1},{3,2},{5,4},{6,5},{7,6},{9,8},{10,9},{11,10},{13,12},{... | collective-permute-start | bytes 276488 | tf_op jit(solution)/shard_map/ppermute | solution.py:407

commit v2 on v1

--- a/solution.py
+++ b/solution.py
@@ -60,37 +60,35 @@
 def up_kernel(size_x, size_y, pack_ref, rows_ref, cols_ref, inverse_ref, leaf_ref, top_ref, check):
     point = [rows_ref[j : j + 1, :] for j in range(3)]
 
-    def column(index, carry):
-        i = index // size_y
-        j = index % size_y
+    def one_column(i, j):
         row = [pack_ref[c, i, pl.ds(j, 1), :] for c in range(6)]
+        charge = jnp.concatenate(row[3:] + [jnp.zeros((5, 2 * LANES), F32)], axis=0)
         for half in range(2):
             lanes = slice(half * LANES, (half + 1) * LANES)
-            delta = []
-            for axis in range(3):
-                source = jnp.broadcast_to(row[axis][:, lanes], (LANES, LANES)).T
-                delta.append(1.5 * point[axis] - source)
+            delta = [1.5 * cols_ref[axis] - row[axis][:, lanes] for axis in range(3)]
             kernel = lax.rsqrt(
                 delta[0] * delta[0] + delta[1] * delta[1] + delta[2] * delta[2] + SMOOTH2
             )
-            charge = jnp.concatenate(
-                [row[3 + c][:, lanes] for c in range(3)] + [jnp.zeros((5, LANES), F32)], axis=0
-            )
-            c_high, c_low = split(charge)
-            k_high, k_low = split(kernel)
-            total = bdot(
-                two_terms(
-                    jnp.concatenate([c_high, c_low], axis=0),
-                    jnp.zeros((16, LANES), BF16),
-                )[:16],
-                jnp.concatenate([k_high, k_low], axis=0),
+            high, low = split(charge[:, lanes])
+            both = jnp.concatenate([high, low], axis=0)
+            first = jnp.concatenate([both, both], axis=1)
+            total = lax.dot_general(
+                first,
+                jnp.concatenate(split(kernel), axis=1),
+                (((1,), (1,)), ((), ())),
+                preferred_element_type=F32,
             )
             total = total[:8] + total[8:]
             for c in range(3):
                 check[half, c, i, pl.ds(j, 1), :] = total[c : c + 1]
-        return carry
-
-    lax.fori_loop(0, size_x * size_y, column, 0)
+
+    def columns(index, carry):
+        for k in range(4):
+            step = index * 4 + k
+            one_column(step // size_y, step % size_y)
+        return carry
+
+    lax.fori_loop(0, size_x * size_y // 4, columns, 0)
     matrix = inverse_ref[...]
     rows = 6 * size_x * size_y
     charges = 0.5 * dot_nt(check[...].reshape(rows, LANES), matrix)
@@ -126,6 +124,9 @@
     ext_y = size_y + 2
     lane = lax.broadcasted_iota(jnp.int32, (1, 2 * LANES), 1)
     lift = jnp.where(lane < LANES, -0.5, 0.5).astype(F32)
+    wide_row = lax.broadcasted_iota(jnp.int32, (16, 2 * LANES), 0)
+    level = wide_row // 3
+    kind = wide_row % 3
 
     def prepare(index, carry):
         i = index // ext_y
@@ -138,21 +139,40 @@
                 spread[index, axis, lanes, :] = jnp.broadcast_to(
                     value[:, lanes], (LANES, LANES)
                 ).T
-        zero = jnp.zeros_like(x)
-        one = jnp.ones_like(x)
-
-        def weighted(factors):
-            return jnp.concatenate(
-                [factor * row[3 + c] for factor in factors for c in range(3)] + [zero], axis=0
-            )
-
-        moments[index, 0] = weighted([one, x, y, z, x * x + y * y + z * z])
-        moments[index, 1] = weighted([zero, one, zero, zero, 2.0 * x])
-        moments[index, 2] = weighted([zero, zero, one, zero, 2.0 * y])
-        moments[index, 3] = weighted([zero, zero, zero, zero, one])
-        return carry
-
-    lax.fori_loop(0, (size_x + 2) * ext_y, prepare, 0)
+        wide = (16, 2 * LANES)
+        charge = jnp.where(
+            kind == 0,
+            jnp.broadcast_to(row[3], wide),
+            jnp.where(kind == 1, jnp.broadcast_to(row[4], wide), jnp.broadcast_to(row[5], wide)),
+        )
+        charge = jnp.where(level < 5, charge, 0.0)
+        square = x * x + y * y + z * z
+        factor = jnp.where(
+            level == 0,
+            1.0,
+            jnp.where(
+                level == 1,
+                jnp.broadcast_to(x, wide),
+                jnp.where(
+                    level == 2,
+                    jnp.broadcast_to(y, wide),
+                    jnp.where(
+                        level == 3, jnp.broadcast_to(z, wide), jnp.broadcast_to(square, wide)
+                    ),
+                ),
+            ),
+        )
+        moments[index, 0] = charge * factor
+        moments[index, 1] = charge * jnp.where(
+            level == 1, 1.0, jnp.where(level == 4, jnp.broadcast_to(2.0 * x, wide), 0.0)
+        )
+        moments[index, 2] = charge * jnp.where(
+            level == 2, 1.0, jnp.where(level == 4, jnp.broadcast_to(2.0 * y, wide), 0.0)
+        )
+        moments[index, 3] = jnp.where(level == 4, charge, 0.0)
+        return carry
+
+    lax.fori_loop(0, (size_x + 2) * ext_y, prepare, 0, unroll=2)
 
     def target(index, carry):
         i = index // size_y
@@ -197,15 +217,73 @@
     lax.fori_loop(0, size_x * size_y, target, 0)
 
 
+def leaf_kernel(size_x, size_y, leaf_ref, rows_ref, cols_ref, down_ref, base):
+    for axis in range(3):
+        base[axis] = 0.9 * rows_ref[axis : axis + 1, :] - 0.9 * cols_ref[axis]
+    down_ref[...] = jnp.zeros_like(down_ref)
+    odd_y = lax.broadcasted_iota(jnp.int32, (size_y, LANES), 0) % 2
+    near_y = {-3: jnp.where(odd_y == 1, 1.0, 0.0), 3: jnp.where(odd_y == 0, 1.0, 0.0)}
+
+    def one_row(shift_x, shifts_y):
+        dx = base[0] - shift_x.astype(F32)
+        tables = []
+        highs = []
+        lows = []
+        for shift_y in shifts_y:
+            dy = base[1] - float(shift_y)
+            flat = dx * dx + dy * dy + SMOOTH2
+            table = []
+            for shift_z in (-1, 0, 1):
+                dz = base[2] - float(shift_z)
+                table.append(lax.rsqrt(flat + dz * dz).astype(BF16))
+            tables.append(jnp.concatenate([table[1], table[0]], axis=1))
+            tables.append(jnp.concatenate([table[2], table[1]], axis=1))
+            for depth in range(2):
+                pieces = []
+                for c in range(3):
+                    for x in range(size_x):
+                        near_x = (shift_x > -3) if x % 2 == 0 else (shift_x < 3)
+                        piece = jnp.where(
+                            near_x,
+                            leaf_ref[depth, c, x + 3 + shift_x, 3 + shift_y : 3 + shift_y + size_y],
+                            0.0,
+                        )
+                        if abs(shift_y) == 3:
+                            piece = piece * near_y[shift_y]
+                        pieces.append(piece)
+                high, low = split(jnp.concatenate(pieces, axis=0))
+                highs.append(high)
+                lows.append(low)
+        rows = 3 * size_x * size_y
+        both = bdot(
+            jnp.concatenate(
+                [jnp.concatenate(highs, axis=1), jnp.concatenate(lows, axis=1)], axis=0
+            ),
+            jnp.concatenate(tables, axis=0),
+        )
+        down_ref[...] += both[:rows] + both[rows:]
+
+    def outer(step, carry):
+        one_row(jnp.where(step < 2, step - 3, step), (-3, -2, -1, 0, 1, 2, 3))
+        return carry
+
+    def inner(step, carry):
+        one_row(step - 1, (-3, -2, 2, 3))
+        return carry
+
+    lax.fori_loop(0, 4, outer, 0)
+    lax.fori_loop(0, 3, inner, 0)
+
+
 def far_kernel(
     size_x,
     size_y,
     tops_x,
     tops_y,
+    chunk,
     scalar_ref,
-    shift_ref,
     counts_ref,
-    leaf_ref,
+    down_ref,
     tops_ref,
     near_ref,
     pack_ref,
@@ -227,100 +305,61 @@
     along = tops_y + half_y - 1
     point = [rows_ref[j : j + 1, :] for j in range(3)]
     for axis in range(3):
-        base[axis] = point[axis] - cols_ref[axis]
+        base[axis] = 1.8 * point[axis] - 1.8 * cols_ref[axis]
 
     windows[...] = jnp.zeros_like(windows)
-
-    def place(index, carry):
-        i = index // tops_y
-        j = index % tops_y
-        device = (i // half_x) * (tops_y // half_y) + j // half_y
-        inside = (i % half_x) * half_y + j % half_y
+    mine = scalar_ref[2]
+    lanes_y = tops_y // half_y
+
+    def place(device, carry):
+        slot = jnp.bitwise_xor(device, mine)
+        i = (device // lanes_y) * half_x
+        j = (device % lanes_y) * half_y
         for c in range(3):
-            row = tops_ref[device, pl.ds(c * half_x * half_y + inside, 1), :]
-            for x in range(half_x):
-                windows[
-                    i + half_x - 1 - x, pl.ds((j + half_y - 1) * group + x * 4 + c, 1), :
-                ] = row
-        return carry
-
-    lax.fori_loop(0, tops_x * tops_y, place, 0)
+            for p in range(half_x):
+                for q in range(half_y):
+                    row = tops_ref[slot, (c * half_x + p) * half_y + q, :][None]
+                    for x in range(half_x):
+                        windows[
+                            i + p + half_x - 1 - x,
+                            pl.ds((j + q + half_y - 1) * group + x * 4 + c, 1),
+                            :,
+                        ] = row
+        return carry
+
+    lax.fori_loop(0, tops_ref.shape[0], place, 0)
     first_x = scalar_ref[0]
     first_y = scalar_ref[1]
     top_down[...] = jnp.zeros_like(top_down)
-
-    def top_row(wx, carry):
+    parts = -(-along // chunk)
+
+    def top_row(step, carry):
+        wx = step // parts
+        start = (step % parts) * chunk
         gap_x = first_x - (wx - (half_x - 1))
-        dx = 1.8 * base[0] + 2.0 * gap_x.astype(F32)
-        dz = 1.8 * base[2]
-        squares = dx * dx + dz * dz + SMOOTH2
-
-        def top_step(wy, inner):
+        dx = base[0] + 2.0 * gap_x.astype(F32)
+        squares = dx * dx + base[2] * base[2] + SMOOTH2
+        tables = []
+        pieces = []
+        for k in range(chunk):
+            wy = start + k
             gap_y = first_y - (wy - (half_y - 1))
             distant = (jnp.abs(gap_x) >= 2) | (jnp.abs(gap_y) >= 2)
-            dy = 1.8 * base[1] + 2.0 * gap_y.astype(F32)
-            table = lax.rsqrt(squares + dy * dy)
-            t_high, t_low = split(table)
+            dy = base[1] + 2.0 * gap_y.astype(F32)
+            tables.append(lax.rsqrt(squares + dy * dy).astype(BF16))
             rows = windows[wx, pl.ds(wy * group, half_y * group), :]
-            rows = jnp.where(distant, rows, 0.0)
-            r_high, r_low = split(rows)
-            both = bdot(jnp.concatenate([r_high, r_low], axis=0), t_high)
-            top_down[...] += both[: half_y * group] + both[half_y * group :] + bdot(r_high, t_low)
-            return inner
-
-        return lax.fori_loop(0, along, top_step, carry)
-
-    lax.fori_loop(0, across, top_row, 0)
+            pieces.append(jnp.where(distant, rows, 0.0))
+        high, low = split(jnp.concatenate(pieces, axis=1))
+        top_down[...] += bdot(
+            jnp.concatenate([high, low], axis=0), jnp.concatenate(tables, axis=0)
+        )
+        return carry
+
+    lax.fori_loop(0, across * parts, top_row, 0)
     matrix = inverse_ref[...]
-    top_local = dot_nt(top_down[...], matrix)
-
-    down[...] = jnp.zeros_like(down)
-    odd_y = lax.broadcasted_iota(jnp.int32, (size_y, LANES), 0) % 2
-
-    def leaf_step(step, carry):
-        shift_x = shift_ref[2 * step]
-        shift_y = shift_ref[2 * step + 1]
-        dx = 0.9 * base[0] - shift_x.astype(F32)
-        dy = 0.9 * base[1] - shift_y.astype(F32)
-        flat = dx * dx + dy * dy + SMOOTH2
-        tables = []
-        for shift_z in (-1, 0, 1):
-            dz = 0.9 * base[2] - float(shift_z)
-            tables.append(split(lax.rsqrt(flat + dz * dz)))
-        wide = [
-            jnp.concatenate(
-                [
-                    jnp.concatenate([tables[1][t], tables[0][t]], axis=1),
-                    jnp.concatenate([tables[2][t], tables[1][t]], axis=1),
-                ],
-                axis=0,
-            )
-            for t in range(2)
-        ]
-        near_y = jnp.where(
-            ((shift_y > -3) | (odd_y == 1)) & ((shift_y < 3) | (odd_y == 0)), 1.0, 0.0
-        )
-        highs = []
-        lows = []
-        for depth in range(2):
-            pieces = []
-            for c in range(3):
-                for x in range(size_x):
-                    near_x = (shift_x > -3) if x % 2 == 0 else (shift_x < 3)
-                    pieces.append(
-                        leaf_ref[depth, c, x + 3 + shift_x, pl.ds(3 + shift_y, size_y), :]
-                        * jnp.where(near_x, near_y, 0.0)
-                    )
-            high, low = split(jnp.concatenate(pieces, axis=0))
-            highs.append(high)
-            lows.append(low)
-        high = jnp.concatenate(highs, axis=1)
-        low = jnp.concatenate(lows, axis=1)
-        down[...] += bdot(high, wide[0]) + bdot(low, wide[0]) + bdot(high, wide[1])
-        return carry
-
-    lax.fori_loop(0, shift_ref.shape[0] // 2, leaf_step, 0)
-
+    rows = half_y * group
+    top_local = dot_nt(top_down[:rows] + top_down[rows:], matrix)
+    down[...] = down_ref[...]
     for a in range(2):
         for b in range(2):
             for e in range(2):
@@ -347,7 +386,7 @@
 
     lane = lax.broadcasted_iota(jnp.int32, (1, LANES), 1)
 
-    def column(index, carry):
+    def one_column(index):
         i = index // size_y
         j = index % size_y
         row = [pack_ref[c, i, pl.ds(j, 1), :] for c in range(3)]
@@ -390,9 +429,29 @@
             out_ref[c, i, pl.ds(j, 1), :] = potential[c : c + 1]
             for axis in range(3):
                 out_ref[3 + 3 * c + axis, i, pl.ds(j, 1), :] = slopes[axis][c : c + 1]
-        return carry
-
-    lax.fori_loop(0, size_x * size_y, column, 0)
+
+    def columns(index, carry):
+        for k in range(4):
+            one_column(index * 4 + k)
+        return carry
+
+    lax.fori_loop(0, size_x * size_y // 4, columns, 0)
+
+
+def gathered(block):
+    held = block[None]
+    for axis in ("gy", "gx"):
+        count = lax.axis_size(axis)
+        bit = 1
+        while bit < count:
+            radix = 4 if bit * 4 <= count else 2
+            received = [
+                lax.ppermute(held, axis, [(i, i ^ (k * bit)) for i in range(count)])
+                for k in range(1, radix)
+            ]
+            held = jnp.concatenate([held] + received, axis=0)
+            bit *= radix
+    return held
 
 
 def extended(cells, sides):
@@ -452,7 +511,7 @@
 
     neighbours = extended(pack, (("gx", 1, 1), ("gy", 2, 1)))
     border = extended(leaf_charges, (("gx", 2, 3), ("gy", 3, 3)))
-    gathered = lax.all_gather(top_charges, ("gx", "gy"), axis=0)
+    tops = gathered(top_charges)
 
     near = pl.pallas_call(
         functools.partial(near_kernel, size_x, size_y),
@@ -466,48 +525,40 @@
         name="near",
     )(neighbours)
 
-    shifts = np.array(
-        [
-            (x, y)
-            for x in range(-3, 4)
-            for y in range(-3, 4)
-            if abs(x) >= 2 or abs(y) >= 2
-        ],
-        np.int32,
-    ).reshape(-1)
-    first = jnp.stack([lax.axis_index("gx") * half_x, lax.axis_index("gy") * half_y])
+    down = pl.pallas_call(
+        functools.partial(leaf_kernel, size_x, size_y),
+        out_shape=jax.ShapeDtypeStruct((3 * size_x * size_y, 2 * LANES), F32),
+        scratch_shapes=[pltpu.VMEM((3, LANES, LANES), F32)],
+        compiler_params=params,
+        cost_estimate=pl.CostEstimate(flops=6 * 10**9, bytes_accessed=10**6, transcendentals=0),
+        name="leaf",
+    )(border, rows, cols)
+
+    gx = lax.axis_index("gx")
+    gy = lax.axis_index("gy")
+    scalars = jnp.stack([gx * half_x, gy * half_y, gx * lanes_y + gy]).astype(jnp.int32)
     across = tops_x + half_x - 1
-    along = tops_y + 2 * half_y - 2
+    along = tops_y + half_y - 1
+    parts = -(-along // 20)
+    chunk = -(-along // parts)
     smem = pl.BlockSpec(memory_space=pltpu.SMEM)
     vmem = pl.BlockSpec(memory_space=pltpu.VMEM)
     return pl.pallas_call(
-        functools.partial(far_kernel, size_x, size_y, tops_x, tops_y),
+        functools.partial(far_kernel, size_x, size_y, tops_x, tops_y, chunk),
         out_shape=jax.ShapeDtypeStruct((12, size_x, size_y, depth * LANES), F32),
-        in_specs=[smem] * 3 + [vmem] * 8,
+        in_specs=[smem] * 2 + [vmem] * 8,
         out_specs=vmem,
         scratch_shapes=[
             pltpu.VMEM((3, LANES, LANES), F32),
-            pltpu.VMEM((across, along * half_x * 4, LANES), F32),
+            pltpu.VMEM((across, (parts * chunk + half_y - 1) * half_x * 4, LANES), F32),
             pltpu.VMEM((3 * size_x * size_y, 2 * LANES), F32),
-            pltpu.VMEM((half_y * half_x * 4, LANES), F32),
+            pltpu.VMEM((2 * half_y * half_x * 4, LANES), F32),
             pltpu.VMEM((2, 3, size_x, size_y, LANES), F32),
         ],
         compiler_params=params,
         cost_estimate=pl.CostEstimate(flops=10**10, bytes_accessed=10**6, transcendentals=0),
         name="far",
-    )(
-        first.astype(jnp.int32),
-        jnp.asarray(shifts),
-        counts.reshape(-1),
-        border,
-        gathered,
-        near,
-        pack,
-        rows,
-        cols,
-        patterns,
-        matrix,
-    )
+    )(scalars, counts.reshape(-1), down, tops, near, pack, rows, cols, patterns, matrix)
 
 
 def solution(mesh):

time: 250 us -> 122 us (0.49)
  blocking collectives: 76.5 us -> 0 us
  Pallas kernels: 144 us -> 78.4 us
  starting transfers between devices: 19.4 us -> 33.4 us
    all_gather x1 -> x0, blocking collectives: 76.5 us -> none  [body(): gathered = lax.all_gather(top_charges, ('gx', 'gy'), axis=0)]
    pallas_call x1, Pallas kernels: 76.9 us -> 15.1 us  [body(): pl.pallas_call(functools.partial(far_kernel, size_x, size_y, tops_x, tops...]
    ppermute x0 -> x7, starting transfers between devices: none -> 14.9 us  [gathered(): lax.ppermute(held, axis, [(i, i ^ k * bit) for i in range(count)])]
    pallas_call x1, Pallas kernels: 12.7 us -> 6.14 us  [body(): pl.pallas_call(functools.partial(up_kernel, size_x, size_y), out_shape=(j...]
    pallas_call x0 -> x1, Pallas kernels: none -> 4.66 us  [body(): pl.pallas_call(functools.partial(leaf_kernel, size_x, size_y), out_shape=...]
  transfers between devices with their start and end apart: 8 -> 15, of which waited for: 0 -> 0; matrix products, arithmetic and copies ran while one was open for 2% -> 4% of each run, Pallas kernels for 27% -> 47%
where the time goes in v2:
time: 122 us; the launch traced here: 121 us
  Pallas kernels  78.4 us (64%)
  starting transfers between devices  33.4 us (27%)
  other arithmetic  4.86 us (4%)
  local copies, waits for them, and re-layouts  4.24 us (3%)
    pallas_call x1, Pallas kernels, body(): pl.pallas_call(functools.partial(near_kernel, size_x, size_y), out_shape=...  52.4 us
    pallas_call x1, Pallas kernels, body(): pl.pallas_call(functools.partial(far_kernel, size_x, size_y, tops_x, tops...  15.1 us
    ppermute x7, starting transfers between devices, gathered(): lax.ppermute(held, axis, [(i, i ^ k * bit) for i in range(count)])  14.9 us
    ppermute x4, starting transfers between devices, extended(): lax.ppermute(tail, axis, [(i, i + 1) for i in range(count - 1)])  13.4 us
    pallas_call x1, Pallas kernels, body(): pl.pallas_call(functools.partial(up_kernel, size_x, size_y), out_shape=(j...  6.14 us
    ppermute x4, starting transfers between devices, extended(): lax.ppermute(head, axis, [(i + 1, i) for i in range(count - 1)])  5.17 us
    pallas_call x1, Pallas kernels, body(): pl.pallas_call(functools.partial(leaf_kernel, size_x, size_y), out_shape=...  4.66 us
  transfers between devices with their start and end apart: 15, of which 0 were waited for; matrix products, arithmetic and copies ran while one was open for 4% of the time, Pallas kernels for 47%

profile of v2, /device:TPU:0, one launch (start us, length us, event | category | flops | bytes accessed | tf_op | source)
XLA Modules:
  0.0 121.2 jit_solution(13922617561471362954)
XLA Ops:
  0.0 0.8 fusion.2
  0.8 0.9 broadcast_multiply_fusion
  3.2 6.1 %up.1 = (f32[2,3,4,8,128]{4,3,2,1,0:T(8,128)}, f32[24,128]{1,0:T(8,128)}) custom-call(f32[6,4,8,256]{3,2,1,0:T(8,128)} %pad_maximum_fusion.2.pack_ref, f32[8,128]{1,0:T(8,128)} %constant.25.clone.rows_ref, f32[3,128,128]{2,1,0:T(8,128)} %constant.26.clone.cols_ref, f32[128,128]{1,0:T(8,128)} %pad.4.inverse_ref), custom_call_target="tpu_custom_call" | custom-call | flops 1000000000 | bytes 1000000 | tf_op jit(solution)/shard_map/up/pallas_call | solution.py:500
  9.3 3.0 %collective-permute-start.4 = (f32[1,24,128]{2,1,0:T(8,128)}, f32[1,24,128]{2,1,0:T(8,128)S(1)}, u32[]{:S(2)}, u32[]{:S(2)}) collective-permute-start(f32[1,24,128]{2,1,0:T(8,128)} %bitcast.12), channel_id=1, source_target_pairs={{0,1},{1,0},{2,3},{3,2},{4,5},{5,4},{6,7},{7,6},{8,9},{9,8},{10,11... | collective-permute-start | bytes 36872 | tf_op jit(solution)/shard_map/ppermute | solution.py:449
  12.4 2.6 %collective-permute-start.5 = (f32[1,24,128]{2,1,0:T(8,128)}, f32[1,24,128]{2,1,0:T(8,128)S(1)}, u32[]{:S(2)}, u32[]{:S(2)}) collective-permute-start(f32[1,24,128]{2,1,0:T(8,128)} %bitcast.13), channel_id=1, source_target_pairs={{0,2},{1,3},{2,0},{3,1},{4,6},{5,7},{6,4},{7,5},{8,10},{9,11},{10,... | collective-permute-start | bytes 36872 | tf_op jit(solution)/shard_map/ppermute | solution.py:449
  15.0 1.0 fusion.4
  15.9 1.3 %collective-permute-start = (f32[2,3,3,8,128]{4,3,2,1,0:T(8,128)S(1)}, f32[2,3,3,8,128]{4,3,2,1,0:T(8,128)S(1)}, u32[]{:S(2)}, u32[]{:S(2)}) collective-permute-start(f32[2,3,3,8,128]{4,3,2,1,0:T(8,128)S(1)} %get-tuple-element.16), channel_id=1, source_target_pairs={{0,4},{4,8},{8,12},{12,16},{16,20},{20,24},{24,28},{1,5},{5,9},{9,... | collective-permute-start | bytes 221192 | tf_op jit(solution)/shard_map/ppermute | solution.py:464
  17.2 1.3 %collective-permute-start.1 = (f32[2,3,3,8,128]{4,3,2,1,0:T(8,128)S(1)}, f32[2,3,3,8,128]{4,3,2,1,0:T(8,128)S(1)}, u32[]{:S(2)}, u32[]{:S(2)}) collective-permute-start(f32[2,3,3,8,128]{4,3,2,1,0:T(8,128)S(1)} %get-tuple-element.15), channel_id=1, source_target_pairs={{4,0},{8,4},{12,8},{16,12},{20,16},{24,20},{28,24},{5,1},{9,5},{13... | collective-permute-start | bytes 221192 | tf_op jit(solution)/shard_map/ppermute | solution.py:466
  20.0 5.0 %collective-permute-start.11 = (f32[6,1,8,256]{3,2,1,0:T(8,128)S(1)}, f32[6,1,8,256]{3,2,1,0:T(8,128)S(1)}, u32[]{:S(2)}, u32[]{:S(2)}) collective-permute-start(f32[6,1,8,256]{3,2,1,0:T(8,128)S(1)} %get-tuple-element.13), channel_id=1, source_target_pairs={{0,4},{4,8},{8,12},{12,16},{16,20},{20,24},{24,28},{1,5},{5,9},{9,... | collective-permute-start | bytes 147464 | tf_op jit(solution)/shard_map/ppermute | solution.py:464
  25.0 1.3 %collective-permute-start.12 = (f32[6,1,8,256]{3,2,1,0:T(8,128)S(1)}, f32[6,1,8,256]{3,2,1,0:T(8,128)S(1)}, u32[]{:S(2)}, u32[]{:S(2)}) collective-permute-start(f32[6,1,8,256]{3,2,1,0:T(8,128)S(1)} %get-tuple-element.14), channel_id=1, source_target_pairs={{4,0},{8,4},{12,8},{16,12},{20,16},{24,20},{28,24},{5,1},{9,5},{13... | collective-permute-start | bytes 147464 | tf_op jit(solution)/shard_map/ppermute | solution.py:466
  26.3 2.4 %collective-permute-start.7 = (f32[4,24,128]{2,1,0:T(8,128)S(1)}, f32[4,24,128]{2,1,0:T(8,128)S(1)}, u32[]{:S(2)}, u32[]{:S(2)}) collective-permute-start(f32[4,24,128]{2,1,0:T(8,128)S(1)} %pad_maximum_fusion.3), channel_id=1, source_target_pairs={{0,4},{4,0},{8,12},{12,8},{16,20},{20,16},{24,28},{28,24},{1,5},{5... | collective-permute-start | bytes 147464 | tf_op jit(solution)/shard_map/ppermute | solution.py:449
  28.8 2.5 %collective-permute-start.8 = (f32[4,24,128]{2,1,0:T(8,128)S(1)}, f32[4,24,128]{2,1,0:T(8,128)S(1)}, u32[]{:S(2)}, u32[]{:S(2)}) collective-permute-start(f32[4,24,128]{2,1,0:T(8,128)S(1)} %pad_maximum_fusion.3), channel_id=1, source_target_pairs={{0,8},{4,12},{8,0},{12,4},{16,24},{20,28},{24,16},{28,20},{1,9},{5... | collective-permute-start | bytes 147464 | tf_op jit(solution)/shard_map/ppermute | solution.py:449
  31.2 4.3 %collective-permute-start.9 = (f32[4,24,128]{2,1,0:T(8,128)S(1)}, f32[4,24,128]{2,1,0:T(8,128)S(1)}, u32[]{:S(2)}, u32[]{:S(2)}) collective-permute-start(f32[4,24,128]{2,1,0:T(8,128)S(1)} %pad_maximum_fusion.3), channel_id=1, source_target_pairs={{0,12},{4,8},{8,4},{12,0},{16,28},{20,24},{24,20},{28,16},{1,13},{... | collective-permute-start | bytes 147464 | tf_op jit(solution)/shard_map/ppermute | solution.py:449
  35.6 2.6 %collective-permute-start.13 = (f32[6,6,1,256]{3,2,1,0:T(1,128)S(1)}, f32[6,6,1,256]{3,2,1,0:T(1,128)S(1)}, u32[]{:S(2)}, u32[]{:S(2)}) collective-permute-start(f32[6,6,1,256]{3,2,1,0:T(1,128)S(1)} %get-tuple-element.9), channel_id=1, source_target_pairs={{0,1},{1,2},{2,3},{4,5},{5,6},{6,7},{8,9},{9,10},{10,11},{12,13},{... | collective-permute-start | bytes 110600 | tf_op jit(solution)/shard_map/ppermute | solution.py:464
  38.2 1.3 %collective-permute-start.14 = (f32[6,6,1,256]{3,2,1,0:T(1,128)S(1)}, f32[6,6,1,256]{3,2,1,0:T(1,128)S(1)}, u32[]{:S(2)}, u32[]{:S(2)}) collective-permute-start(f32[6,6,1,256]{3,2,1,0:T(1,128)S(1)} %get-tuple-element.10), channel_id=1, source_target_pairs={{1,0},{2,1},{3,2},{5,4},{6,5},{7,6},{9,8},{10,9},{11,10},{13,12},{... | collective-permute-start | bytes 110600 | tf_op jit(solution)/shard_map/ppermute | solution.py:466
  39.7 0.8 copy-done.1
  40.5 4.6 %collective-permute-start.2 = (f32[2,3,10,3,128]{4,3,2,1,0:T(4,128)S(1)}, f32[2,3,10,3,128]{4,3,2,1,0:T(4,128)S(1)}, u32[]{:S(2)}, u32[]{:S(2)}) collective-permute-start(f32[2,3,10,3,128]{4,3,2,1,0:T(4,128)S(1)} %get-tuple-element.11), channel_id=1, source_target_pairs={{0,1},{1,2},{2,3},{4,5},{5,6},{6,7},{8,9},{9,10},{10,11},{12,13},{... | collective-permute-start | bytes 276488 | tf_op jit(solution)/shard_map/ppermute | solution.py:464
  45.1 1.3 %collective-permute-start.3 = (f32[2,3,10,3,128]{4,3,2,1,0:T(4,128)S(1)}, f32[2,3,10,3,128]{4,3,2,1,0:T(4,128)S(1)}, u32[]{:S(2)}, u32[]{:S(2)}) collective-permute-start(f32[2,3,10,3,128]{4,3,2,1,0:T(4,128)S(1)} %get-tuple-element.12), channel_id=1, source_target_pairs={{1,0},{2,1},{3,2},{5,4},{6,5},{7,6},{9,8},{10,9},{11,10},{13,12},{... | collective-permute-start | bytes 276488 | tf_op jit(solution)/shard_map/ppermute | solution.py:466
  46.4 0.9 pad_maximum_fusion.ext_ref
  47.3 52.4 %near.1.near_ref = f32[32,16,256]{2,1,0:T(8,128)} custom-call(f32[6,6,10,256]{3,2,1,0:T(8,128)} %pad_maximum_fusion.ext_ref), custom_call_target="tpu_custom_call" | custom-call | flops 40000000000 | bytes 1000000 | tf_op jit(solution)/shard_map/near/pallas_call | solution.py:516
  99.8 0.9 pad_maximum_fusion.1.leaf_ref
  100.7 4.7 %leaf.1.down_ref = f32[96,256]{1,0:T(8,128)} custom-call(f32[2,3,10,14,128]{4,3,2,1,0:T(8,128)} %pad_maximum_fusion.1.leaf_ref, f32[8,128]{1,0:T(8,128)} %constant.25.clone.rows_ref, f32[3,128,128]{2,1,0:T(8,128)} %constant.26.clone.cols_ref), custom_call_target="tpu_custom_call" | custom-call | flops 6000000000 | bytes 1000000 | tf_op jit(solution)/shard_map/leaf/pallas_call | solution.py:528
  105.4 0.7 copy-done.5
  106.1 15.1 %far.1 = f32[12,4,8,256]{3,2,1,0:T(8,128)} custom-call(s32[3]{0:T(128)} %pad_add_fusion.scalar_ref, s32[64]{0:T(128)} %reshape.14.counts_ref, f32[96,256]{1,0:T(8,128)} %leaf.1.down_ref, f32[32,24,128]{2,1,0:T(8,128)} %copy-done.5, f32[32,16,256]{2,1,0:T(8,128)} %near.1.near_ref, f32[6,4,8,256]{3,2,1,0:T(8,128)} %pad_maximum_fusion.2.pack_ref, ...), custom_call_target="tpu_custom_call" | custom-call | flops 10000000000 | bytes 1000000 | tf_op jit(solution)/shard_map/far/pallas_call | solution.py:546
  (48 shorter events, 3.2 us)
Async XLA Ops:
  0.8 1.0 copy-start
  1.7 0.8 copy-start.2
  9.3 10.7 %collective-permute-start.4 = (f32[1,24,128]{2,1,0:T(8,128)}, f32[1,24,128]{2,1,0:T(8,128)S(1)}, u32[]{:S(2)}, u32[]{:S(2)}) collective-permute-start(f32[1,24,128]{2,1,0:T(8,128)} %bitcast.12), channel_id=1, source_target_pairs={{0,1},{1,0},{2,3},{3,2},{4,5},{5,4},{6,7},{7,6},{8,9},{9,8},{10,11... | collective-permute-start | bytes 36872 | tf_op jit(solution)/shard_map/ppermute | solution.py:449
  12.4 12.6 %collective-permute-start.5 = (f32[1,24,128]{2,1,0:T(8,128)}, f32[1,24,128]{2,1,0:T(8,128)S(1)}, u32[]{:S(2)}, u32[]{:S(2)}) collective-permute-start(f32[1,24,128]{2,1,0:T(8,128)} %bitcast.13), channel_id=1, source_target_pairs={{0,2},{1,3},{2,0},{3,1},{4,6},{5,7},{6,4},{7,5},{8,10},{9,11},{10,... | collective-permute-start | bytes 36872 | tf_op jit(solution)/shard_map/ppermute | solution.py:449
  15.0 11.3 %collective-permute-start.6 = (f32[1,24,128]{2,1,0:T(8,128)}, f32[1,24,128]{2,1,0:T(8,128)S(1)}, u32[]{:S(2)}, u32[]{:S(2)}) collective-permute-start(f32[1,24,128]{2,1,0:T(8,128)} %bitcast.14), channel_id=1, source_target_pairs={{0,3},{1,2},{2,1},{3,0},{4,7},{5,6},{6,5},{7,4},{8,11},{9,10},{10,... | collective-permute-start | bytes 36872 | tf_op jit(solution)/shard_map/ppermute | solution.py:449
  15.0 3.6 %copy-start.3 = (f32[24,128]{1,0:T(8,128)S(1)}, f32[24,128]{1,0:T(8,128)}, u32[]{:S(2)}) copy-start(f32[24,128]{1,0:T(8,128)} %get-tuple-element.8) | copy-start | bytes 36868
  15.9 23.7 %collective-permute-start = (f32[2,3,3,8,128]{4,3,2,1,0:T(8,128)S(1)}, f32[2,3,3,8,128]{4,3,2,1,0:T(8,128)S(1)}, u32[]{:S(2)}, u32[]{:S(2)}) collective-permute-start(f32[2,3,3,8,128]{4,3,2,1,0:T(8,128)S(1)} %get-tuple-element.16), channel_id=1, source_target_pairs={{0,4},{4,8},{8,12},{12,16},{16,20},{20,24},{24,28},{1,5},{5,9},{9,... | collective-permute-start | bytes 221192 | tf_op jit(solution)/shard_map/ppermute | solution.py:464
  17.2 23.2 %collective-permute-start.1 = (f32[2,3,3,8,128]{4,3,2,1,0:T(8,128)S(1)}, f32[2,3,3,8,128]{4,3,2,1,0:T(8,128)S(1)}, u32[]{:S(2)}, u32[]{:S(2)}) collective-permute-start(f32[2,3,3,8,128]{4,3,2,1,0:T(8,128)S(1)} %get-tuple-element.15), channel_id=1, source_target_pairs={{4,0},{8,4},{12,8},{16,12},{20,16},{24,20},{28,24},{5,1},{9,5},{13... | collective-permute-start | bytes 221192 | tf_op jit(solution)/shard_map/ppermute | solution.py:466
  18.6 0.7 copy-start.4
  20.0 8.8 %collective-permute-start.11 = (f32[6,1,8,256]{3,2,1,0:T(8,128)S(1)}, f32[6,1,8,256]{3,2,1,0:T(8,128)S(1)}, u32[]{:S(2)}, u32[]{:S(2)}) collective-permute-start(f32[6,1,8,256]{3,2,1,0:T(8,128)S(1)} %get-tuple-element.13), channel_id=1, source_target_pairs={{0,4},{4,8},{8,12},{12,16},{16,20},{20,24},{24,28},{1,5},{5,9},{9,... | collective-permute-start | bytes 147464 | tf_op jit(solution)/shard_map/ppermute | solution.py:464
  25.0 6.2 %collective-permute-start.12 = (f32[6,1,8,256]{3,2,1,0:T(8,128)S(1)}, f32[6,1,8,256]{3,2,1,0:T(8,128)S(1)}, u32[]{:S(2)}, u32[]{:S(2)}) collective-permute-start(f32[6,1,8,256]{3,2,1,0:T(8,128)S(1)} %get-tuple-element.14), channel_id=1, source_target_pairs={{4,0},{8,4},{12,8},{16,12},{20,16},{24,20},{28,24},{5,1},{9,5},{13... | collective-permute-start | bytes 147464 | tf_op jit(solution)/shard_map/ppermute | solution.py:466
  26.3 9.3 %collective-permute-start.7 = (f32[4,24,128]{2,1,0:T(8,128)S(1)}, f32[4,24,128]{2,1,0:T(8,128)S(1)}, u32[]{:S(2)}, u32[]{:S(2)}) collective-permute-start(f32[4,24,128]{2,1,0:T(8,128)S(1)} %pad_maximum_fusion.3), channel_id=1, source_target_pairs={{0,4},{4,0},{8,12},{12,8},{16,20},{20,16},{24,28},{28,24},{1,5},{5... | collective-permute-start | bytes 147464 | tf_op jit(solution)/shard_map/ppermute | solution.py:449
  28.8 9.4 %collective-permute-start.8 = (f32[4,24,128]{2,1,0:T(8,128)S(1)}, f32[4,24,128]{2,1,0:T(8,128)S(1)}, u32[]{:S(2)}, u32[]{:S(2)}) collective-permute-start(f32[4,24,128]{2,1,0:T(8,128)S(1)} %pad_maximum_fusion.3), channel_id=1, source_target_pairs={{0,8},{4,12},{8,0},{12,4},{16,24},{20,28},{24,16},{28,20},{1,9},{5... | collective-permute-start | bytes 147464 | tf_op jit(solution)/shard_map/ppermute | solution.py:449
  31.2 8.3 %collective-permute-start.9 = (f32[4,24,128]{2,1,0:T(8,128)S(1)}, f32[4,24,128]{2,1,0:T(8,128)S(1)}, u32[]{:S(2)}, u32[]{:S(2)}) collective-permute-start(f32[4,24,128]{2,1,0:T(8,128)S(1)} %pad_maximum_fusion.3), channel_id=1, source_target_pairs={{0,12},{4,8},{8,4},{12,0},{16,28},{20,24},{24,20},{28,16},{1,13},{... | collective-permute-start | bytes 147464 | tf_op jit(solution)/shard_map/ppermute | solution.py:449
  35.6 10.8 %collective-permute-start.13 = (f32[6,6,1,256]{3,2,1,0:T(1,128)S(1)}, f32[6,6,1,256]{3,2,1,0:T(1,128)S(1)}, u32[]{:S(2)}, u32[]{:S(2)}) collective-permute-start(f32[6,6,1,256]{3,2,1,0:T(1,128)S(1)} %get-tuple-element.9), channel_id=1, source_target_pairs={{0,1},{1,2},{2,3},{4,5},{5,6},{6,7},{8,9},{9,10},{10,11},{12,13},{... | collective-permute-start | bytes 110600 | tf_op jit(solution)/shard_map/ppermute | solution.py:464
  38.2 8.2 %collective-permute-start.14 = (f32[6,6,1,256]{3,2,1,0:T(1,128)S(1)}, f32[6,6,1,256]{3,2,1,0:T(1,128)S(1)}, u32[]{:S(2)}, u32[]{:S(2)}) collective-permute-start(f32[6,6,1,256]{3,2,1,0:T(1,128)S(1)} %get-tuple-element.10), channel_id=1, source_target_pairs={{1,0},{2,1},{3,2},{5,4},{6,5},{7,6},{9,8},{10,9},{11,10},{13,12},{... | collective-permute-start | bytes 110600 | tf_op jit(solution)/shard_map/ppermute | solution.py:466
  39.5 0.9 copy-start.1
  39.6 65.8 %collective-permute-start.10 = (f32[16,24,128]{2,1,0:T(8,128)S(1)}, f32[16,24,128]{2,1,0:T(8,128)S(1)}, u32[]{:S(2)}, u32[]{:S(2)}) collective-permute-start(f32[16,24,128]{2,1,0:T(8,128)S(1)} %get-tuple-element.17), channel_id=1, source_target_pairs={{0,16},{4,20},{8,24},{12,28},{16,0},{20,4},{24,8},{28,12},{1,17},{... | collective-permute-start | bytes 589832 | tf_op jit(solution)/shard_map/ppermute | solution.py:449
  40.5 59.2 %collective-permute-start.2 = (f32[2,3,10,3,128]{4,3,2,1,0:T(4,128)S(1)}, f32[2,3,10,3,128]{4,3,2,1,0:T(4,128)S(1)}, u32[]{:S(2)}, u32[]{:S(2)}) collective-permute-start(f32[2,3,10,3,128]{4,3,2,1,0:T(4,128)S(1)} %get-tuple-element.11), channel_id=1, source_target_pairs={{0,1},{1,2},{2,3},{4,5},{5,6},{6,7},{8,9},{9,10},{10,11},{12,13},{... | collective-permute-start | bytes 276488 | tf_op jit(solution)/shard_map/ppermute | solution.py:464
  45.1 54.7 %collective-permute-start.3 = (f32[2,3,10,3,128]{4,3,2,1,0:T(4,128)S(1)}, f32[2,3,10,3,128]{4,3,2,1,0:T(4,128)S(1)}, u32[]{:S(2)}, u32[]{:S(2)}) collective-permute-start(f32[2,3,10,3,128]{4,3,2,1,0:T(4,128)S(1)} %get-tuple-element.12), channel_id=1, source_target_pairs={{1,0},{2,1},{3,2},{5,4},{6,5},{7,6},{9,8},{10,9},{11,10},{13,12},{... | collective-permute-start | bytes 276488 | tf_op jit(solution)/shard_map/ppermute | solution.py:466
  105.4 0.8 copy-start.5

commit v3 on v2

--- a/solution.py
+++ b/solution.py
@@ -57,23 +57,76 @@
     return inverse * inverse * inverse
 
 
-def up_kernel(size_x, size_y, pack_ref, rows_ref, cols_ref, inverse_ref, leaf_ref, top_ref, check):
+SIDES = (-1, 1)
+WIDTH = 3
+
+
+def edge(side, size, width):
+    return 0 if side < 0 else size - width
+
+
+def landing(side, size, width):
+    return 0 if side < 0 else size + width
+
+
+def parcel_rows(size_x, size_y):
+    tops = 3 * (size_x // 2) * (size_y // 2)
+    leaves_x = 6 * WIDTH * size_y
+    leaves_y = 6 * (size_x + 2 * WIDTH) * WIDTH
+    near_x = leaves_x + 12 * size_y
+    near_y = leaves_y + 12 * (size_x + 2)
+    return (leaves_x, near_x, near_x + tops), (leaves_y, near_y, near_y + 3 * tops)
+
+
+def lies_inside(axis, side):
+    place = lax.axis_index(axis) + side
+    return jnp.where((place >= 0) & (place < lax.axis_size(axis)), 1.0, 0.0)
+
+
+def up_kernel(
+    size_x,
+    size_y,
+    counts_ref,
+    offsets_ref,
+    strengths_ref,
+    rows_ref,
+    cols_ref,
+    inverse_ref,
+    pack_ref,
+    leaf_ref,
+    top_ref,
+    matrix_ref,
+    *rest,
+):
+    parcels = rest[:2]
+    check = rest[2]
     point = [rows_ref[j : j + 1, :] for j in range(3)]
+    lane = lax.broadcasted_iota(jnp.int32, (1, 2 * LANES), 1)
+    expansion = inverse_ref.shape[0]
+    matrix_ref[...] = jnp.zeros_like(matrix_ref)
+    matrix_ref[:expansion, :expansion] = inverse_ref[...]
+    pack_ref[0:3] = offsets_ref[...]
 
     def one_column(i, j):
-        row = [pack_ref[c, i, pl.ds(j, 1), :] for c in range(6)]
-        charge = jnp.concatenate(row[3:] + [jnp.zeros((5, 2 * LANES), F32)], axis=0)
+        row = [offsets_ref[c, i, pl.ds(j, 1), :] for c in range(3)]
+        last = jnp.where(lane < LANES, counts_ref[i, j, 0], counts_ref[i, j, 1] + LANES)
+        charges = []
+        for c in range(3):
+            value = jnp.where(
+                lane < last, STRENGTH_SCALE * strengths_ref[c, i, pl.ds(j, 1), :], 0.0
+            )
+            pack_ref[3 + c, i, pl.ds(j, 1), :] = value
+            charges.append(value)
+        charge = jnp.concatenate(charges + [jnp.zeros((5, 2 * LANES), F32)], axis=0)
         for half in range(2):
             lanes = slice(half * LANES, (half + 1) * LANES)
             delta = [1.5 * cols_ref[axis] - row[axis][:, lanes] for axis in range(3)]
             kernel = lax.rsqrt(
                 delta[0] * delta[0] + delta[1] * delta[1] + delta[2] * delta[2] + SMOOTH2
             )
-            high, low = split(charge[:, lanes])
-            both = jnp.concatenate([high, low], axis=0)
-            first = jnp.concatenate([both, both], axis=1)
+            both = jnp.concatenate(split(charge[:, lanes]), axis=0)
             total = lax.dot_general(
-                first,
+                jnp.concatenate([both, both], axis=1),
                 jnp.concatenate(split(kernel), axis=1),
                 (((1,), (1,)), ((), ())),
                 preferred_element_type=F32,
@@ -89,7 +142,7 @@
         return carry
 
     lax.fori_loop(0, size_x * size_y // 4, columns, 0)
-    matrix = inverse_ref[...]
+    matrix = matrix_ref[...]
     rows = 6 * size_x * size_y
     charges = 0.5 * dot_nt(check[...].reshape(rows, LANES), matrix)
     leaf_ref[...] = charges.reshape(2, 3, size_x, size_y, LANES)
@@ -117,107 +170,276 @@
                     precision=HIGHEST,
                     preferred_element_type=F32,
                 )
-    top_ref[...] = dot_nt(total, matrix)
-
-
-def near_kernel(size_x, size_y, ext_ref, out_ref, spread, moments):
-    ext_y = size_y + 2
-    lane = lax.broadcasted_iota(jnp.int32, (1, 2 * LANES), 1)
-    lift = jnp.where(lane < LANES, -0.5, 0.5).astype(F32)
-    wide_row = lax.broadcasted_iota(jnp.int32, (16, 2 * LANES), 0)
-    level = wide_row // 3
-    kind = wide_row % 3
-
-    def prepare(index, carry):
-        i = index // ext_y
-        j = index % ext_y
-        row = [ext_ref[c, i, pl.ds(j, 1), :] for c in range(6)]
-        x, y, z = row[0], row[1], row[2] + lift
-        for axis, value in enumerate((x, y, z)):
+    tops = dot_nt(total, matrix)
+    top_ref[...] = tops
+    (_, second, end), _ = parcel_rows(size_x, size_y)
+    for side, parcel in zip(SIDES, parcels):
+        row = 0
+        start = edge(side, size_x, WIDTH)
+        for depth in range(2):
+            for c in range(3):
+                for x in range(start, start + WIDTH):
+                    parcel[row : row + size_y] = leaf_ref[depth, c, x]
+                    row += size_y
+        for c in range(6):
             for half in range(2):
                 lanes = slice(half * LANES, (half + 1) * LANES)
-                spread[index, axis, lanes, :] = jnp.broadcast_to(
-                    value[:, lanes], (LANES, LANES)
-                ).T
-        wide = (16, 2 * LANES)
-        charge = jnp.where(
-            kind == 0,
-            jnp.broadcast_to(row[3], wide),
-            jnp.where(kind == 1, jnp.broadcast_to(row[4], wide), jnp.broadcast_to(row[5], wide)),
+                parcel[row : row + size_y] = pack_ref[c, edge(side, size_x, 1), :, lanes]
+                row += size_y
+        parcel[second:end] = tops
+
+
+def turn_kernel(
+    size_x, size_y, leaf_ref, pack_ref, top_ref, below_ref, above_ref, low_ref, high_ref, tops_ref
+):
+    (_, near_x, end_x), (_, near_y, _) = parcel_rows(size_x, size_y)
+    count = end_x - near_x
+    for place, ref in ((0, below_ref), (2, above_ref)):
+        tops_ref[place * count : (place + 1) * count] = ref[near_x:end_x]
+    tops_ref[count : 2 * count] = top_ref[...]
+    inside = [lies_inside("gx", side) for side in SIDES]
+    for side, parcel in zip(SIDES, (low_ref, high_ref)):
+        row = 0
+        start = edge(side, size_y, WIDTH)
+        for depth in range(2):
+            for c in range(3):
+                for x in range(-WIDTH, size_x + WIDTH):
+                    if 0 <= x < size_x:
+                        value = leaf_ref[depth, c, x, start : start + WIDTH]
+                    else:
+                        which = int(x >= size_x)
+                        ref = (below_ref, above_ref)[which]
+                        cell = x - size_x if which else x + WIDTH
+                        at = ((depth * 3 + c) * WIDTH + cell) * size_y + start
+                        value = ref[at : at + WIDTH] * inside[which]
+                    parcel[row : row + WIDTH] = value
+                    row += WIDTH
+        start = edge(side, size_y, 1)
+        first, _, _ = parcel_rows(size_x, size_y)[0]
+        for c in range(6):
+            for x in range(-1, size_x + 1):
+                for half in range(2):
+                    if 0 <= x < size_x:
+                        lanes = slice(half * LANES, (half + 1) * LANES)
+                        value = pack_ref[c, x, start : start + 1, lanes]
+                    else:
+                        which = int(x >= size_x)
+                        ref = (below_ref, above_ref)[which]
+                        at = first + (c * 2 + half) * size_y + start
+                        value = ref[at : at + 1]
+                        if c >= 3:
+                            value = value * inside[which]
+                    parcel[row : row + 1] = value
+                    row += 1
+        parcel[near_y : near_y + 3 * count] = tops_ref[...]
+
+
+def near_masks():
+    row = lax.broadcasted_iota(jnp.int32, (16, 2 * LANES), 0)
+    lane = lax.broadcasted_iota(jnp.int32, (1, 2 * LANES), 1)
+    return row // 3, row % 3, jnp.where(lane < LANES, -0.5, 0.5).astype(F32)
+
+
+def prepare_column(row, slot, masks, spread, moments):
+    level, kind, lift = masks
+    x, y, z = row[0], row[1], row[2] + lift
+    square = x * x + y * y + z * z
+    for axis, value in enumerate((-2.0 * x, -2.0 * y, -2.0 * z, square)):
+        for half in range(2):
+            lanes = slice(half * LANES, (half + 1) * LANES)
+            spread[slot, axis, lanes, :] = jnp.broadcast_to(value[:, lanes], (LANES, LANES)).T
+
+    def wide(value):
+        return jnp.broadcast_to(value, (16, 2 * LANES))
+
+    charge = jnp.where(
+        kind == 0, wide(row[3]), jnp.where(kind == 1, wide(row[4]), wide(row[5]))
+    )
+    charge = jnp.where(level < 5, charge, 0.0)
+    factor = jnp.where(level == 3, wide(z), wide(square))
+    factor = jnp.where(level == 2, wide(y), factor)
+    factor = jnp.where(level == 1, wide(x), factor)
+    moments[slot, 0] = charge * jnp.where(level == 0, 1.0, factor)
+    last = jnp.where(level == 4, charge, 0.0)
+    moments[slot, 1] = jnp.where(level == 1, charge, last * wide(2.0 * x))
+    moments[slot, 2] = jnp.where(level == 2, charge, last * wide(2.0 * y))
+    moments[slot, 3] = last
+
+
+def near_sums(target, blocks, spread, moments):
+    total = jnp.zeros((32, 2 * LANES), F32)
+    for slot, shift_x, shift_y in blocks:
+        weight = (
+            moments[slot, 0]
+            + shift_x * moments[slot, 1]
+            + shift_y * moments[slot, 2]
+            + (shift_x * shift_x + shift_y * shift_y) * moments[slot, 3]
         )
-        charge = jnp.where(level < 5, charge, 0.0)
-        square = x * x + y * y + z * z
-        factor = jnp.where(
-            level == 0,
-            1.0,
-            jnp.where(
-                level == 1,
-                jnp.broadcast_to(x, wide),
-                jnp.where(
-                    level == 2,
-                    jnp.broadcast_to(y, wide),
-                    jnp.where(
-                        level == 3, jnp.broadcast_to(z, wide), jnp.broadcast_to(square, wide)
-                    ),
+        w_high, w_low = split(weight)
+        x = target[0] - shift_x
+        y = target[1] - shift_y
+        z = target[2]
+        square = x * x + y * y + z * z + SMOOTH2
+        for half in range(2):
+            part = slice(half * LANES, (half + 1) * LANES)
+            highs = []
+            lows = []
+            for side in range(2):
+                lanes = slice(side * LANES, (side + 1) * LANES)
+                distance = (
+                    (square[:, lanes] + spread[slot, 3, part, :])
+                    + x[:, lanes] * spread[slot, 0, part, :]
+                    + y[:, lanes] * spread[slot, 1, part, :]
+                    + z[:, lanes] * spread[slot, 2, part, :]
+                )
+                inverse = lax.rsqrt(distance)
+                high, low = split(inverse * inverse * inverse)
+                highs.append(high)
+                lows.append(low)
+            total = total + bdot(
+                two_terms(w_high[:, part], w_low[:, part]),
+                jnp.concatenate(
+                    [jnp.concatenate(highs, axis=1), jnp.concatenate(lows, axis=1)], axis=0
                 ),
-            ),
-        )
-        moments[index, 0] = charge * factor
-        moments[index, 1] = charge * jnp.where(
-            level == 1, 1.0, jnp.where(level == 4, jnp.broadcast_to(2.0 * x, wide), 0.0)
-        )
-        moments[index, 2] = charge * jnp.where(
-            level == 2, 1.0, jnp.where(level == 4, jnp.broadcast_to(2.0 * y, wide), 0.0)
-        )
-        moments[index, 3] = jnp.where(level == 4, charge, 0.0)
+            )
+    return total[:16] + total[16:]
+
+
+def run_tasks(size_y, tasks, table_ref, pack_ref, out_ref, lift, spread, moments, adds):
+    for start, amount, sources in tasks:
+        together = 1
+        while together * sources < 6 and amount % (2 * together) == 0:
+            together *= 2
+
+        def one(index, start, sources):
+            at = start + index * (2 + 3 * sources)
+            i = table_ref[at]
+            j = table_ref[at + 1]
+            target = [pack_ref[c, i, pl.ds(j, 1), :] for c in range(3)]
+            target[2] = target[2] + lift
+            blocks = [
+                (
+                    table_ref[at + 2 + 3 * k],
+                    table_ref[at + 3 + 3 * k].astype(F32),
+                    table_ref[at + 4 + 3 * k].astype(F32),
+                )
+                for k in range(sources)
+            ]
+            return i * size_y + j, near_sums(target, blocks, spread, moments)
+
+        def step(index, carry, start=start, sources=sources, together=together):
+            found = [one(index * together + k, start, sources) for k in range(together)]
+            for place, total in found:
+                out_ref[place] = total + out_ref[place] if adds else total
+            return carry
+
+        lax.fori_loop(0, amount // together, step, 0)
+
+
+def own_kernel(size_x, size_y, tasks, table_ref, pack_ref, out_ref, spread, moments):
+    masks = near_masks()
+
+    def prepare(index, carry):
+        for k in range(2):
+            slot = index * 2 + k
+            row = [pack_ref[c, slot // size_y, pl.ds(slot % size_y, 1), :] for c in range(6)]
+            prepare_column(row, slot, masks, spread, moments)
         return carry
 
-    lax.fori_loop(0, (size_x + 2) * ext_y, prepare, 0, unroll=2)
-
-    def target(index, carry):
-        i = index // size_y
-        j = index % size_y
-        row = [ext_ref[c, i + 1, pl.ds(j + 1, 1), :] for c in range(3)]
-        total = jnp.zeros((32, 2 * LANES), F32)
-        for shift_x in (-1, 0, 1):
-            for shift_y in (-1, 0, 1):
-                source = (i + 1 + shift_x) * ext_y + j + 1 + shift_y
-                weight = moments[source, 0]
-                if shift_x:
-                    weight = weight + float(shift_x) * moments[source, 1]
-                if shift_y:
-                    weight = weight + float(shift_y) * moments[source, 2]
-                if shift_x or shift_y:
-                    weight = weight + float(shift_x**2 + shift_y**2) * moments[source, 3]
-                w_high, w_low = split(weight)
-                place = [row[0] - float(shift_x), row[1] - float(shift_y), row[2] + lift]
-                for half in range(2):
-                    part = slice(half * LANES, (half + 1) * LANES)
-                    highs = []
-                    lows = []
-                    for side in range(2):
-                        lanes = slice(side * LANES, (side + 1) * LANES)
-                        delta = [
-                            place[axis][:, lanes] - spread[source, axis, part, :]
-                            for axis in range(3)
-                        ]
-                        high, low = split(cubes(*delta))
-                        highs.append(high)
-                        lows.append(low)
-                    total = total + bdot(
-                        two_terms(w_high[:, part], w_low[:, part]),
-                        jnp.concatenate(
-                            [jnp.concatenate(highs, axis=1), jnp.concatenate(lows, axis=1)],
-                            axis=0,
-                        ),
+    lax.fori_loop(0, size_x * size_y // 2, prepare, 0)
+    run_tasks(size_y, tasks, table_ref, pack_ref, out_ref, masks[2], spread, moments, False)
+
+
+def halo_kernel(size_x, size_y, axis, tasks, table_ref, before_ref, pack_ref, *rest):
+    parcels = rest[:2]
+    out_ref, spread, moments, held = rest[2:]
+    masks = near_masks()
+    out_ref[...] = before_ref[...]
+    ends = parcel_rows(size_x, size_y)[0 if axis == "gx" else 1]
+    cells = size_y if axis == "gx" else size_x + 2
+    for number, (side, parcel) in enumerate(zip(SIDES, parcels)):
+        row = ends[0]
+        inside = lies_inside(axis, side)
+        for c in range(6):
+            for half in range(2):
+                lanes = slice(half * LANES, (half + 1) * LANES)
+                if axis == "gx":
+                    value = parcel[row : row + cells]
+                    row += cells
+                else:
+                    value = parcel[pl.ds(ends[0] + c * 2 * cells + half, cells, stride=2), :]
+                held[c, number * cells : (number + 1) * cells, lanes] = (
+                    value if c < 3 else value * inside
+                )
+
+    def prepare(index, carry):
+        for k in range(2):
+            slot = index * 2 + k
+            row = [held[c, pl.ds(slot, 1), :] for c in range(6)]
+            prepare_column(row, slot, masks, spread, moments)
+        return carry
+
+    lax.fori_loop(0, cells, prepare, 0)
+    run_tasks(size_y, tasks, table_ref, pack_ref, out_ref, masks[2], spread, moments, True)
+
+
+def near_tables(size_x, size_y):
+    kinds = ({}, {}, {})
+    for i in range(size_x):
+        for j in range(size_y):
+            found = ([], [], [])
+            for x in (-1, 0, 1):
+                for y in (-1, 0, 1):
+                    if not 0 <= j + y < size_y:
+                        found[2].extend([int(y > 0) * (size_x + 2) + i + x + 1, x, y])
+                    elif not 0 <= i + x < size_x:
+                        found[1].extend([int(x > 0) * size_y + j + y, x, y])
+                    else:
+                        found[0].extend([(i + x) * size_y + j + y, x, y])
+            for groups, sources in zip(kinds, found):
+                if sources:
+                    groups.setdefault(len(sources) // 3, []).append([i, j] + sources)
+    result = []
+    for groups in kinds:
+        flat = []
+        tasks = []
+        for sources in sorted(groups, reverse=True):
+            tasks.append((len(flat), len(groups[sources]), sources))
+            for entry in groups[sources]:
+                flat += entry
+        result.append((np.array(flat, np.int32), tasks))
+    return result
+
+
+def leaf_kernel(size_x, size_y, own_ref, rows_ref, cols_ref, *rest):
+    parcels = rest[:4]
+    down_ref, base, leaf_ref = rest[4:]
+    for depth in range(2):
+        for c in range(3):
+            for x in range(size_x):
+                leaf_ref[depth, c, WIDTH + x, WIDTH : WIDTH + size_y] = own_ref[depth, c, x]
+    for side, parcel in zip(SIDES, parcels[:2]):
+        inside = lies_inside("gx", side)
+        start = landing(side, size_x, WIDTH)
+        row = 0
+        for depth in range(2):
+            for c in range(3):
+                for x in range(start, start + WIDTH):
+                    leaf_ref[depth, c, x, WIDTH : WIDTH + size_y] = (
+                        parcel[row : row + size_y] * inside
                     )
-        out_ref[index] = total[:16] + total[16:]
-        return carry
-
-    lax.fori_loop(0, size_x * size_y, target, 0)
-
-
-def leaf_kernel(size_x, size_y, leaf_ref, rows_ref, cols_ref, down_ref, base):
+                    row += size_y
+    for side, parcel in zip(SIDES, parcels[2:]):
+        inside = lies_inside("gy", side)
+        start = landing(side, size_y, WIDTH)
+        row = 0
+        for depth in range(2):
+            for c in range(3):
+                for x in range(size_x + 2 * WIDTH):
+                    leaf_ref[depth, c, x, start : start + WIDTH] = (
+                        parcel[row : row + WIDTH] * inside
+                    )
+                    row += WIDTH
     for axis in range(3):
         base[axis] = 0.9 * rows_ref[axis : axis + 1, :] - 0.9 * cols_ref[axis]
     down_ref[...] = jnp.zeros_like(down_ref)
@@ -281,7 +503,7 @@
     tops_x,
     tops_y,
     chunk,
-    scalar_ref,
+    slot_ref,
     counts_ref,
     down_ref,
     tops_ref,
@@ -308,13 +530,19 @@
         base[axis] = 1.8 * point[axis] - 1.8 * cols_ref[axis]
 
     windows[...] = jnp.zeros_like(windows)
-    mine = scalar_ref[2]
+    lanes_x = tops_x // half_x
     lanes_y = tops_y // half_y
+    mine_x = lax.axis_index("gx")
+    mine_y = lax.axis_index("gy")
 
     def place(device, carry):
-        slot = jnp.bitwise_xor(device, mine)
-        i = (device // lanes_y) * half_x
-        j = (device % lanes_y) * half_y
+        place_x = device // lanes_y
+        place_y = device % lanes_y
+        away_x = lax.rem(place_x - mine_x + lanes_x, lanes_x)
+        away_y = lax.rem(place_y - mine_y + lanes_y, lanes_y)
+        slot = slot_ref[away_x * lanes_y + away_y]
+        i = place_x * half_x
+        j = place_y * half_y
         for c in range(3):
             for p in range(half_x):
                 for q in range(half_y):
@@ -327,9 +555,9 @@
                         ] = row
         return carry
 
-    lax.fori_loop(0, tops_ref.shape[0], place, 0)
-    first_x = scalar_ref[0]
-    first_y = scalar_ref[1]
+    lax.fori_loop(0, lanes_x * lanes_y, place, 0)
+    first_x = mine_x * half_x
+    first_y = mine_y * half_y
     top_down[...] = jnp.zeros_like(top_down)
     parts = -(-along // chunk)
 
@@ -405,7 +633,7 @@
             total = bdot(two_terms(*split(weight)), jnp.concatenate([high, low], axis=0))
             total = total[:16] + total[16:] + near_ref[index, :, lanes]
             place[2] = place[2] + (half - 0.5)
-            living = jnp.where(lane < counts_ref[2 * index + half], 1.0, 0.0)
+            living = jnp.where(lane < counts_ref[i, j, half], 1.0, 0.0)
             square = (
                 place[0] * place[0] + place[1] * place[1] + place[2] * place[2] + SMOOTH2
             )
@@ -438,36 +666,41 @@
     lax.fori_loop(0, size_x * size_y // 4, columns, 0)
 
 
-def gathered(block):
-    held = block[None]
-    for axis in ("gy", "gx"):
-        count = lax.axis_size(axis)
-        bit = 1
-        while bit < count:
-            radix = 4 if bit * 4 <= count else 2
-            received = [
-                lax.ppermute(held, axis, [(i, i ^ (k * bit)) for i in range(count)])
-                for k in range(1, radix)
+def moved(array, axis, step):
+    count = lax.axis_size(axis)
+    return lax.ppermute(array, axis, [((i + step) % count, i) for i in range(count)])
+
+
+def widened(blocks, away, axis, name):
+    count = lax.axis_size(name)
+    half = 1
+    while 2 * half + 1 < count:
+        missing = count - 2 * half - 1
+        if missing <= 2 * half + 1:
+            first = -((missing - 1) // 2)
+            steps = (half + 1 - first,)
+        else:
+            first = -half
+            missing = 2 * half + 1
+            steps = (missing, -missing)
+        sent = []
+        known = []
+        for array, places in zip(blocks, away):
+            pick = [k for k, place in enumerate(places) if 0 <= place[axis] - first < missing]
+            known += [places[k] for k in pick]
+            if len(pick) == len(places):
+                sent.append(array)
+            else:
+                size = array.shape[0] // len(places)
+                sent += [array[k * size : (k + 1) * size] for k in pick]
+        whole = sent[0] if len(sent) == 1 else jnp.concatenate(sent, axis=0)
+        for step in steps:
+            blocks = blocks + [moved(whole, name, step)]
+            away = away + [
+                [tuple(p + step * (k == axis) for k, p in enumerate(place)) for place in known]
             ]
-            held = jnp.concatenate([held] + received, axis=0)
-            bit *= radix
-    return held
-
-
-def extended(cells, sides):
-    for axis, dim, width in sides:
-        count = lax.axis_size(axis)
-        head = lax.slice_in_dim(cells, 0, width, axis=dim)
-        tail = lax.slice_in_dim(cells, cells.shape[dim] - width, cells.shape[dim], axis=dim)
-        cells = jnp.concatenate(
-            [
-                lax.ppermute(tail, axis, [(i, i + 1) for i in range(count - 1)]),
-                cells,
-                lax.ppermute(head, axis, [(i + 1, i) for i in range(count - 1)]),
-            ],
-            axis=dim,
-        )
-    return cells
+        half = half + steps[0] if len(steps) == 2 else count
+    return blocks, away
 
 
 def body(offsets, strengths, counts, check_inverse):
@@ -490,59 +723,121 @@
         for k in range(5):
             patterns[half, 3 * k : 3 * k + 3, :] = factors[k]
     patterns = jnp.asarray(patterns)
-    pad = LANES - expansion
-    matrix = jnp.pad(check_inverse, ((0, pad), (0, pad)))
-    slot = jnp.arange(LANES)
-    living = (slot < counts[:, :, :, None]).astype(F32).reshape(1, size_x, size_y, depth * LANES)
-    pack = jnp.concatenate([offsets, STRENGTH_SCALE * strengths * living], axis=0)
 
     params = pltpu.CompilerParams(vmem_limit_bytes=58 * 2**20)
-    leaf_charges, top_charges = pl.pallas_call(
+    smem = pl.BlockSpec(memory_space=pltpu.SMEM)
+    vmem = pl.BlockSpec(memory_space=pltpu.VMEM)
+
+    def cost(flops):
+        return pl.CostEstimate(flops=flops, bytes_accessed=10**6, transcendentals=0)
+
+    top_rows = 3 * half_x * half_y
+    (_, _, end_x), (_, near_y, end_y) = parcel_rows(size_x, size_y)
+    made = pl.pallas_call(
         functools.partial(up_kernel, size_x, size_y),
         out_shape=(
+            jax.ShapeDtypeStruct((6, size_x, size_y, depth * LANES), F32),
             jax.ShapeDtypeStruct((2, 3, size_x, size_y, LANES), F32),
-            jax.ShapeDtypeStruct((3 * half_x * half_y, LANES), F32),
+            jax.ShapeDtypeStruct((top_rows, LANES), F32),
+            jax.ShapeDtypeStruct((LANES, LANES), F32),
+            *[jax.ShapeDtypeStruct((end_x, LANES), F32)] * 2,
         ),
+        in_specs=[smem] + [vmem] * 5,
+        out_specs=(vmem,) * 6,
         scratch_shapes=[pltpu.VMEM((2, 3, size_x, size_y, LANES), F32)],
         compiler_params=params,
-        cost_estimate=pl.CostEstimate(flops=10**9, bytes_accessed=10**6, transcendentals=0),
+        cost_estimate=cost(6 * 10**9),
         name="up",
-    )(pack, rows, cols, matrix)
-
-    neighbours = extended(pack, (("gx", 1, 1), ("gy", 2, 1)))
-    border = extended(leaf_charges, (("gx", 2, 3), ("gy", 3, 3)))
-    tops = gathered(top_charges)
-
-    near = pl.pallas_call(
-        functools.partial(near_kernel, size_x, size_y),
-        out_shape=jax.ShapeDtypeStruct((size_x * size_y, 16, 2 * LANES), F32),
+    )(counts, offsets, strengths, rows, cols, check_inverse)
+    pack, leaf_charges, top_charges, matrix, to_below, to_above = made
+    below = moved(to_above, "gx", -1)
+    above = moved(to_below, "gx", 1)
+
+    (own_table, own_tasks), *beside = near_tables(size_x, size_y)
+    near_shape = jax.ShapeDtypeStruct((size_x * size_y, 16, 2 * LANES), F32)
+    own = pl.pallas_call(
+        functools.partial(own_kernel, size_x, size_y, own_tasks),
+        out_shape=near_shape,
+        in_specs=[smem, vmem],
+        out_specs=vmem,
         scratch_shapes=[
-            pltpu.VMEM(((size_x + 2) * (size_y + 2), 3, 2 * LANES, LANES), F32),
-            pltpu.VMEM(((size_x + 2) * (size_y + 2), 4, 16, 2 * LANES), F32),
+            pltpu.VMEM((size_x * size_y, 4, 2 * LANES, LANES), F32),
+            pltpu.VMEM((size_x * size_y, 4, 16, 2 * LANES), F32),
         ],
         compiler_params=params,
-        cost_estimate=pl.CostEstimate(flops=4 * 10**10, bytes_accessed=10**6, transcendentals=0),
-        name="near",
-    )(neighbours)
+        cost_estimate=cost(3 * 10**10),
+        name="own",
+    )(jnp.asarray(own_table), pack)
+
+    to_low, to_high, tops = pl.pallas_call(
+        functools.partial(turn_kernel, size_x, size_y),
+        out_shape=(
+            jax.ShapeDtypeStruct((end_y, LANES), F32),
+            jax.ShapeDtypeStruct((end_y, LANES), F32),
+            jax.ShapeDtypeStruct((3 * top_rows, LANES), F32),
+        ),
+        in_specs=[vmem] * 5,
+        out_specs=(vmem,) * 3,
+        compiler_params=params,
+        cost_estimate=cost(10**9),
+        name="turn",
+    )(leaf_charges, pack, top_charges, below, above)
+    low = moved(to_high, "gy", -1)
+    high = moved(to_low, "gy", 1)
+    blocks, away = widened(
+        [low[near_y:], tops, high[near_y:]],
+        [[(x, y) for x in (-1, 0, 1)] for y in (-1, 0, 1)],
+        1,
+        "gy",
+    )
+
+    def beside_near(axis, before, parcels):
+        table, tasks = beside[0 if axis == "gx" else 1]
+        columns = 2 * (size_y if axis == "gx" else size_x + 2)
+        return pl.pallas_call(
+            functools.partial(halo_kernel, size_x, size_y, axis, tasks),
+            out_shape=near_shape,
+            in_specs=[smem] + [vmem] * 4,
+            out_specs=vmem,
+            scratch_shapes=[
+                pltpu.VMEM((columns, 4, 2 * LANES, LANES), F32),
+                pltpu.VMEM((columns, 4, 16, 2 * LANES), F32),
+                pltpu.VMEM((6, columns, 2 * LANES), F32),
+            ],
+            compiler_params=params,
+            cost_estimate=cost(10**10),
+            name="beside_" + axis,
+        )(jnp.asarray(table), before, pack, *parcels)
+
+    near = beside_near("gx", own, (below, above))
+    blocks, away = widened(blocks, away, 0, "gx")
+    away = [place for places in away for place in places]
+    blocks = jnp.concatenate(blocks, axis=0).reshape(len(away), top_rows, LANES)
+    slots = np.zeros((lanes_x, lanes_y), np.int32)
+    for slot, (x, y) in reversed(list(enumerate(away))):
+        slots[x % lanes_x, y % lanes_y] = slot
+    near = beside_near("gy", near, (low, high))
 
     down = pl.pallas_call(
         functools.partial(leaf_kernel, size_x, size_y),
         out_shape=jax.ShapeDtypeStruct((3 * size_x * size_y, 2 * LANES), F32),
-        scratch_shapes=[pltpu.VMEM((3, LANES, LANES), F32)],
+        in_specs=[vmem] * 7,
+        out_specs=vmem,
+        scratch_shapes=[
+            pltpu.VMEM((3, LANES, LANES), F32),
+            pltpu.VMEM(
+                (2, 3, size_x + 2 * WIDTH, size_y + 2 * WIDTH, LANES), F32
+            ),
+        ],
         compiler_params=params,
-        cost_estimate=pl.CostEstimate(flops=6 * 10**9, bytes_accessed=10**6, transcendentals=0),
+        cost_estimate=cost(6 * 10**9),
         name="leaf",
-    )(border, rows, cols)
-
-    gx = lax.axis_index("gx")
-    gy = lax.axis_index("gy")
-    scalars = jnp.stack([gx * half_x, gy * half_y, gx * lanes_y + gy]).astype(jnp.int32)
+    )(leaf_charges, rows, cols, below, above, low, high)
+
     across = tops_x + half_x - 1
     along = tops_y + half_y - 1
     parts = -(-along // 20)
     chunk = -(-along // parts)
-    smem = pl.BlockSpec(memory_space=pltpu.SMEM)
-    vmem = pl.BlockSpec(memory_space=pltpu.VMEM)
     return pl.pallas_call(
         functools.partial(far_kernel, size_x, size_y, tops_x, tops_y, chunk),
         out_shape=jax.ShapeDtypeStruct((12, size_x, size_y, depth * LANES), F32),
@@ -556,9 +851,20 @@
             pltpu.VMEM((2, 3, size_x, size_y, LANES), F32),
         ],
         compiler_params=params,
-        cost_estimate=pl.CostEstimate(flops=10**10, bytes_accessed=10**6, transcendentals=0),
+        cost_estimate=cost(10**10),
         name="far",
-    )(scalars, counts.reshape(-1), down, tops, near, pack, rows, cols, patterns, matrix)
+    )(
+        jnp.asarray(slots.reshape(-1)),
+        counts,
+        down,
+        blocks,
+        near,
+        pack,
+        rows,
+        cols,
+        patterns,
+        matrix,
+    )
 
 
 def solution(mesh):

time: 122 us -> 101 us (0.83)
  starting transfers between devices: 33.4 us -> 12.3 us
  Pallas kernels: 78.4 us -> 84.5 us
  other arithmetic: 4.86 us -> 0.01 us
    ppermute x15 -> x7, starting transfers between devices: 33.4 us -> 12.3 us  [moved(): lax.ppermute(array, axis, [((i + step) % count, i) for i in range(count)])]
    pallas_call x1 -> x4, Pallas kernels: 52.4 us -> 57.9 us  [the longest x1 37.4 us: body(): pl.pallas_call(functools.partial(own_kernel, size_x, size_y, own_tasks),...]
    concatenate x5 -> x1, other arithmetic: 2.56 us -> 0.01 us  [widened(): whole = sent[0] if len(sent) == 1 else jnp.concatenate(sent, axis=0)]
    unnamed x21 -> x16, local copies, waits for them, and re-layouts: 1.94 us -> 4.17 us
    mul x2 -> x0, other arithmetic: 1.7 us -> none  [body(): STRENGTH_SCALE * strengths * living]
  transfers between devices with their start and end apart: 15 -> 7, of which waited for: 0 -> 0; matrix products, arithmetic and copies ran while one was open for 4% -> 0% of each run, Pallas kernels for 47% -> 60%
where the time goes in v3:
time: 101 us
  Pallas kernels  84.5 us (84%)
  starting transfers between devices  12.3 us (12%)
  local copies, waits for them, and re-layouts  4.2 us (4%)
    pallas_call x1, Pallas kernels, body(): pl.pallas_call(functools.partial(own_kernel, size_x, size_y, own_tasks),...  37.4 us
    pallas_call x2, Pallas kernels, beside_near(): pl.pallas_call(functools.partial(halo_kernel, size_x, size_y, axis, tasks...  18.5 us
    pallas_call x1, Pallas kernels, body(): pl.pallas_call(functools.partial(far_kernel, size_x, size_y, tops_x, tops...  15.4 us
    ppermute x7, starting transfers between devices, moved(): lax.ppermute(array, axis, [((i + step) % count, i) for i in range(count)])  12.3 us
    pallas_call x1, Pallas kernels, body(): pl.pallas_call(functools.partial(up_kernel, size_x, size_y), out_shape=(j...  6.4 us
    pallas_call x1, Pallas kernels, body(): pl.pallas_call(functools.partial(leaf_kernel, size_x, size_y), out_shape=...  4.87 us
    unnamed x16, local copies, waits for them, and re-layouts  4.17 us
  transfers between devices with their start and end apart: 7, of which 0 were waited for; matrix products, arithmetic and copies ran while one was open for 0% of the time, Pallas kernels for 60%

profile of v3, /device:TPU:0, one launch (start us, length us, event | category | flops | bytes accessed | tf_op | source)
XLA Modules:
  0.0 101.1 jit_solution(13770147228013977554)
XLA Ops:
  0.0 1.4 %copy.13.counts_ref = s32[4,8,2]{2,1,0:T(8,128)} copy(s32[4,8,2]{1,2,0:T(2,128)} %param.13) | data formatting | bytes 512 | tf_op args[2]
  1.4 6.4 %up.1 = (f32[6,4,8,256]{3,2,1,0:T(8,128)}, f32[2,3,4,8,128]{4,3,2,1,0:T(8,128)}, f32[24,128]{1,0:T(8,128)}, f32[128,128]{1,0:T(8,128)}, f32[264,128]{1,0:T(8,128)}, /*index=5*/f32[264,128]{1,0:T(8,128)}) custom-call(s32[4,8,2]{2,1,0:T(8,128)} %copy.13.counts_ref, f32[3,4,8,256]{3,2,1,0:T(8,128)} %offsets_ref.1, f32[3,4,8,256]{3,2,1,0:T(8,128)} %strengths_ref.1, ...), custom_call_target="tpu_custom_call" | custom-call | flops 6000000000 | bytes 1000000 | tf_op jit(solution)/shard_map/up/pallas_call | solution.py:736
  7.8 0.5 collective-permute-start
  8.2 2.9 %collective-permute-start.1 = (f32[264,128]{1,0:T(8,128)}, f32[264,128]{1,0:T(8,128)S(1)}, u32[]{:S(2)}, u32[]{:S(2)}) collective-permute-start(f32[264,128]{1,0:T(8,128)} %get-tuple-element.16), channel_id=1, source_target_pairs={{4,0},{8,4},{12,8},{16,12},{20,16},{24,20},{28,24},{0,28},{5,1},{9... | collective-permute-start | bytes 405512 | tf_op jit(solution)/shard_map/ppermute | solution.py:671
  11.1 37.4 %own.1.before_ref = f32[32,16,256]{2,1,0:T(8,128)} custom-call(s32[724]{0:T(1024)} %constant.17.clone.table_ref, f32[6,4,8,256]{3,2,1,0:T(8,128)} %get-tuple-element.17.pack_ref), custom_call_target="tpu_custom_call" | custom-call | flops 30000001024 | bytes 1000000 | tf_op jit(solution)/shard_map/own/pallas_call | solution.py:758
  48.6 0.0 collective-permute-done.below_ref.rest_0_
  48.6 0.7 copy-done.4
  49.3 0.0 copy-done.5
  49.3 1.9 %turn.1 = (f32[324,128]{1,0:T(8,128)}, f32[324,128]{1,0:T(8,128)}, f32[72,128]{1,0:T(8,128)}) custom-call(f32[2,3,4,8,128]{4,3,2,1,0:T(8,128)} %get-tuple-element.14.leaf_ref.own_ref, f32[6,4,8,256]{3,2,1,0:T(8,128)} %get-tuple-element.17.pack_ref, f32[24,128]{1,0:T(8,128)} %get-tuple-element.18.top_ref, f32[264,128]{1,0:T(8,128)} %copy-done.4, ...), custom_call_target="tpu_custom_call" | custom-call | flops 1000000000 | bytes 1000000 | tf_op jit(solution)/shard_map/turn/pallas_call | solution.py:772
  51.2 3.3 %collective-permute-start.4 = (f32[72,128]{1,0:T(8,128)}, f32[72,128]{1,0:T(8,128)S(1)}, u32[]{:S(2)}, u32[]{:S(2)}) collective-permute-start(f32[72,128]{1,0:T(8,128)} %get-tuple-element.21), channel_id=1, source_target_pairs={{2,0},{3,1},{0,2},{1,3},{6,4},{7,5},{4,6},{5,7},{10,8},{11,9},{8,1... | collective-permute-start | bytes 110600 | tf_op jit(solution)/shard_map/ppermute | solution.py:671
  54.5 1.6 %collective-permute-start.2 = (f32[324,128]{1,0:T(8,128)}, f32[324,128]{1,0:T(8,128)S(1)}, u32[]{:S(2)}, u32[]{:S(2)}) collective-permute-start(f32[324,128]{1,0:T(8,128)} %get-tuple-element.19), channel_id=1, source_target_pairs={{3,0},{0,1},{1,2},{2,3},{7,4},{4,5},{5,6},{6,7},{11,8},{8,9},{9,10... | collective-permute-start | bytes 497672 | tf_op jit(solution)/shard_map/ppermute | solution.py:671
  56.1 2.2 %collective-permute-start.3 = (f32[324,128]{1,0:T(8,128)}, f32[324,128]{1,0:T(8,128)S(1)}, u32[]{:S(2)}, u32[]{:S(2)}) collective-permute-start(f32[324,128]{1,0:T(8,128)} %get-tuple-element.20), channel_id=1, source_target_pairs={{1,0},{2,1},{3,2},{0,3},{5,4},{6,5},{7,6},{4,7},{9,8},{10,9},{11,1... | collective-permute-start | bytes 497672 | tf_op jit(solution)/shard_map/ppermute | solution.py:671
  58.3 11.0 %beside_gx.1.before_ref = f32[32,16,256]{2,1,0:T(8,128)} custom-call(s32[164]{0:T(256)} %constant.18.clone.table_ref, f32[32,16,256]{2,1,0:T(8,128)} %own.1.before_ref, f32[6,4,8,256]{3,2,1,0:T(8,128)} %get-tuple-element.17.pack_ref, f32[264,128]{1,0:T(8,128)} %copy-done.4, f32[264,128]{1,0:T(8,128)} %copy-done.5), custom_call_target="tpu_custom_call" | custom-call | flops 10000000000 | bytes 1000000 | tf_op jit(solution)/shard_map/beside_gx/pallas_call | solution.py:797
  69.3 0.0 collective-permute-done.2.rest_2_.rest_0_
  69.3 0.7 copy-done
  70.1 0.0 collective-permute-done.3.rest_3_.rest_1_
  70.2 0.6 copy-done.2
  70.8 0.0 collective-permute-start.6
  70.8 1.7 %collective-permute-start.5 = (f32[288,128]{1,0:T(8,128)S(1)}, f32[288,128]{1,0:T(8,128)S(1)}, u32[]{:S(2)}, u32[]{:S(2)}) collective-permute-start(f32[288,128]{1,0:T(8,128)S(1)} %pad_maximum_fusion), channel_id=1, source_target_pairs={{12,0},{16,4},{20,8},{24,12},{28,16},{0,20},{4,24},{8,28},{13,1},{... | collective-permute-start | bytes 442376 | tf_op jit(solution)/shard_map/ppermute | solution.py:671
  72.5 7.5 %beside_gy.1.near_ref = f32[32,16,256]{2,1,0:T(8,128)} custom-call(s32[88]{0:T(128)} %constant.19.clone.table_ref, f32[32,16,256]{2,1,0:T(8,128)} %beside_gx.1.before_ref, f32[6,4,8,256]{3,2,1,0:T(8,128)} %get-tuple-element.17.pack_ref, f32[324,128]{1,0:T(8,128)} %copy-done.1, f32[324,128]{1,0:T(8,128)} %copy-done.2), custom_call_target="tpu_custom_call" | custom-call | flops 10000000000 | bytes 1000000 | tf_op jit(solution)/shard_map/beside_gy/pallas_call | solution.py:797
  80.0 4.9 %leaf.1.down_ref = f32[96,256]{1,0:T(8,128)} custom-call(f32[2,3,4,8,128]{4,3,2,1,0:T(8,128)} %get-tuple-element.14.leaf_ref.own_ref, f32[8,128]{1,0:T(8,128)} %constant.14.clone.rows_ref, f32[3,128,128]{2,1,0:T(8,128)} %constant.15.clone.cols_ref, f32[264,128]{1,0:T(8,128)} %copy-done.4, f32[264,128]{1,0:T(8,128)} %copy-done.5, f32[324,128]{1,0:T(8,128)} %copy-done.1, ...), custom_call_target="tpu_custom_call" | custom-call | flops 6000000000 | bytes 1000000 | tf_op jit(solution)/shard_map/leaf/pallas_call | solution.py:821
  84.9 0.0 collective-permute-done.5
  85.0 0.7 copy-done.3
  85.7 15.4 %far.1 = f32[12,4,8,256]{3,2,1,0:T(8,128)} custom-call(s32[32]{0:T(128)} %constant.20.clone.slot_ref, s32[4,8,2]{2,1,0:T(8,128)} %copy.13.counts_ref, f32[96,256]{1,0:T(8,128)} %leaf.1.down_ref, f32[36,24,128]{2,1,0:T(8,128)} %bitcast.1, f32[32,16,256]{2,1,0:T(8,128)} %beside_gy.1.near_ref, f32[6,4,8,256]{3,2,1,0:T(8,128)} %get-tuple-element.17.pack_ref, ...), custom_call_target="tpu_custom_call" | custom-call | flops 10000000000 | bytes 1000000 | tf_op jit(solution)/shard_map/far/pallas_call | solution.py:841
  (17 shorter events, 0.1 us)
Async XLA Ops:
  7.8 40.8 %collective-permute-start = (f32[264,128]{1,0:T(8,128)}, f32[264,128]{1,0:T(8,128)S(1)}, u32[]{:S(2)}, u32[]{:S(2)}) collective-permute-start(f32[264,128]{1,0:T(8,128)} %get-tuple-element.15), channel_id=1, source_target_pairs={{28,0},{0,4},{4,8},{8,12},{12,16},{16,20},{20,24},{24,28},{29,1},{... | collective-permute-start | bytes 405512 | tf_op jit(solution)/shard_map/ppermute | solution.py:671
  8.2 40.4 %collective-permute-start.1 = (f32[264,128]{1,0:T(8,128)}, f32[264,128]{1,0:T(8,128)S(1)}, u32[]{:S(2)}, u32[]{:S(2)}) collective-permute-start(f32[264,128]{1,0:T(8,128)} %get-tuple-element.16), channel_id=1, source_target_pairs={{4,0},{8,4},{12,8},{16,12},{20,16},{24,20},{28,24},{0,28},{5,1},{9... | collective-permute-start | bytes 405512 | tf_op jit(solution)/shard_map/ppermute | solution.py:671
  48.6 0.7 copy-start.4
  48.6 0.7 copy-start.5
  51.2 18.9 %collective-permute-start.4 = (f32[72,128]{1,0:T(8,128)}, f32[72,128]{1,0:T(8,128)S(1)}, u32[]{:S(2)}, u32[]{:S(2)}) collective-permute-start(f32[72,128]{1,0:T(8,128)} %get-tuple-element.21), channel_id=1, source_target_pairs={{2,0},{3,1},{0,2},{1,3},{6,4},{7,5},{4,6},{5,7},{10,8},{11,9},{8,1... | collective-permute-start | bytes 110600 | tf_op jit(solution)/shard_map/ppermute | solution.py:671
  54.5 14.8 %collective-permute-start.2 = (f32[324,128]{1,0:T(8,128)}, f32[324,128]{1,0:T(8,128)S(1)}, u32[]{:S(2)}, u32[]{:S(2)}) collective-permute-start(f32[324,128]{1,0:T(8,128)} %get-tuple-element.19), channel_id=1, source_target_pairs={{3,0},{0,1},{1,2},{2,3},{7,4},{4,5},{5,6},{6,7},{11,8},{8,9},{9,10... | collective-permute-start | bytes 497672 | tf_op jit(solution)/shard_map/ppermute | solution.py:671
  56.1 14.0 %collective-permute-start.3 = (f32[324,128]{1,0:T(8,128)}, f32[324,128]{1,0:T(8,128)S(1)}, u32[]{:S(2)}, u32[]{:S(2)}) collective-permute-start(f32[324,128]{1,0:T(8,128)} %get-tuple-element.20), channel_id=1, source_target_pairs={{1,0},{2,1},{3,2},{0,3},{5,4},{6,5},{7,6},{4,7},{9,8},{10,9},{11,1... | collective-permute-start | bytes 497672 | tf_op jit(solution)/shard_map/ppermute | solution.py:671
  69.3 0.8 copy-start
  69.3 0.8 copy-start.1
  70.1 0.7 copy-start.2
  70.8 14.2 %collective-permute-start.6 = (f32[288,128]{1,0:T(8,128)S(1)}, f32[288,128]{1,0:T(8,128)S(1)}, u32[]{:S(2)}, u32[]{:S(2)}) collective-permute-start(f32[288,128]{1,0:T(8,128)S(1)} %pad_maximum_fusion), channel_id=1, source_target_pairs={{20,0},{24,4},{28,8},{0,12},{4,16},{8,20},{12,24},{16,28},{21,1},{... | collective-permute-start | bytes 442376 | tf_op jit(solution)/shard_map/ppermute | solution.py:671
  70.8 14.2 %collective-permute-start.5 = (f32[288,128]{1,0:T(8,128)S(1)}, f32[288,128]{1,0:T(8,128)S(1)}, u32[]{:S(2)}, u32[]{:S(2)}) collective-permute-start(f32[288,128]{1,0:T(8,128)S(1)} %pad_maximum_fusion), channel_id=1, source_target_pairs={{12,0},{16,4},{20,8},{24,12},{28,16},{0,20},{4,24},{8,28},{13,1},{... | collective-permute-start | bytes 442376 | tf_op jit(solution)/shard_map/ppermute | solution.py:671
  85.0 0.8 copy-start.3

commit v4 on v3

--- a/solution.py
+++ b/solution.py
@@ -109,7 +109,8 @@
 
     def one_column(i, j):
         row = [offsets_ref[c, i, pl.ds(j, 1), :] for c in range(3)]
-        last = jnp.where(lane < LANES, counts_ref[i, j, 0], counts_ref[i, j, 1] + LANES)
+        at = (i * size_y + j) * 2
+        last = jnp.where(lane < LANES, counts_ref[at], counts_ref[at + 1] + LANES)
         charges = []
         for c in range(3):
             value = jnp.where(
@@ -244,10 +245,20 @@
     level, kind, lift = masks
     x, y, z = row[0], row[1], row[2] + lift
     square = x * x + y * y + z * z
-    for axis, value in enumerate((-2.0 * x, -2.0 * y, -2.0 * z, square)):
-        for half in range(2):
-            lanes = slice(half * LANES, (half + 1) * LANES)
-            spread[slot, axis, lanes, :] = jnp.broadcast_to(value[:, lanes], (LANES, LANES)).T
+    values = jnp.concatenate(
+        [-2.0 * x, -2.0 * y, -2.0 * z, square, jnp.zeros((4, 2 * LANES), F32)], axis=0
+    )
+    first = values.astype(BF16).astype(F32)
+    second = (values - first).astype(BF16).astype(F32)
+    terms = jnp.concatenate(
+        [first, second, (values - first) - second, jnp.zeros_like(values)], axis=0
+    ).T.astype(BF16)
+    term = lax.broadcasted_iota(jnp.int32, (32, 4 * LANES), 0)
+    place = lax.broadcasted_iota(jnp.int32, (32, 4 * LANES), 1) // LANES
+    chosen = jnp.where((term % 8 == place) & (term < 24), 1.0, 0.0).astype(BF16)
+    laid = bdot(terms, chosen)
+    for axis in range(4):
+        spread[slot, axis] = laid[:, axis * LANES : (axis + 1) * LANES]
 
     def wide(value):
         return jnp.broadcast_to(value, (16, 2 * LANES))
@@ -266,41 +277,49 @@
     moments[slot, 3] = last
 
 
+def shifted(moments, slot, shift_x, shift_y):
+    return (
+        moments[slot, 0]
+        + shift_x * moments[slot, 1]
+        + shift_y * moments[slot, 2]
+        + (shift_x * shift_x + shift_y * shift_y) * moments[slot, 3]
+    )
+
+
+def pair_cubes(target, slot, shift_x, shift_y, spread):
+    x = target[0] - shift_x
+    y = target[1] - shift_y
+    z = target[2]
+    square = x * x + y * y + z * z + SMOOTH2
+    result = []
+    for half in range(2):
+        part = slice(half * LANES, (half + 1) * LANES)
+        highs = []
+        lows = []
+        for side in range(2):
+            lanes = slice(side * LANES, (side + 1) * LANES)
+            distance = (
+                (square[:, lanes] + spread[slot, 3, part, :])
+                + x[:, lanes] * spread[slot, 0, part, :]
+                + y[:, lanes] * spread[slot, 1, part, :]
+                + z[:, lanes] * spread[slot, 2, part, :]
+            )
+            inverse = lax.rsqrt(distance)
+            high, low = split(inverse * inverse * inverse)
+            highs.append(high)
+            lows.append(low)
+        result.append((jnp.concatenate(highs, axis=1), jnp.concatenate(lows, axis=1)))
+    return result
+
+
 def near_sums(target, blocks, spread, moments):
     total = jnp.zeros((32, 2 * LANES), F32)
     for slot, shift_x, shift_y in blocks:
-        weight = (
-            moments[slot, 0]
-            + shift_x * moments[slot, 1]
-            + shift_y * moments[slot, 2]
-            + (shift_x * shift_x + shift_y * shift_y) * moments[slot, 3]
-        )
-        w_high, w_low = split(weight)
-        x = target[0] - shift_x
-        y = target[1] - shift_y
-        z = target[2]
-        square = x * x + y * y + z * z + SMOOTH2
-        for half in range(2):
+        w_high, w_low = split(shifted(moments, slot, shift_x, shift_y))
+        for half, terms in enumerate(pair_cubes(target, slot, shift_x, shift_y, spread)):
             part = slice(half * LANES, (half + 1) * LANES)
-            highs = []
-            lows = []
-            for side in range(2):
-                lanes = slice(side * LANES, (side + 1) * LANES)
-                distance = (
-                    (square[:, lanes] + spread[slot, 3, part, :])
-                    + x[:, lanes] * spread[slot, 0, part, :]
-                    + y[:, lanes] * spread[slot, 1, part, :]
-                    + z[:, lanes] * spread[slot, 2, part, :]
-                )
-                inverse = lax.rsqrt(distance)
-                high, low = split(inverse * inverse * inverse)
-                highs.append(high)
-                lows.append(low)
             total = total + bdot(
-                two_terms(w_high[:, part], w_low[:, part]),
-                jnp.concatenate(
-                    [jnp.concatenate(highs, axis=1), jnp.concatenate(lows, axis=1)], axis=0
-                ),
+                two_terms(w_high[:, part], w_low[:, part]), jnp.concatenate(terms, axis=0)
             )
     return total[:16] + total[16:]
 
@@ -308,7 +327,7 @@
 def run_tasks(size_y, tasks, table_ref, pack_ref, out_ref, lift, spread, moments, adds):
     for start, amount, sources in tasks:
         together = 1
-        while together * sources < 6 and amount % (2 * together) == 0:
+        while together * sources < 12 and amount % (2 * together) == 0:
             together *= 2
 
         def one(index, start, sources):
@@ -340,14 +359,62 @@
     masks = near_masks()
 
     def prepare(index, carry):
-        for k in range(2):
-            slot = index * 2 + k
+        for k in range(4):
+            slot = index * 4 + k
             row = [pack_ref[c, slot // size_y, pl.ds(slot % size_y, 1), :] for c in range(6)]
             prepare_column(row, slot, masks, spread, moments)
         return carry
 
-    lax.fori_loop(0, size_x * size_y // 2, prepare, 0)
-    run_tasks(size_y, tasks, table_ref, pack_ref, out_ref, masks[2], spread, moments, False)
+    lax.fori_loop(0, size_x * size_y // 4, prepare, 0)
+    out_ref[...] = jnp.zeros_like(out_ref)
+
+    def places(i, j):
+        row = [pack_ref[c, i, pl.ds(j, 1), :] for c in range(3)]
+        return [row[0], row[1], row[2] + masks[2]]
+
+    def one(at, others):
+        i = table_ref[at]
+        j = table_ref[at + 1]
+        slot = i * size_y + j
+        total = near_sums(places(i, j), [(slot, 0.0, 0.0)], spread, moments)
+        found = []
+        for k in range(others):
+            i, j, away_x, away_y = [table_ref[at + 2 + 4 * k + m] for m in range(4)]
+            away_x = away_x.astype(F32)
+            away_y = away_y.astype(F32)
+            other = i * size_y + j
+            (h_first, l_first), (h_second, l_second) = pair_cubes(
+                places(i, j), slot, -away_x, -away_y, spread
+            )
+            high = jnp.concatenate([h_first, h_second], axis=0)
+            low = jnp.concatenate([l_first, l_second], axis=0)
+            there = bdot(
+                two_terms(*split(shifted(moments, slot, -away_x, -away_y))),
+                jnp.concatenate([high, low], axis=0),
+            )
+            found.append((other, there[:16] + there[16:]))
+            here = lax.dot_general(
+                two_terms(*split(shifted(moments, other, away_x, away_y))),
+                jnp.concatenate([high, low], axis=1),
+                (((1,), (1,)), ((), ())),
+                preferred_element_type=F32,
+            )
+            total = total + here[:16] + here[16:]
+        found.append((slot, total))
+        return found
+
+    for start, amount, others in tasks:
+        together = 3 if amount % 3 == 0 else 1
+
+        def step(index, carry, start=start, others=others, together=together):
+            found = []
+            for k in range(together):
+                found += one(start + (index * together + k) * (2 + 4 * others), others)
+            for place, total in found:
+                out_ref[place] += total
+            return carry
+
+        lax.fori_loop(0, amount // together, step, 0)
 
 
 def halo_kernel(size_x, size_y, axis, tasks, table_ref, before_ref, pack_ref, *rest):
@@ -373,13 +440,13 @@
                 )
 
     def prepare(index, carry):
-        for k in range(2):
-            slot = index * 2 + k
+        for k in range(4):
+            slot = index * 4 + k
             row = [held[c, pl.ds(slot, 1), :] for c in range(6)]
             prepare_column(row, slot, masks, spread, moments)
         return carry
 
-    lax.fori_loop(0, cells, prepare, 0)
+    lax.fori_loop(0, 2 * cells // 4, prepare, 0)
     run_tasks(size_y, tasks, table_ref, pack_ref, out_ref, masks[2], spread, moments, True)
 
 
@@ -387,6 +454,11 @@
     kinds = ({}, {}, {})
     for i in range(size_x):
         for j in range(size_y):
+            pairs = []
+            for x, y in ((0, 1), (1, -1), (1, 0), (1, 1)):
+                if i + x < size_x and 0 <= j + y < size_y:
+                    pairs += [i + x, j + y, x, y]
+            kinds[0].setdefault(len(pairs) // 4, []).append([i, j] + pairs)
             found = ([], [], [])
             for x in (-1, 0, 1):
                 for y in (-1, 0, 1):
@@ -394,9 +466,7 @@
                         found[2].extend([int(y > 0) * (size_x + 2) + i + x + 1, x, y])
                     elif not 0 <= i + x < size_x:
                         found[1].extend([int(x > 0) * size_y + j + y, x, y])
-                    else:
-                        found[0].extend([(i + x) * size_y + j + y, x, y])
-            for groups, sources in zip(kinds, found):
+            for groups, sources in zip(kinds[1:], found[1:]):
                 if sources:
                     groups.setdefault(len(sources) // 3, []).append([i, j] + sources)
     result = []
@@ -633,7 +703,7 @@
             total = bdot(two_terms(*split(weight)), jnp.concatenate([high, low], axis=0))
             total = total[:16] + total[16:] + near_ref[index, :, lanes]
             place[2] = place[2] + (half - 0.5)
-            living = jnp.where(lane < counts_ref[i, j, half], 1.0, 0.0)
+            living = jnp.where(lane < counts_ref[2 * index + half], 1.0, 0.0)
             square = (
                 place[0] * place[0] + place[1] * place[1] + place[2] * place[2] + SMOOTH2
             )
@@ -748,7 +818,7 @@
         compiler_params=params,
         cost_estimate=cost(6 * 10**9),
         name="up",
-    )(counts, offsets, strengths, rows, cols, check_inverse)
+    )(counts.reshape(-1), offsets, strengths, rows, cols, check_inverse)
     pack, leaf_charges, top_charges, matrix, to_below, to_above = made
     below = moved(to_above, "gx", -1)
     above = moved(to_below, "gx", 1)
@@ -855,7 +925,7 @@
         name="far",
     )(
         jnp.asarray(slots.reshape(-1)),
-        counts,
+        counts.reshape(-1),
         down,
         blocks,
         near,

time: 101 us -> 87.5 us (0.87)
  Pallas kernels: 84.5 us -> 70.4 us
    pallas_call x1, Pallas kernels: 37.4 us -> 25.3 us  [body(): pl.pallas_call(functools.partial(own_kernel, size_x, size_y, own_tasks),...]
    pallas_call x2, Pallas kernels: 18.5 us -> 16.5 us  [beside_near(): pl.pallas_call(functools.partial(halo_kernel, size_x, size_y, axis, tasks...]
  transfers between devices with their start and end apart: 7 -> 7, of which waited for: 0 -> 0; matrix products, arithmetic and copies ran while one was open for 0% -> 0% of each run, Pallas kernels for 60% -> 54%
where the time goes in v4:
time: 87.5 us; the launch traced here: 87.1 us
  Pallas kernels  70.4 us (80%)
  starting transfers between devices  12.3 us (14%)
  local copies, waits for them, and re-layouts  4.28 us (5%)
    pallas_call x1, Pallas kernels, body(): pl.pallas_call(functools.partial(own_kernel, size_x, size_y, own_tasks),...  25.3 us
    pallas_call x2, Pallas kernels, beside_near(): pl.pallas_call(functools.partial(halo_kernel, size_x, size_y, axis, tasks...  16.5 us
    pallas_call x1, Pallas kernels, body(): pl.pallas_call(functools.partial(far_kernel, size_x, size_y, tops_x, tops...  15.4 us
    ppermute x7, starting transfers between devices, moved(): lax.ppermute(array, axis, [((i + step) % count, i) for i in range(count)])  12.3 us
    pallas_call x1, Pallas kernels, body(): pl.pallas_call(functools.partial(up_kernel, size_x, size_y), out_shape=(j...  6.39 us
    pallas_call x1, Pallas kernels, body(): pl.pallas_call(functools.partial(leaf_kernel, size_x, size_y), out_shape=...  4.88 us
    unnamed x16, local copies, waits for them, and re-layouts  3.57 us
    pallas_call x1, Pallas kernels, body(): pl.pallas_call(functools.partial(turn_kernel, size_x, size_y), out_shape=...  1.92 us
  transfers between devices with their start and end apart: 7, of which 0 were waited for; matrix products, arithmetic and copies ran while one was open for 0% of the time, Pallas kernels for 54%

profile of v4, /device:TPU:0, one launch (start us, length us, event | category | flops | bytes accessed | tf_op | source)
XLA Modules:
  0.0 87.1 jit_solution(4127652526678431003)
XLA Ops:
  0.0 0.8 copy.13
  0.8 0.7 reshape.7.counts_ref
  1.5 6.4 %up.1 = (f32[6,4,8,256]{3,2,1,0:T(8,128)}, f32[2,3,4,8,128]{4,3,2,1,0:T(8,128)}, f32[24,128]{1,0:T(8,128)}, f32[128,128]{1,0:T(8,128)}, f32[264,128]{1,0:T(8,128)}, /*index=5*/f32[264,128]{1,0:T(8,128)}) custom-call(s32[64]{0:T(128)} %reshape.7.counts_ref, f32[3,4,8,256]{3,2,1,0:T(8,128)} %offsets_ref.1, f32[3,4,8,256]{3,2,1,0:T(8,128)} %strengths_ref.1, ...), custom_call_target="tpu_custom_call" | custom-call | flops 6000000000 | bytes 1000000 | tf_op jit(solution)/shard_map/up/pallas_call | solution.py:806
  7.8 0.5 collective-permute-start
  8.3 2.9 %collective-permute-start.1 = (f32[264,128]{1,0:T(8,128)}, f32[264,128]{1,0:T(8,128)S(1)}, u32[]{:S(2)}, u32[]{:S(2)}) collective-permute-start(f32[264,128]{1,0:T(8,128)} %get-tuple-element.16), channel_id=1, source_target_pairs={{4,0},{8,4},{12,8},{16,12},{20,16},{24,20},{28,24},{0,28},{5,1},{9... | collective-permute-start | bytes 405512 | tf_op jit(solution)/shard_map/ppermute | solution.py:741
  11.2 25.3 %own.1.before_ref = f32[32,16,256]{2,1,0:T(8,128)} custom-call(s32[440]{0:T(512)} %constant.17.clone.table_ref, f32[6,4,8,256]{3,2,1,0:T(8,128)} %get-tuple-element.17.pack_ref), custom_call_target="tpu_custom_call" | custom-call | flops 30000001024 | bytes 1000000 | tf_op jit(solution)/shard_map/own/pallas_call | solution.py:828
  36.5 0.0 collective-permute-done.1.above_ref.rest_1_
  36.5 0.7 copy-done.4
  37.2 0.0 copy-done.5
  37.2 1.9 %turn.1 = (f32[324,128]{1,0:T(8,128)}, f32[324,128]{1,0:T(8,128)}, f32[72,128]{1,0:T(8,128)}) custom-call(f32[2,3,4,8,128]{4,3,2,1,0:T(8,128)} %get-tuple-element.14.leaf_ref.own_ref, f32[6,4,8,256]{3,2,1,0:T(8,128)} %get-tuple-element.17.pack_ref, f32[24,128]{1,0:T(8,128)} %get-tuple-element.18.top_ref, f32[264,128]{1,0:T(8,128)} %copy-done.4, ...), custom_call_target="tpu_custom_call" | custom-call | flops 1000000000 | bytes 1000000 | tf_op jit(solution)/shard_map/turn/pallas_call | solution.py:842
  39.1 3.3 %collective-permute-start.4 = (f32[72,128]{1,0:T(8,128)}, f32[72,128]{1,0:T(8,128)S(1)}, u32[]{:S(2)}, u32[]{:S(2)}) collective-permute-start(f32[72,128]{1,0:T(8,128)} %get-tuple-element.21), channel_id=1, source_target_pairs={{2,0},{3,1},{0,2},{1,3},{6,4},{7,5},{4,6},{5,7},{10,8},{11,9},{8,1... | collective-permute-start | bytes 110600 | tf_op jit(solution)/shard_map/ppermute | solution.py:741
  42.5 1.6 %collective-permute-start.2 = (f32[324,128]{1,0:T(8,128)}, f32[324,128]{1,0:T(8,128)S(1)}, u32[]{:S(2)}, u32[]{:S(2)}) collective-permute-start(f32[324,128]{1,0:T(8,128)} %get-tuple-element.19), channel_id=1, source_target_pairs={{3,0},{0,1},{1,2},{2,3},{7,4},{4,5},{5,6},{6,7},{11,8},{8,9},{9,10... | collective-permute-start | bytes 497672 | tf_op jit(solution)/shard_map/ppermute | solution.py:741
  44.0 2.2 %collective-permute-start.3 = (f32[324,128]{1,0:T(8,128)}, f32[324,128]{1,0:T(8,128)S(1)}, u32[]{:S(2)}, u32[]{:S(2)}) collective-permute-start(f32[324,128]{1,0:T(8,128)} %get-tuple-element.20), channel_id=1, source_target_pairs={{1,0},{2,1},{3,2},{0,3},{5,4},{6,5},{7,6},{4,7},{9,8},{10,9},{11,1... | collective-permute-start | bytes 497672 | tf_op jit(solution)/shard_map/ppermute | solution.py:741
  46.3 9.8 %beside_gx.1.before_ref = f32[32,16,256]{2,1,0:T(8,128)} custom-call(s32[164]{0:T(256)} %constant.18.clone.table_ref, f32[32,16,256]{2,1,0:T(8,128)} %own.1.before_ref, f32[6,4,8,256]{3,2,1,0:T(8,128)} %get-tuple-element.17.pack_ref, f32[264,128]{1,0:T(8,128)} %copy-done.4, f32[264,128]{1,0:T(8,128)} %copy-done.5), custom_call_target="tpu_custom_call" | custom-call | flops 10000000000 | bytes 1000000 | tf_op jit(solution)/shard_map/beside_gx/pallas_call | solution.py:867
  56.2 0.7 copy-done
  56.9 0.0 collective-permute-done.3.rest_3_.rest_1_
  56.9 0.0 collective-permute-done.4
  57.0 0.6 copy-done.2
  57.6 0.0 collective-permute-start.6
  57.6 1.7 %collective-permute-start.5 = (f32[288,128]{1,0:T(8,128)S(1)}, f32[288,128]{1,0:T(8,128)S(1)}, u32[]{:S(2)}, u32[]{:S(2)}) collective-permute-start(f32[288,128]{1,0:T(8,128)S(1)} %pad_maximum_fusion), channel_id=1, source_target_pairs={{12,0},{16,4},{20,8},{24,12},{28,16},{0,20},{4,24},{8,28},{13,1},{... | collective-permute-start | bytes 442376 | tf_op jit(solution)/shard_map/ppermute | solution.py:741
  59.3 6.7 %beside_gy.1.near_ref = f32[32,16,256]{2,1,0:T(8,128)} custom-call(s32[88]{0:T(128)} %constant.19.clone.table_ref, f32[32,16,256]{2,1,0:T(8,128)} %beside_gx.1.before_ref, f32[6,4,8,256]{3,2,1,0:T(8,128)} %get-tuple-element.17.pack_ref, f32[324,128]{1,0:T(8,128)} %copy-done.1, f32[324,128]{1,0:T(8,128)} %copy-done.2), custom_call_target="tpu_custom_call" | custom-call | flops 10000000000 | bytes 1000000 | tf_op jit(solution)/shard_map/beside_gy/pallas_call | solution.py:867
  66.0 4.9 %leaf.1.down_ref = f32[96,256]{1,0:T(8,128)} custom-call(f32[2,3,4,8,128]{4,3,2,1,0:T(8,128)} %get-tuple-element.14.leaf_ref.own_ref, f32[8,128]{1,0:T(8,128)} %constant.14.clone.rows_ref, f32[3,128,128]{2,1,0:T(8,128)} %constant.15.clone.cols_ref, f32[264,128]{1,0:T(8,128)} %copy-done.4, f32[264,128]{1,0:T(8,128)} %copy-done.5, f32[324,128]{1,0:T(8,128)} %copy-done.1, ...), custom_call_target="tpu_custom_call" | custom-call | flops 6000000000 | bytes 1000000 | tf_op jit(solution)/shard_map/leaf/pallas_call | solution.py:891
  71.0 0.7 copy-done.3
  71.7 15.4 %far.1 = f32[12,4,8,256]{3,2,1,0:T(8,128)} custom-call(s32[32]{0:T(128)} %constant.20.clone.slot_ref, s32[64]{0:T(128)} %reshape.7.counts_ref, f32[96,256]{1,0:T(8,128)} %leaf.1.down_ref, f32[36,24,128]{2,1,0:T(8,128)} %bitcast.1, f32[32,16,256]{2,1,0:T(8,128)} %beside_gy.1.near_ref, f32[6,4,8,256]{3,2,1,0:T(8,128)} %get-tuple-element.17.pack_ref, ...), custom_call_target="tpu_custom_call" | custom-call | flops 10000000000 | bytes 1000000 | tf_op jit(solution)/shard_map/far/pallas_call | solution.py:911
  (18 shorter events, 0.1 us)
Async XLA Ops:
  7.8 28.7 %collective-permute-start = (f32[264,128]{1,0:T(8,128)}, f32[264,128]{1,0:T(8,128)S(1)}, u32[]{:S(2)}, u32[]{:S(2)}) collective-permute-start(f32[264,128]{1,0:T(8,128)} %get-tuple-element.15), channel_id=1, source_target_pairs={{28,0},{0,4},{4,8},{8,12},{12,16},{16,20},{20,24},{24,28},{29,1},{... | collective-permute-start | bytes 405512 | tf_op jit(solution)/shard_map/ppermute | solution.py:741
  8.3 28.2 %collective-permute-start.1 = (f32[264,128]{1,0:T(8,128)}, f32[264,128]{1,0:T(8,128)S(1)}, u32[]{:S(2)}, u32[]{:S(2)}) collective-permute-start(f32[264,128]{1,0:T(8,128)} %get-tuple-element.16), channel_id=1, source_target_pairs={{4,0},{8,4},{12,8},{16,12},{20,16},{24,20},{28,24},{0,28},{5,1},{9... | collective-permute-start | bytes 405512 | tf_op jit(solution)/shard_map/ppermute | solution.py:741
  36.5 0.7 copy-start.4
  36.5 0.7 copy-start.5
  39.1 17.8 %collective-permute-start.4 = (f32[72,128]{1,0:T(8,128)}, f32[72,128]{1,0:T(8,128)S(1)}, u32[]{:S(2)}, u32[]{:S(2)}) collective-permute-start(f32[72,128]{1,0:T(8,128)} %get-tuple-element.21), channel_id=1, source_target_pairs={{2,0},{3,1},{0,2},{1,3},{6,4},{7,5},{4,6},{5,7},{10,8},{11,9},{8,1... | collective-permute-start | bytes 110600 | tf_op jit(solution)/shard_map/ppermute | solution.py:741
  42.5 13.7 %collective-permute-start.2 = (f32[324,128]{1,0:T(8,128)}, f32[324,128]{1,0:T(8,128)S(1)}, u32[]{:S(2)}, u32[]{:S(2)}) collective-permute-start(f32[324,128]{1,0:T(8,128)} %get-tuple-element.19), channel_id=1, source_target_pairs={{3,0},{0,1},{1,2},{2,3},{7,4},{4,5},{5,6},{6,7},{11,8},{8,9},{9,10... | collective-permute-start | bytes 497672 | tf_op jit(solution)/shard_map/ppermute | solution.py:741
  44.0 12.9 %collective-permute-start.3 = (f32[324,128]{1,0:T(8,128)}, f32[324,128]{1,0:T(8,128)S(1)}, u32[]{:S(2)}, u32[]{:S(2)}) collective-permute-start(f32[324,128]{1,0:T(8,128)} %get-tuple-element.20), channel_id=1, source_target_pairs={{1,0},{2,1},{3,2},{0,3},{5,4},{6,5},{7,6},{4,7},{9,8},{10,9},{11,1... | collective-permute-start | bytes 497672 | tf_op jit(solution)/shard_map/ppermute | solution.py:741
  56.1 0.8 copy-start
  56.1 0.8 copy-start.1
  56.9 0.7 copy-start.2
  57.6 13.4 %collective-permute-start.6 = (f32[288,128]{1,0:T(8,128)S(1)}, f32[288,128]{1,0:T(8,128)S(1)}, u32[]{:S(2)}, u32[]{:S(2)}) collective-permute-start(f32[288,128]{1,0:T(8,128)S(1)} %pad_maximum_fusion), channel_id=1, source_target_pairs={{20,0},{24,4},{28,8},{0,12},{4,16},{8,20},{12,24},{16,28},{21,1},{... | collective-permute-start | bytes 442376 | tf_op jit(solution)/shard_map/ppermute | solution.py:741
  57.6 13.3 %collective-permute-start.5 = (f32[288,128]{1,0:T(8,128)S(1)}, f32[288,128]{1,0:T(8,128)S(1)}, u32[]{:S(2)}, u32[]{:S(2)}) collective-permute-start(f32[288,128]{1,0:T(8,128)S(1)} %pad_maximum_fusion), channel_id=1, source_target_pairs={{12,0},{16,4},{20,8},{24,12},{28,16},{0,20},{4,24},{8,28},{13,1},{... | collective-permute-start | bytes 442376 | tf_op jit(solution)/shard_map/ppermute | solution.py:741
  71.0 0.8 copy-start.3

commit v5 on v4

--- a/solution.py
+++ b/solution.py
@@ -14,7 +14,6 @@
 LANES = 128
 F32 = jnp.float32
 BF16 = jnp.bfloat16
-HIGHEST = lax.Precision.HIGHEST
 
 
 def sphere_points(amount):
@@ -36,12 +35,6 @@
     return jnp.dot(left, right, preferred_element_type=F32)
 
 
-def dot_nt(left, right):
-    return lax.dot_general(
-        left, right, (((1,), (1,)), ((), ())), precision=HIGHEST, preferred_element_type=F32
-    )
-
-
 def two_terms(high, low):
     return jnp.concatenate(
         [
@@ -52,9 +45,45 @@
     )
 
 
-def cubes(dx, dy, dz):
-    inverse = lax.rsqrt(dx * dx + dy * dy + dz * dz + SMOOTH2)
-    return inverse * inverse * inverse
+def dot_split(left, right):
+    rows = left.shape[0]
+    both = bdot(two_terms(*split(left)), jnp.concatenate(split(right), axis=0))
+    return both[:rows] + both[rows:]
+
+
+def dot_split_nt(left, right):
+    rows = left.shape[0]
+    both = lax.dot_general(
+        two_terms(*split(left)),
+        jnp.concatenate(split(right), axis=1),
+        (((1,), (1,)), ((), ())),
+        preferred_element_type=F32,
+    )
+    return both[:rows] + both[rows:]
+
+
+def lay_points(cols_ref, rows_ref):
+    for axis in range(3):
+        row = rows_ref[axis : axis + 1, :]
+        cols_ref[axis] = jnp.broadcast_to(row, (LANES, LANES)).T
+
+
+def lay_surface(surface, cols_ref):
+    total = jnp.zeros((LANES, LANES), F32)
+    for axis in range(3):
+        surface[axis] = -3.0 * cols_ref[axis]
+        total = total + 2.25 * cols_ref[axis] * cols_ref[axis]
+    surface[3] = total
+
+
+def surface_distance(surface, place):
+    square = place[0] * place[0] + place[1] * place[1] + place[2] * place[2] + SMOOTH2
+    return (
+        (square + surface[3])
+        + place[0] * surface[0]
+        + place[1] * surface[1]
+        + place[2] * surface[2]
+    )
 
 
 SIDES = (-1, 1)
@@ -90,41 +119,59 @@
     offsets_ref,
     strengths_ref,
     rows_ref,
-    cols_ref,
     inverse_ref,
     pack_ref,
     leaf_ref,
     top_ref,
     matrix_ref,
+    living_ref,
     *rest,
 ):
     parcels = rest[:2]
-    check = rest[2]
+    check, surface, cols_ref, strong, inverse, arrived = rest[2:]
+    copies = [
+        pltpu.make_async_copy(source, target, arrived.at[k])
+        for k, (source, target) in enumerate(
+            (
+                (offsets_ref, pack_ref.at[0:3]),
+                (strengths_ref, strong),
+                (inverse_ref, inverse),
+            )
+        )
+    ]
+    for copy in copies:
+        copy.start()
+    lay_points(cols_ref, rows_ref)
+    lay_surface(surface, cols_ref)
+    for copy in copies:
+        copy.wait()
     point = [rows_ref[j : j + 1, :] for j in range(3)]
-    lane = lax.broadcasted_iota(jnp.int32, (1, 2 * LANES), 1)
+    lane = lax.broadcasted_iota(jnp.int32, (1, LANES), 1)
     expansion = inverse_ref.shape[0]
     matrix_ref[...] = jnp.zeros_like(matrix_ref)
-    matrix_ref[:expansion, :expansion] = inverse_ref[...]
-    pack_ref[0:3] = offsets_ref[...]
+    matrix_ref[:expansion, :expansion] = inverse[...]
 
     def one_column(i, j):
-        row = [offsets_ref[c, i, pl.ds(j, 1), :] for c in range(3)]
-        at = (i * size_y + j) * 2
-        last = jnp.where(lane < LANES, counts_ref[at], counts_ref[at + 1] + LANES)
+        row = [pack_ref[c, i, pl.ds(j, 1), :] for c in range(3)]
+        count = counts_ref[i, pl.ds(j, 1), :]
+        living = jnp.concatenate(
+            [
+                jnp.where(lane < jnp.broadcast_to(count[:, k : k + 1], (1, LANES)), 1.0, 0.0)
+                for k in range(2)
+            ],
+            axis=1,
+        )
+        living_ref[i, pl.ds(j, 1), :] = living
         charges = []
         for c in range(3):
-            value = jnp.where(
-                lane < last, STRENGTH_SCALE * strengths_ref[c, i, pl.ds(j, 1), :], 0.0
-            )
+            value = STRENGTH_SCALE * strong[c, i, pl.ds(j, 1), :] * living
             pack_ref[3 + c, i, pl.ds(j, 1), :] = value
             charges.append(value)
         charge = jnp.concatenate(charges + [jnp.zeros((5, 2 * LANES), F32)], axis=0)
         for half in range(2):
             lanes = slice(half * LANES, (half + 1) * LANES)
-            delta = [1.5 * cols_ref[axis] - row[axis][:, lanes] for axis in range(3)]
-            kernel = lax.rsqrt(
-                delta[0] * delta[0] + delta[1] * delta[1] + delta[2] * delta[2] + SMOOTH2
-            )
+            place = [row[axis][:, lanes] for axis in range(3)]
+            kernel = lax.rsqrt(surface_distance(surface, place))
             both = jnp.concatenate(split(charge[:, lanes]), axis=0)
             total = lax.dot_general(
                 jnp.concatenate([both, both], axis=1),
@@ -145,11 +192,14 @@
     lax.fori_loop(0, size_x * size_y // 4, columns, 0)
     matrix = matrix_ref[...]
     rows = 6 * size_x * size_y
-    charges = 0.5 * dot_nt(check[...].reshape(rows, LANES), matrix)
+    charges = 0.5 * dot_split_nt(check[...].reshape(rows, LANES), matrix)
     leaf_ref[...] = charges.reshape(2, 3, size_x, size_y, LANES)
     half_x = size_x // 2
     half_y = size_y // 2
-    total = jnp.zeros((3 * half_x * half_y, LANES), F32)
+    count = 3 * half_x * half_y
+    padding = -count % 16
+    filler = [jnp.zeros((padding, LANES), F32)] if padding else []
+    total = jnp.zeros((count + padding, LANES), F32)
     for a in range(2):
         for b in range(2):
             for e in range(2):
@@ -165,13 +215,8 @@
                     for c in range(3)
                     for x in range(half_x)
                 ]
-                total = total + jnp.dot(
-                    jnp.concatenate(pieces, axis=0),
-                    table,
-                    precision=HIGHEST,
-                    preferred_element_type=F32,
-                )
-    tops = dot_nt(total, matrix)
+                total = total + dot_split(jnp.concatenate(pieces + filler, axis=0), table)
+    tops = dot_split_nt(total, matrix)[:count]
     top_ref[...] = tops
     (_, second, end), _ = parcel_rows(size_x, size_y)
     for side, parcel in zip(SIDES, parcels):
@@ -481,9 +526,10 @@
     return result
 
 
-def leaf_kernel(size_x, size_y, own_ref, rows_ref, cols_ref, *rest):
+def leaf_kernel(size_x, size_y, own_ref, rows_ref, *rest):
     parcels = rest[:4]
-    down_ref, base, leaf_ref = rest[4:]
+    down_ref, base, leaf_ref, cols_ref = rest[4:]
+    lay_points(cols_ref, rows_ref)
     for depth in range(2):
         for c in range(3):
             for x in range(size_x):
@@ -574,13 +620,12 @@
     tops_y,
     chunk,
     slot_ref,
-    counts_ref,
+    living_ref,
     down_ref,
     tops_ref,
     near_ref,
     pack_ref,
     rows_ref,
-    cols_ref,
     pattern_ref,
     inverse_ref,
     out_ref,
@@ -589,6 +634,9 @@
     down,
     top_down,
     local,
+    surface,
+    squares_y,
+    cols_ref,
 ):
     half_x = size_x // 2
     half_y = size_y // 2
@@ -596,6 +644,7 @@
     across = tops_x + half_x - 1
     along = tops_y + half_y - 1
     point = [rows_ref[j : j + 1, :] for j in range(3)]
+    lay_points(cols_ref, rows_ref)
     for axis in range(3):
         base[axis] = 1.8 * point[axis] - 1.8 * cols_ref[axis]
 
@@ -631,7 +680,14 @@
     top_down[...] = jnp.zeros_like(top_down)
     parts = -(-along // chunk)
 
-    def top_row(step, carry):
+    def square_y(wy, carry):
+        dy = base[1] + 2.0 * (first_y - (wy - (half_y - 1))).astype(F32)
+        squares_y[wy] = dy * dy
+        return carry
+
+    lax.fori_loop(0, parts * chunk, square_y, 0)
+
+    def top_row(step):
         wx = step // parts
         start = (step % parts) * chunk
         gap_x = first_x - (wx - (half_x - 1))
@@ -643,20 +699,27 @@
             wy = start + k
             gap_y = first_y - (wy - (half_y - 1))
             distant = (jnp.abs(gap_x) >= 2) | (jnp.abs(gap_y) >= 2)
-            dy = base[1] + 2.0 * gap_y.astype(F32)
-            tables.append(lax.rsqrt(squares + dy * dy).astype(BF16))
+            tables.append(lax.rsqrt(squares + squares_y[wy]).astype(BF16))
             rows = windows[wx, pl.ds(wy * group, half_y * group), :]
             pieces.append(jnp.where(distant, rows, 0.0))
         high, low = split(jnp.concatenate(pieces, axis=1))
-        top_down[...] += bdot(
-            jnp.concatenate([high, low], axis=0), jnp.concatenate(tables, axis=0)
-        )
+        return bdot(jnp.concatenate([high, low], axis=0), jnp.concatenate(tables, axis=0))
+
+    together = 3
+    steps = across * parts
+
+    def top_rows(index, carry):
+        found = [top_row(index * together + k) for k in range(together)]
+        top_down[...] += sum(found[1:], found[0])
         return carry
 
-    lax.fori_loop(0, across * parts, top_row, 0)
+    lax.fori_loop(0, steps // together, top_rows, 0)
+    for step in range(steps - steps % together, steps):
+        top_down[...] += top_row(jnp.int32(step))
     matrix = inverse_ref[...]
     rows = half_y * group
-    top_local = dot_nt(top_down[:rows] + top_down[rows:], matrix)
+    top_local = dot_split_nt(top_down[:rows] + top_down[rows:], matrix)
+    lay_surface(surface, cols_ref)
     down[...] = down_ref[...]
     for a in range(2):
         for b in range(2):
@@ -668,9 +731,7 @@
                 table = lax.rsqrt(
                     delta[0] * delta[0] + delta[1] * delta[1] + delta[2] * delta[2] + SMOOTH2
                 )
-                inherited = jnp.dot(
-                    top_local, table, precision=HIGHEST, preferred_element_type=F32
-                )
+                inherited = dot_split(top_local, table)
                 for y in range(half_y):
                     for x in range(half_x):
                         for c in range(3):
@@ -679,21 +740,20 @@
                                 y * group + x * 4 + c : y * group + x * 4 + c + 1
                             ]
     for e in range(2):
-        part = 0.5 * dot_nt(down[:, e * LANES : (e + 1) * LANES], matrix)
+        part = 0.5 * dot_split_nt(down[:, e * LANES : (e + 1) * LANES], matrix)
         local[e] = part.reshape(3, size_x, size_y, LANES)
-
-    lane = lax.broadcasted_iota(jnp.int32, (1, LANES), 1)
 
     def one_column(index):
         i = index // size_y
         j = index % size_y
         row = [pack_ref[c, i, pl.ds(j, 1), :] for c in range(3)]
+        alive = living_ref[i, pl.ds(j, 1), :]
         results = []
         for half in range(2):
             lanes = slice(half * LANES, (half + 1) * LANES)
             place = [row[axis][:, lanes] for axis in range(3)]
-            delta = [place[axis] - 1.5 * cols_ref[axis] for axis in range(3)]
-            high, low = split(cubes(*delta))
+            inverse = lax.rsqrt(surface_distance(surface, place))
+            high, low = split(inverse * inverse * inverse)
             charge = jnp.concatenate(
                 [local[half, c, i, pl.ds(j, 1), :] for c in range(3)], axis=0
             )
@@ -703,7 +763,7 @@
             total = bdot(two_terms(*split(weight)), jnp.concatenate([high, low], axis=0))
             total = total[:16] + total[16:] + near_ref[index, :, lanes]
             place[2] = place[2] + (half - 0.5)
-            living = jnp.where(lane < counts_ref[2 * index + half], 1.0, 0.0)
+            living = alive[:, lanes]
             square = (
                 place[0] * place[0] + place[1] * place[1] + place[2] * place[2] + SMOOTH2
             )
@@ -784,7 +844,6 @@
     tops_y = lanes_y * half_y
     points = sphere_points(expansion)
     rows = jnp.asarray(np.concatenate([points, np.zeros((5, LANES), np.float32)], axis=0))
-    cols = jnp.asarray(np.repeat(points[:, :, None], LANES, axis=2))
     patterns = np.zeros((2, 16, LANES), np.float32)
     for half in range(2):
         lifted = (1.5 * points).astype(np.float32)
@@ -794,9 +853,12 @@
             patterns[half, 3 * k : 3 * k + 3, :] = factors[k]
     patterns = jnp.asarray(patterns)
 
-    params = pltpu.CompilerParams(vmem_limit_bytes=58 * 2**20)
+    def params(mebibytes):
+        return pltpu.CompilerParams(vmem_limit_bytes=mebibytes * 2**20)
+
     smem = pl.BlockSpec(memory_space=pltpu.SMEM)
     vmem = pl.BlockSpec(memory_space=pltpu.VMEM)
+    hbm = pl.BlockSpec(memory_space=pltpu.HBM)
 
     def cost(flops):
         return pl.CostEstimate(flops=flops, bytes_accessed=10**6, transcendentals=0)
@@ -810,16 +872,24 @@
             jax.ShapeDtypeStruct((2, 3, size_x, size_y, LANES), F32),
             jax.ShapeDtypeStruct((top_rows, LANES), F32),
             jax.ShapeDtypeStruct((LANES, LANES), F32),
+            jax.ShapeDtypeStruct((size_x, size_y, depth * LANES), F32),
             *[jax.ShapeDtypeStruct((end_x, LANES), F32)] * 2,
         ),
-        in_specs=[smem] + [vmem] * 5,
-        out_specs=(vmem,) * 6,
-        scratch_shapes=[pltpu.VMEM((2, 3, size_x, size_y, LANES), F32)],
-        compiler_params=params,
+        in_specs=[vmem, hbm, hbm, vmem, hbm],
+        out_specs=(vmem,) * 7,
+        scratch_shapes=[
+            pltpu.VMEM((2, 3, size_x, size_y, LANES), F32),
+            pltpu.VMEM((4, LANES, LANES), F32),
+            pltpu.VMEM((3, LANES, LANES), F32),
+            pltpu.VMEM(strengths.shape, F32),
+            pltpu.VMEM(check_inverse.shape, F32),
+            pltpu.SemaphoreType.DMA((3,)),
+        ],
+        compiler_params=params(12),
         cost_estimate=cost(6 * 10**9),
         name="up",
-    )(counts.reshape(-1), offsets, strengths, rows, cols, check_inverse)
-    pack, leaf_charges, top_charges, matrix, to_below, to_above = made
+    )(counts, offsets, strengths, rows, check_inverse)
+    pack, leaf_charges, top_charges, matrix, living, to_below, to_above = made
     below = moved(to_above, "gx", -1)
     above = moved(to_below, "gx", 1)
 
@@ -834,7 +904,7 @@
             pltpu.VMEM((size_x * size_y, 4, 2 * LANES, LANES), F32),
             pltpu.VMEM((size_x * size_y, 4, 16, 2 * LANES), F32),
         ],
-        compiler_params=params,
+        compiler_params=params(28),
         cost_estimate=cost(3 * 10**10),
         name="own",
     )(jnp.asarray(own_table), pack)
@@ -848,7 +918,7 @@
         ),
         in_specs=[vmem] * 5,
         out_specs=(vmem,) * 3,
-        compiler_params=params,
+        compiler_params=params(12),
         cost_estimate=cost(10**9),
         name="turn",
     )(leaf_charges, pack, top_charges, below, above)
@@ -874,7 +944,7 @@
                 pltpu.VMEM((columns, 4, 16, 2 * LANES), F32),
                 pltpu.VMEM((6, columns, 2 * LANES), F32),
             ],
-            compiler_params=params,
+            compiler_params=params(20),
             cost_estimate=cost(10**10),
             name="beside_" + axis,
         )(jnp.asarray(table), before, pack, *parcels)
@@ -891,18 +961,19 @@
     down = pl.pallas_call(
         functools.partial(leaf_kernel, size_x, size_y),
         out_shape=jax.ShapeDtypeStruct((3 * size_x * size_y, 2 * LANES), F32),
-        in_specs=[vmem] * 7,
+        in_specs=[vmem] * 6,
         out_specs=vmem,
         scratch_shapes=[
             pltpu.VMEM((3, LANES, LANES), F32),
             pltpu.VMEM(
                 (2, 3, size_x + 2 * WIDTH, size_y + 2 * WIDTH, LANES), F32
             ),
+            pltpu.VMEM((3, LANES, LANES), F32),
         ],
-        compiler_params=params,
+        compiler_params=params(12),
         cost_estimate=cost(6 * 10**9),
         name="leaf",
-    )(leaf_charges, rows, cols, below, above, low, high)
+    )(leaf_charges, rows, below, above, low, high)
 
     across = tops_x + half_x - 1
     along = tops_y + half_y - 1
@@ -911,7 +982,7 @@
     return pl.pallas_call(
         functools.partial(far_kernel, size_x, size_y, tops_x, tops_y, chunk),
         out_shape=jax.ShapeDtypeStruct((12, size_x, size_y, depth * LANES), F32),
-        in_specs=[smem] * 2 + [vmem] * 8,
+        in_specs=[smem] + [vmem] * 8,
         out_specs=vmem,
         scratch_shapes=[
             pltpu.VMEM((3, LANES, LANES), F32),
@@ -919,19 +990,21 @@
             pltpu.VMEM((3 * size_x * size_y, 2 * LANES), F32),
             pltpu.VMEM((2 * half_y * half_x * 4, LANES), F32),
             pltpu.VMEM((2, 3, size_x, size_y, LANES), F32),
+            pltpu.VMEM((4, LANES, LANES), F32),
+            pltpu.VMEM((parts * chunk, LANES, LANES), F32),
+            pltpu.VMEM((3, LANES, LANES), F32),
         ],
-        compiler_params=params,
+        compiler_params=params(40),
         cost_estimate=cost(10**10),
         name="far",
     )(
         jnp.asarray(slots.reshape(-1)),
-        counts.reshape(-1),
+        living,
         down,
         blocks,
         near,
         pack,
         rows,
-        cols,
         patterns,
         matrix,
     )

time: 87.5 us -> 73.6 us (0.84)
  Pallas kernels: 70.4 us -> 56.5 us
    pallas_call x1, Pallas kernels: 15.4 us -> 11.4 us  [body(): pl.pallas_call(functools.partial(far_kernel, size_x, size_y, tops_x, tops...]
    pallas_call x2, Pallas kernels: 16.5 us -> 13.6 us  [beside_near(): pl.pallas_call(functools.partial(halo_kernel, size_x, size_y, axis, tasks...]
    pallas_call x1, Pallas kernels: 6.39 us -> 4.08 us  [body(): pl.pallas_call(functools.partial(up_kernel, size_x, size_y), out_shape=(j...]
    pallas_call x1, Pallas kernels: 4.88 us -> 3.06 us  [body(): pl.pallas_call(functools.partial(leaf_kernel, size_x, size_y), out_shape=...]
    pallas_call x1, Pallas kernels: 1.92 us -> 0.11 us  [body(): pl.pallas_call(functools.partial(turn_kernel, size_x, size_y), out_shape=...]
    pallas_call x1, Pallas kernels: 25.3 us -> 24.2 us  [body(): pl.pallas_call(functools.partial(own_kernel, size_x, size_y, own_tasks),...]
    unnamed x16 -> x22, local copies, waits for them, and re-layouts: 3.57 us -> 4.14 us
  transfers between devices with their start and end apart: 7 -> 7, of which waited for: 0 -> 0; matrix products, arithmetic and copies ran while one was open for 0% -> 0% of each run, Pallas kernels for 54% -> 56%
where the time goes in v5:
time: 73.6 us; the launch traced here: 73.3 us
  Pallas kernels  56.5 us (77%)
  starting transfers between devices  12.4 us (17%)
  local copies, waits for them, and re-layouts  4.17 us (6%)
    pallas_call x1, Pallas kernels, body(): pl.pallas_call(functools.partial(own_kernel, size_x, size_y, own_tasks),...  24.2 us
    pallas_call x2, Pallas kernels, beside_near(): pl.pallas_call(functools.partial(halo_kernel, size_x, size_y, axis, tasks...  13.6 us
    ppermute x7, starting transfers between devices, moved(): lax.ppermute(array, axis, [((i + step) % count, i) for i in range(count)])  12.4 us
    pallas_call x1, Pallas kernels, body(): pl.pallas_call(functools.partial(far_kernel, size_x, size_y, tops_x, tops...  11.4 us
    unnamed x22, local copies, waits for them, and re-layouts  4.14 us
    pallas_call x1, Pallas kernels, body(): pl.pallas_call(functools.partial(up_kernel, size_x, size_y), out_shape=(j...  4.08 us
    pallas_call x1, Pallas kernels, body(): pl.pallas_call(functools.partial(leaf_kernel, size_x, size_y), out_shape=...  3.06 us
  transfers between devices with their start and end apart: 7, of which 0 were waited for; matrix products, arithmetic and copies ran while one was open for 0% of the time, Pallas kernels for 56%

profile of v5, /device:TPU:0, one launch (start us, length us, event | category | flops | bytes accessed | tf_op | source)
XLA Modules:
  0.0 73.3 jit_solution(8361477848578593980)
XLA Ops:
  0.0 0.8 %copy.11.counts_ref = s32[4,8,2]{2,1,0:T(8,128)S(1)} copy(s32[4,8,2]{1,2,0:T(2,128)} %param.12) | data formatting | bytes 512 | tf_op args[2]
  0.8 0.9 %copy-done = f32[3,4,8,256]{3,2,1,0:T(8,128)S(1)} copy-done((f32[3,4,8,256]{3,2,1,0:T(8,128)S(1)}, f32[3,4,8,256]{3,2,1,0:T(8,128)}, u32[]{:S(2)}) %copy-start) | copy-done | bytes 98328
  1.7 0.9 %copy-done.1 = f32[3,4,8,256]{3,2,1,0:T(8,128)S(1)} copy-done((f32[3,4,8,256]{3,2,1,0:T(8,128)S(1)}, f32[3,4,8,256]{3,2,1,0:T(8,128)}, u32[]{:S(2)}) %copy-start.1) | copy-done | bytes 98328
  2.6 0.8 %copy-done.2 = f32[121,121]{1,0:T(8,128)S(1)} copy-done((f32[121,121]{1,0:T(8,128)S(1)}, f32[121,121]{1,0:T(8,128)}, u32[]{:S(2)}) %copy-start.2) | copy-done | bytes 58588
  3.4 4.1 %up.1 = (f32[6,4,8,256]{3,2,1,0:T(8,128)S(1)}, f32[2,3,4,8,128]{4,3,2,1,0:T(8,128)S(1)}, f32[24,128]{1,0:T(8,128)S(1)}, f32[128,128]{1,0:T(8,128)S(1)}, f32[4,8,...) custom-call(s32[4,8,2]{2,1,0:T(8,128)S(1)} %copy.11.counts_ref, f32[3,4,8,256]{3,2,1,0:T(8,128)S(1)} %copy-done, ...), custom_call_target="tpu_custom_call" | custom-call | flops 6000000000 | bytes 1000000 | tf_op jit(solution)/shard_map/up/pallas_call | solution.py:868
  7.5 0.0 copy-start.5
  7.5 0.5 collective-permute-start
  8.0 2.9 %collective-permute-start.1 = (f32[264,128]{1,0:T(8,128)S(1)}, f32[264,128]{1,0:T(8,128)S(1)}, u32[]{:S(2)}, u32[]{:S(2)}) collective-permute-start(f32[264,128]{1,0:T(8,128)S(1)} %get-tuple-element.18), channel_id=1, source_target_pairs={{4,0},{8,4},{12,8},{16,12},{20,16},{24,20},{28,24},{0,28},{5,1},{9... | collective-permute-start | bytes 405512 | tf_op jit(solution)/shard_map/ppermute | solution.py:801
  11.0 24.2 %own.1.before_ref = f32[32,16,256]{2,1,0:T(8,128)S(1)} custom-call(s32[440]{0:T(512)S(1)} %copy-done.5, f32[6,4,8,256]{3,2,1,0:T(8,128)S(1)} %get-tuple-element.19.pack_ref), custom_call_target="tpu_custom_call" | custom-call | flops 30000001024 | bytes 1000000 | tf_op jit(solution)/shard_map/own/pallas_call | solution.py:898
  35.2 0.0 collective-permute-done.below_ref.rest_0_
  35.2 0.1 turn.1
  35.3 3.3 %collective-permute-start.4 = (f32[72,128]{1,0:T(8,128)S(1)}, f32[72,128]{1,0:T(8,128)S(1)}, u32[]{:S(2)}, u32[]{:S(2)}) collective-permute-start(f32[72,128]{1,0:T(8,128)S(1)} %get-tuple-element.23), channel_id=1, source_target_pairs={{2,0},{3,1},{0,2},{1,3},{6,4},{7,5},{4,6},{5,7},{10,8},{11,9},{8,1... | collective-permute-start | bytes 110600 | tf_op jit(solution)/shard_map/ppermute | solution.py:801
  38.7 1.6 %collective-permute-start.2 = (f32[324,128]{1,0:T(8,128)S(1)}, f32[324,128]{1,0:T(8,128)S(1)}, u32[]{:S(2)}, u32[]{:S(2)}) collective-permute-start(f32[324,128]{1,0:T(8,128)S(1)} %get-tuple-element.21), channel_id=1, source_target_pairs={{3,0},{0,1},{1,2},{2,3},{7,4},{4,5},{5,6},{6,7},{11,8},{8,9},{9,10... | collective-permute-start | bytes 497672 | tf_op jit(solution)/shard_map/ppermute | solution.py:801
  40.2 2.2 %collective-permute-start.3 = (f32[324,128]{1,0:T(8,128)S(1)}, f32[324,128]{1,0:T(8,128)S(1)}, u32[]{:S(2)}, u32[]{:S(2)}) collective-permute-start(f32[324,128]{1,0:T(8,128)S(1)} %get-tuple-element.22), channel_id=1, source_target_pairs={{1,0},{2,1},{3,2},{0,3},{5,4},{6,5},{7,6},{4,7},{9,8},{10,9},{11,1... | collective-permute-start | bytes 497672 | tf_op jit(solution)/shard_map/ppermute | solution.py:801
  42.5 8.4 %beside_gx.1.before_ref = f32[32,16,256]{2,1,0:T(8,128)S(1)} custom-call(s32[164]{0:T(256)S(1)} %copy-done.6, f32[32,16,256]{2,1,0:T(8,128)S(1)} %own.1.before_ref, f32[6,4,8,256]{3,2,1,0:T(8,128)S(1)} %get-tuple-element.19.pack_ref, f32[264,128]{1,0:T(8,128)S(1)} %collective-permute-done.below_ref.rest_0_, ...), custom_call_target="tpu_custom_call" | custom-call | flops 10000000000 | bytes 1000000 | tf_op jit(solution)/shard_map/beside_gx/pallas_call | solution.py:937
  50.9 0.0 collective-permute-done.2.rest_2_.rest_0_
  50.9 0.0 copy-start.8
  51.0 0.1 collective-permute-start.6
  51.0 1.7 %collective-permute-start.5 = (f32[288,128]{1,0:T(8,128)S(1)}, f32[288,128]{1,0:T(8,128)S(1)}, u32[]{:S(2)}, u32[]{:S(2)}) collective-permute-start(f32[288,128]{1,0:T(8,128)S(1)} %pad_maximum_fusion), channel_id=1, source_target_pairs={{12,0},{16,4},{20,8},{24,12},{28,16},{0,20},{4,24},{8,28},{13,1},{... | collective-permute-start | bytes 442376 | tf_op jit(solution)/shard_map/ppermute | solution.py:801
  52.8 5.2 %beside_gy.1.near_ref = f32[32,16,256]{2,1,0:T(8,128)S(1)} custom-call(s32[88]{0:T(128)S(1)} %copy-done.8, f32[32,16,256]{2,1,0:T(8,128)S(1)} %beside_gx.1.before_ref, f32[6,4,8,256]{3,2,1,0:T(8,128)S(1)} %get-tuple-element.19.pack_ref, f32[324,128]{1,0:T(8,128)S(1)} %collective-permute-done.2.rest_2_.rest_0_, ...), custom_call_target="tpu_custom_call" | custom-call | flops 10000000000 | bytes 1000000 | tf_op jit(solution)/shard_map/beside_gy/pallas_call | solution.py:937
  58.0 3.1 %leaf.1.down_ref = f32[96,256]{1,0:T(8,128)S(1)} custom-call(f32[2,3,4,8,128]{4,3,2,1,0:T(8,128)S(1)} %get-tuple-element.16.leaf_ref.own_ref, f32[8,128]{1,0:T(8,128)S(1)} %copy-done.4, f32[264,128]{1,0:T(8,128)S(1)} %collective-permute-done.below_ref.rest_0_, f32[264,128]{1,0:T(8,128)S(1)} %collective-permute-done.1.above_ref.rest_1_, ...), custom_call_target="tpu_custom_call" | custom-call | flops 6000000000 | bytes 1000000 | tf_op jit(solution)/shard_map/leaf/pallas_call | solution.py:961
  61.1 0.0 copy-start.3
  61.2 0.7 copy-done.3
  61.8 11.4 %far.1 = f32[12,4,8,256]{3,2,1,0:T(8,128)} custom-call(s32[32]{0:T(128)S(1)} %copy-done.7, f32[4,8,256]{2,1,0:T(8,128)S(1)} %get-tuple-element.15.living_ref, f32[96,256]{1,0:T(8,128)S(1)} %leaf.1.down_ref, f32[36,24,128]{2,1,0:T(8,128)S(1)} %bitcast.1, f32[32,16,256]{2,1,0:T(8,128)S(1)} %beside_gy.1.near_ref, ...), custom_call_target="tpu_custom_call" | custom-call | flops 10000000000 | bytes 1000000 | tf_op jit(solution)/shard_map/far/pallas_call | solution.py:982
  (23 shorter events, 0.1 us)
Async XLA Ops:
  0.0 0.8 %copy-start.4 = (f32[8,128]{1,0:T(8,128)S(1)}, f32[8,128]{1,0:T(8,128)}, u32[]{:S(2)}) copy-start(f32[8,128]{1,0:T(8,128)} %constant.12.clone.rows_ref) | copy-start | bytes 12292
  0.8 0.9 %copy-start = (f32[3,4,8,256]{3,2,1,0:T(8,128)S(1)}, f32[3,4,8,256]{3,2,1,0:T(8,128)}, u32[]{:S(2)}) copy-start(f32[3,4,8,256]{3,2,1,0:T(8,128)} %offsets_ref.1) | copy-start | bytes 294916
  1.7 0.9 %copy-start.1 = (f32[3,4,8,256]{3,2,1,0:T(8,128)S(1)}, f32[3,4,8,256]{3,2,1,0:T(8,128)}, u32[]{:S(2)}) copy-start(f32[3,4,8,256]{3,2,1,0:T(8,128)} %strengths_ref.1) | copy-start | bytes 294916
  2.6 0.8 %copy-start.2 = (f32[121,121]{1,0:T(8,128)S(1)}, f32[121,121]{1,0:T(8,128)}, u32[]{:S(2)}) copy-start(f32[121,121]{1,0:T(8,128)} %inverse_ref.1) | copy-start | bytes 175696
  7.5 3.5 %copy-start.5 = (s32[440]{0:T(512)S(1)}, s32[440]{0:T(512)}, u32[]{:S(2)}) copy-start(s32[440]{0:T(512)} %constant.14.clone.table_ref) | copy-start | bytes 5284
  7.5 27.7 %collective-permute-start = (f32[264,128]{1,0:T(8,128)S(1)}, f32[264,128]{1,0:T(8,128)S(1)}, u32[]{:S(2)}, u32[]{:S(2)}) collective-permute-start(f32[264,128]{1,0:T(8,128)S(1)} %get-tuple-element.17), channel_id=1, source_target_pairs={{28,0},{0,4},{4,8},{8,12},{12,16},{16,20},{20,24},{24,28},{29,1},{... | collective-permute-start | bytes 405512 | tf_op jit(solution)/shard_map/ppermute | solution.py:801
  8.0 27.2 %collective-permute-start.1 = (f32[264,128]{1,0:T(8,128)S(1)}, f32[264,128]{1,0:T(8,128)S(1)}, u32[]{:S(2)}, u32[]{:S(2)}) collective-permute-start(f32[264,128]{1,0:T(8,128)S(1)} %get-tuple-element.18), channel_id=1, source_target_pairs={{4,0},{8,4},{12,8},{16,12},{20,16},{24,20},{28,24},{0,28},{5,1},{9... | collective-permute-start | bytes 405512 | tf_op jit(solution)/shard_map/ppermute | solution.py:801
  35.3 15.6 %collective-permute-start.4 = (f32[72,128]{1,0:T(8,128)S(1)}, f32[72,128]{1,0:T(8,128)S(1)}, u32[]{:S(2)}, u32[]{:S(2)}) collective-permute-start(f32[72,128]{1,0:T(8,128)S(1)} %get-tuple-element.23), channel_id=1, source_target_pairs={{2,0},{3,1},{0,2},{1,3},{6,4},{7,5},{4,6},{5,7},{10,8},{11,9},{8,1... | collective-permute-start | bytes 110600 | tf_op jit(solution)/shard_map/ppermute | solution.py:801
  38.7 3.8 %copy-start.6 = (s32[164]{0:T(256)S(1)}, s32[164]{0:T(256)}, u32[]{:S(2)}) copy-start(s32[164]{0:T(256)} %constant.15.clone.table_ref) | copy-start | bytes 1972
  38.7 12.2 %collective-permute-start.2 = (f32[324,128]{1,0:T(8,128)S(1)}, f32[324,128]{1,0:T(8,128)S(1)}, u32[]{:S(2)}, u32[]{:S(2)}) collective-permute-start(f32[324,128]{1,0:T(8,128)S(1)} %get-tuple-element.21), channel_id=1, source_target_pairs={{3,0},{0,1},{1,2},{2,3},{7,4},{4,5},{5,6},{6,7},{11,8},{8,9},{9,10... | collective-permute-start | bytes 497672 | tf_op jit(solution)/shard_map/ppermute | solution.py:801
  40.2 10.7 %collective-permute-start.3 = (f32[324,128]{1,0:T(8,128)S(1)}, f32[324,128]{1,0:T(8,128)S(1)}, u32[]{:S(2)}, u32[]{:S(2)}) collective-permute-start(f32[324,128]{1,0:T(8,128)S(1)} %get-tuple-element.22), channel_id=1, source_target_pairs={{1,0},{2,1},{3,2},{0,3},{5,4},{6,5},{7,6},{4,7},{9,8},{10,9},{11,1... | collective-permute-start | bytes 497672 | tf_op jit(solution)/shard_map/ppermute | solution.py:801
  50.9 1.8 %copy-start.8 = (s32[88]{0:T(128)S(1)}, s32[88]{0:T(128)}, u32[]{:S(2)}) copy-start(s32[88]{0:T(128)} %constant.16.clone.table_ref) | copy-start | bytes 1060
  51.0 10.1 %collective-permute-start.6 = (f32[288,128]{1,0:T(8,128)S(1)}, f32[288,128]{1,0:T(8,128)S(1)}, u32[]{:S(2)}, u32[]{:S(2)}) collective-permute-start(f32[288,128]{1,0:T(8,128)S(1)} %pad_maximum_fusion), channel_id=1, source_target_pairs={{20,0},{24,4},{28,8},{0,12},{4,16},{8,20},{12,24},{16,28},{21,1},{... | collective-permute-start | bytes 442376 | tf_op jit(solution)/shard_map/ppermute | solution.py:801
  51.0 10.0 %collective-permute-start.5 = (f32[288,128]{1,0:T(8,128)S(1)}, f32[288,128]{1,0:T(8,128)S(1)}, u32[]{:S(2)}, u32[]{:S(2)}) collective-permute-start(f32[288,128]{1,0:T(8,128)S(1)} %pad_maximum_fusion), channel_id=1, source_target_pairs={{12,0},{16,4},{20,8},{24,12},{28,16},{0,20},{4,24},{8,28},{13,1},{... | collective-permute-start | bytes 442376 | tf_op jit(solution)/shard_map/ppermute | solution.py:801
  61.1 0.7 copy-start.3
  61.1 0.7 copy-start.7

commit v6 on v5

--- a/solution.py
+++ b/solution.py
@@ -40,6 +40,21 @@
         [
             jnp.concatenate([high, high], axis=1),
             jnp.concatenate([low, jnp.zeros_like(low)], axis=1),
+        ],
+        axis=0,
+    )
+
+
+def three_terms(value):
+    first = value.astype(BF16)
+    rest = value - first.astype(F32)
+    second = rest.astype(BF16)
+    third = (rest - second.astype(F32)).astype(BF16)
+    return jnp.concatenate(
+        [
+            jnp.concatenate([first, first], axis=1),
+            jnp.concatenate([second, second], axis=1),
+            jnp.concatenate([third, jnp.zeros_like(third)], axis=1),
         ],
         axis=0,
     )
@@ -358,15 +373,15 @@
 
 
 def near_sums(target, blocks, spread, moments):
-    total = jnp.zeros((32, 2 * LANES), F32)
+    total = jnp.zeros((48, 2 * LANES), F32)
     for slot, shift_x, shift_y in blocks:
-        w_high, w_low = split(shifted(moments, slot, shift_x, shift_y))
+        weight = shifted(moments, slot, shift_x, shift_y)
         for half, terms in enumerate(pair_cubes(target, slot, shift_x, shift_y, spread)):
             part = slice(half * LANES, (half + 1) * LANES)
             total = total + bdot(
-                two_terms(w_high[:, part], w_low[:, part]), jnp.concatenate(terms, axis=0)
+                three_terms(weight[:, part]), jnp.concatenate(terms, axis=0)
             )
-    return total[:16] + total[16:]
+    return total[:16] + total[16:32] + total[32:]
 
 
 def run_tasks(size_y, tasks, table_ref, pack_ref, out_ref, lift, spread, moments, adds):
@@ -434,17 +449,17 @@
             high = jnp.concatenate([h_first, h_second], axis=0)
             low = jnp.concatenate([l_first, l_second], axis=0)
             there = bdot(
-                two_terms(*split(shifted(moments, slot, -away_x, -away_y))),
+                three_terms(shifted(moments, slot, -away_x, -away_y)),
                 jnp.concatenate([high, low], axis=0),
             )
-            found.append((other, there[:16] + there[16:]))
+            found.append((other, there[:16] + there[16:32] + there[32:]))
             here = lax.dot_general(
-                two_terms(*split(shifted(moments, other, away_x, away_y))),
+                three_terms(shifted(moments, other, away_x, away_y)),
                 jnp.concatenate([high, low], axis=1),
                 (((1,), (1,)), ((), ())),
                 preferred_element_type=F32,
             )
-            total = total + here[:16] + here[16:]
+            total = total + here[:16] + here[16:32] + here[32:]
         found.append((slot, total))
         return found
 
@@ -515,15 +530,15 @@
                 if sources:
                     groups.setdefault(len(sources) // 3, []).append([i, j] + sources)
     result = []
+    flat = []
     for groups in kinds:
-        flat = []
         tasks = []
         for sources in sorted(groups, reverse=True):
             tasks.append((len(flat), len(groups[sources]), sources))
             for entry in groups[sources]:
                 flat += entry
-        result.append((np.array(flat, np.int32), tasks))
-    return result
+        result.append(tasks)
+    return np.array(flat, np.int32), result
 
 
 def leaf_kernel(size_x, size_y, own_ref, rows_ref, *rest):
@@ -565,8 +580,7 @@
     def one_row(shift_x, shifts_y):
         dx = base[0] - shift_x.astype(F32)
         tables = []
-        highs = []
-        lows = []
+        charges = []
         for shift_y in shifts_y:
             dy = base[1] - float(shift_y)
             flat = dx * dx + dy * dy + SMOOTH2
@@ -589,17 +603,10 @@
                         if abs(shift_y) == 3:
                             piece = piece * near_y[shift_y]
                         pieces.append(piece)
-                high, low = split(jnp.concatenate(pieces, axis=0))
-                highs.append(high)
-                lows.append(low)
-        rows = 3 * size_x * size_y
-        both = bdot(
-            jnp.concatenate(
-                [jnp.concatenate(highs, axis=1), jnp.concatenate(lows, axis=1)], axis=0
-            ),
-            jnp.concatenate(tables, axis=0),
+                charges.append(jnp.concatenate(pieces, axis=0).astype(BF16))
+        down_ref[...] += bdot(
+            jnp.concatenate(charges, axis=1), jnp.concatenate(tables, axis=0)
         )
-        down_ref[...] += both[:rows] + both[rows:]
 
     def outer(step, carry):
         one_row(jnp.where(step < 2, step - 3, step), (-3, -2, -1, 0, 1, 2, 3))
@@ -619,6 +626,7 @@
     tops_x,
     tops_y,
     chunk,
+    slots_at,
     slot_ref,
     living_ref,
     down_ref,
@@ -626,7 +634,6 @@
     near_ref,
     pack_ref,
     rows_ref,
-    pattern_ref,
     inverse_ref,
     out_ref,
     base,
@@ -659,7 +666,7 @@
         place_y = device % lanes_y
         away_x = lax.rem(place_x - mine_x + lanes_x, lanes_x)
         away_y = lax.rem(place_y - mine_y + lanes_y, lanes_y)
-        slot = slot_ref[away_x * lanes_y + away_y]
+        slot = slot_ref[slots_at + away_x * lanes_y + away_y]
         i = place_x * half_x
         j = place_y * half_y
         for c in range(3):
@@ -702,8 +709,9 @@
             tables.append(lax.rsqrt(squares + squares_y[wy]).astype(BF16))
             rows = windows[wx, pl.ds(wy * group, half_y * group), :]
             pieces.append(jnp.where(distant, rows, 0.0))
-        high, low = split(jnp.concatenate(pieces, axis=1))
-        return bdot(jnp.concatenate([high, low], axis=0), jnp.concatenate(tables, axis=0))
+        return bdot(
+            jnp.concatenate(pieces, axis=1).astype(BF16), jnp.concatenate(tables, axis=0)
+        )
 
     together = 3
     steps = across * parts
@@ -717,8 +725,7 @@
     for step in range(steps - steps % together, steps):
         top_down[...] += top_row(jnp.int32(step))
     matrix = inverse_ref[...]
-    rows = half_y * group
-    top_local = dot_split_nt(top_down[:rows] + top_down[rows:], matrix)
+    top_local = dot_split_nt(top_down[...], matrix)
     lay_surface(surface, cols_ref)
     down[...] = down_ref[...]
     for a in range(2):
@@ -743,6 +750,19 @@
         part = 0.5 * dot_split_nt(down[:, e * LANES : (e + 1) * LANES], matrix)
         local[e] = part.reshape(3, size_x, size_y, LANES)
 
+    level = lax.broadcasted_iota(jnp.int32, (16, LANES), 0) // 3
+    kind = lax.broadcasted_iota(jnp.int32, (16, LANES), 0) % 3
+    patterns = []
+    for half in range(2):
+        x = 1.5 * point[0]
+        y = 1.5 * point[1]
+        z = 1.5 * point[2] + (half - 0.5)
+        pattern = jnp.where(level == 0, 1.0, 0.0)
+        for power, value in enumerate((x, y, z, x * x + y * y + z * z)):
+            value = jnp.broadcast_to(value, (16, LANES))
+            pattern = jnp.where(level == power + 1, value, pattern)
+        patterns.append(pattern)
+
     def one_column(index):
         i = index // size_y
         j = index % size_y
@@ -754,11 +774,11 @@
             place = [row[axis][:, lanes] for axis in range(3)]
             inverse = lax.rsqrt(surface_distance(surface, place))
             high, low = split(inverse * inverse * inverse)
-            charge = jnp.concatenate(
-                [local[half, c, i, pl.ds(j, 1), :] for c in range(3)], axis=0
-            )
-            weight = pattern_ref[half] * jnp.concatenate(
-                [charge] * 5 + [jnp.zeros((1, LANES), F32)], axis=0
+            charge = [
+                jnp.broadcast_to(local[half, c, i, pl.ds(j, 1), :], (16, LANES)) for c in range(3)
+            ]
+            weight = patterns[half] * jnp.where(
+                kind == 0, charge[0], jnp.where(kind == 1, charge[1], charge[2])
             )
             total = bdot(two_terms(*split(weight)), jnp.concatenate([high, low], axis=0))
             total = total[:16] + total[16:] + near_ref[index, :, lanes]
@@ -801,9 +821,9 @@
     return lax.ppermute(array, axis, [((i + step) % count, i) for i in range(count)])
 
 
-def widened(blocks, away, axis, name):
-    count = lax.axis_size(name)
+def widening(away, axis, count):
     half = 1
+    plan = []
     while 2 * half + 1 < count:
         missing = count - 2 * half - 1
         if missing <= 2 * half + 1:
@@ -813,24 +833,48 @@
             first = -half
             missing = 2 * half + 1
             steps = (missing, -missing)
+        picks = []
+        known = []
+        for places in away:
+            pick = [k for k, place in enumerate(places) if 0 <= place[axis] - first < missing]
+            picks.append(pick)
+            known += [places[k] for k in pick]
+        plan.append((steps, picks))
+        for step in steps:
+            away = away + [
+                [tuple(p + step * (k == axis) for k, p in enumerate(place)) for place in known]
+            ]
+        half = half + steps[0] if len(steps) == 2 else count
+    return plan, away
+
+
+ROUND = [[(x, y) for x in (-1, 0, 1)] for y in (-1, 0, 1)]
+
+
+def top_slots(lanes_x, lanes_y):
+    _, away = widening(ROUND, 1, lanes_y)
+    _, away = widening(away, 0, lanes_x)
+    slots = np.zeros((lanes_x, lanes_y), np.int32)
+    places = [place for held in away for place in held]
+    for slot, (x, y) in reversed(list(enumerate(places))):
+        slots[x % lanes_x, y % lanes_y] = slot
+    return slots
+
+
+def widened(blocks, away, axis, name):
+    plan, final = widening(away, axis, lax.axis_size(name))
+    for steps, picks in plan:
         sent = []
-        known = []
-        for array, places in zip(blocks, away):
-            pick = [k for k, place in enumerate(places) if 0 <= place[axis] - first < missing]
-            known += [places[k] for k in pick]
+        for array, places, pick in zip(blocks, away, picks):
             if len(pick) == len(places):
                 sent.append(array)
             else:
                 size = array.shape[0] // len(places)
                 sent += [array[k * size : (k + 1) * size] for k in pick]
         whole = sent[0] if len(sent) == 1 else jnp.concatenate(sent, axis=0)
-        for step in steps:
-            blocks = blocks + [moved(whole, name, step)]
-            away = away + [
-                [tuple(p + step * (k == axis) for k, p in enumerate(place)) for place in known]
-            ]
-        half = half + steps[0] if len(steps) == 2 else count
-    return blocks, away
+        blocks = blocks + [moved(whole, name, step) for step in steps]
+        away = final[: len(blocks)]
+    return blocks, final
 
 
 def body(offsets, strengths, counts, check_inverse):
@@ -844,15 +888,6 @@
     tops_y = lanes_y * half_y
     points = sphere_points(expansion)
     rows = jnp.asarray(np.concatenate([points, np.zeros((5, LANES), np.float32)], axis=0))
-    patterns = np.zeros((2, 16, LANES), np.float32)
-    for half in range(2):
-        lifted = (1.5 * points).astype(np.float32)
-        lifted[2] += half - 0.5
-        factors = [np.ones(LANES), *lifted, np.sum(lifted.astype(np.float64) ** 2, axis=0)]
-        for k in range(5):
-            patterns[half, 3 * k : 3 * k + 3, :] = factors[k]
-    patterns = jnp.asarray(patterns)
-
     def params(mebibytes):
         return pltpu.CompilerParams(vmem_limit_bytes=mebibytes * 2**20)
 
@@ -893,7 +928,10 @@
     below = moved(to_above, "gx", -1)
     above = moved(to_below, "gx", 1)
 
-    (own_table, own_tasks), *beside = near_tables(size_x, size_y)
+    table, (own_tasks, *beside) = near_tables(size_x, size_y)
+    slots_at = len(table)
+    slots = top_slots(lanes_x, lanes_y)
+    table = jnp.asarray(np.concatenate([table, slots.reshape(-1)]))
     near_shape = jax.ShapeDtypeStruct((size_x * size_y, 16, 2 * LANES), F32)
     own = pl.pallas_call(
         functools.partial(own_kernel, size_x, size_y, own_tasks),
@@ -907,7 +945,7 @@
         compiler_params=params(28),
         cost_estimate=cost(3 * 10**10),
         name="own",
-    )(jnp.asarray(own_table), pack)
+    )(table, pack)
 
     to_low, to_high, tops = pl.pallas_call(
         functools.partial(turn_kernel, size_x, size_y),
@@ -926,13 +964,13 @@
     high = moved(to_low, "gy", 1)
     blocks, away = widened(
         [low[near_y:], tops, high[near_y:]],
-        [[(x, y) for x in (-1, 0, 1)] for y in (-1, 0, 1)],
+        ROUND,
         1,
         "gy",
     )
 
     def beside_near(axis, before, parcels):
-        table, tasks = beside[0 if axis == "gx" else 1]
+        tasks = beside[0 if axis == "gx" else 1]
         columns = 2 * (size_y if axis == "gx" else size_x + 2)
         return pl.pallas_call(
             functools.partial(halo_kernel, size_x, size_y, axis, tasks),
@@ -947,15 +985,11 @@
             compiler_params=params(20),
             cost_estimate=cost(10**10),
             name="beside_" + axis,
-        )(jnp.asarray(table), before, pack, *parcels)
+        )(table, before, pack, *parcels)
 
     near = beside_near("gx", own, (below, above))
     blocks, away = widened(blocks, away, 0, "gx")
-    away = [place for places in away for place in places]
-    blocks = jnp.concatenate(blocks, axis=0).reshape(len(away), top_rows, LANES)
-    slots = np.zeros((lanes_x, lanes_y), np.int32)
-    for slot, (x, y) in reversed(list(enumerate(away))):
-        slots[x % lanes_x, y % lanes_y] = slot
+    blocks = jnp.concatenate(blocks, axis=0).reshape(-1, top_rows, LANES)
     near = beside_near("gy", near, (low, high))
 
     down = pl.pallas_call(
@@ -980,15 +1014,15 @@
     parts = -(-along // 20)
     chunk = -(-along // parts)
     return pl.pallas_call(
-        functools.partial(far_kernel, size_x, size_y, tops_x, tops_y, chunk),
+        functools.partial(far_kernel, size_x, size_y, tops_x, tops_y, chunk, slots_at),
         out_shape=jax.ShapeDtypeStruct((12, size_x, size_y, depth * LANES), F32),
-        in_specs=[smem] + [vmem] * 8,
+        in_specs=[smem] + [vmem] * 7,
         out_specs=vmem,
         scratch_shapes=[
             pltpu.VMEM((3, LANES, LANES), F32),
             pltpu.VMEM((across, (parts * chunk + half_y - 1) * half_x * 4, LANES), F32),
             pltpu.VMEM((3 * size_x * size_y, 2 * LANES), F32),
-            pltpu.VMEM((2 * half_y * half_x * 4, LANES), F32),
+            pltpu.VMEM((half_y * half_x * 4, LANES), F32),
             pltpu.VMEM((2, 3, size_x, size_y, LANES), F32),
             pltpu.VMEM((4, LANES, LANES), F32),
             pltpu.VMEM((parts * chunk, LANES, LANES), F32),
@@ -998,14 +1032,13 @@
         cost_estimate=cost(10**10),
         name="far",
     )(
-        jnp.asarray(slots.reshape(-1)),
+        table,
         living,
         down,
         blocks,
         near,
         pack,
         rows,
-        patterns,
         matrix,
     )
 

time: 73.6 us -> 72.6 us (0.986)
    unnamed x22 -> x14, local copies, waits for them, and re-layouts: 4.14 us -> 3.45 us
  transfers between devices with their start and end apart: 7 -> 7, of which waited for: 0 -> 0; matrix products, arithmetic and copies ran while one was open for 0% -> 0% of each run, Pallas kernels for 56% -> 57%
where the time goes in v6:
time: 72.6 us; the launch traced here: 72.3 us
  Pallas kernels  56.2 us (77%)
  starting transfers between devices  12.4 us (17%)
  local copies, waits for them, and re-layouts  3.48 us (5%)
    pallas_call x1, Pallas kernels, body(): pl.pallas_call(functools.partial(own_kernel, size_x, size_y, own_tasks),...  24.6 us
    pallas_call x2, Pallas kernels, beside_near(): pl.pallas_call(functools.partial(halo_kernel, size_x, size_y, axis, tasks...  13.9 us
    ppermute x7, starting transfers between devices, moved(): lax.ppermute(array, axis, [((i + step) % count, i) for i in range(count)])  12.4 us
    pallas_call x1, Pallas kernels, body(): pl.pallas_call(functools.partial(far_kernel, size_x, size_y, tops_x, tops...  10.9 us
    pallas_call x1, Pallas kernels, body(): pl.pallas_call(functools.partial(up_kernel, size_x, size_y), out_shape=(j...  4.08 us
    unnamed x14, local copies, waits for them, and re-layouts  3.45 us
    pallas_call x1, Pallas kernels, body(): pl.pallas_call(functools.partial(leaf_kernel, size_x, size_y), out_shape=...  2.64 us
  transfers between devices with their start and end apart: 7, of which 0 were waited for; matrix products, arithmetic and copies ran while one was open for 0% of the time, Pallas kernels for 57%

profile of v6, /device:TPU:0, one launch (start us, length us, event | category | flops | bytes accessed | tf_op | source)
XLA Modules:
  0.0 72.3 jit_solution(16251035088626419684)
XLA Ops:
  0.0 0.8 %copy.7.counts_ref = s32[4,8,2]{2,1,0:T(8,128)S(1)} copy(s32[4,8,2]{1,2,0:T(2,128)} %param.8) | data formatting | bytes 512 | tf_op args[2]
  0.8 0.9 %copy-done = f32[3,4,8,256]{3,2,1,0:T(8,128)S(1)} copy-done((f32[3,4,8,256]{3,2,1,0:T(8,128)S(1)}, f32[3,4,8,256]{3,2,1,0:T(8,128)}, u32[]{:S(2)}) %copy-start) | copy-done | bytes 98328
  1.7 0.9 %copy-done.1 = f32[3,4,8,256]{3,2,1,0:T(8,128)S(1)} copy-done((f32[3,4,8,256]{3,2,1,0:T(8,128)S(1)}, f32[3,4,8,256]{3,2,1,0:T(8,128)}, u32[]{:S(2)}) %copy-start.1) | copy-done | bytes 98328
  2.6 0.8 %copy-done.2 = f32[121,121]{1,0:T(8,128)S(1)} copy-done((f32[121,121]{1,0:T(8,128)S(1)}, f32[121,121]{1,0:T(8,128)}, u32[]{:S(2)}) %copy-start.2) | copy-done | bytes 58588
  3.4 4.1 %up.1 = (f32[6,4,8,256]{3,2,1,0:T(8,128)S(1)}, f32[2,3,4,8,128]{4,3,2,1,0:T(8,128)S(1)}, f32[24,128]{1,0:T(8,128)S(1)}, f32[128,128]{1,0:T(8,128)S(1)}, f32[4,8,...) custom-call(s32[4,8,2]{2,1,0:T(8,128)S(1)} %copy.7.counts_ref, f32[3,4,8,256]{3,2,1,0:T(8,128)S(1)} %copy-done, ...), custom_call_target="tpu_custom_call" | custom-call | flops 6000000000 | bytes 1000000 | tf_op jit(solution)/shard_map/up/pallas_call | solution.py:903
  7.5 0.0 copy-start.4
  7.5 0.5 collective-permute-start
  8.0 2.9 %collective-permute-start.1 = (f32[264,128]{1,0:T(8,128)S(1)}, f32[264,128]{1,0:T(8,128)S(1)}, u32[]{:S(2)}, u32[]{:S(2)}) collective-permute-start(f32[264,128]{1,0:T(8,128)S(1)} %get-tuple-element.18), channel_id=1, source_target_pairs={{4,0},{8,4},{12,8},{16,12},{20,16},{24,20},{28,24},{0,28},{5,1},{9... | collective-permute-start | bytes 405512 | tf_op jit(solution)/shard_map/ppermute | solution.py:821
  11.0 24.6 %own.1.before_ref = f32[32,16,256]{2,1,0:T(8,128)S(1)} custom-call(s32[724]{0:T(1024)S(1)} %copy-done.4, f32[6,4,8,256]{3,2,1,0:T(8,128)S(1)} %get-tuple-element.19.pack_ref), custom_call_target="tpu_custom_call" | custom-call | flops 30000001024 | bytes 1000000 | tf_op jit(solution)/shard_map/own/pallas_call | solution.py:936
  35.5 0.0 collective-permute-done.below_ref.rest_0_
  35.6 0.0 collective-permute-done.1.above_ref.rest_1_
  35.6 0.1 turn.1
  35.7 3.3 %collective-permute-start.4 = (f32[72,128]{1,0:T(8,128)S(1)}, f32[72,128]{1,0:T(8,128)S(1)}, u32[]{:S(2)}, u32[]{:S(2)}) collective-permute-start(f32[72,128]{1,0:T(8,128)S(1)} %get-tuple-element.23), channel_id=1, source_target_pairs={{2,0},{3,1},{0,2},{1,3},{6,4},{7,5},{4,6},{5,7},{10,8},{11,9},{8,1... | collective-permute-start | bytes 110600 | tf_op jit(solution)/shard_map/ppermute | solution.py:821
  39.0 1.6 %collective-permute-start.2 = (f32[324,128]{1,0:T(8,128)S(1)}, f32[324,128]{1,0:T(8,128)S(1)}, u32[]{:S(2)}, u32[]{:S(2)}) collective-permute-start(f32[324,128]{1,0:T(8,128)S(1)} %get-tuple-element.21), channel_id=1, source_target_pairs={{3,0},{0,1},{1,2},{2,3},{7,4},{4,5},{5,6},{6,7},{11,8},{8,9},{9,10... | collective-permute-start | bytes 497672 | tf_op jit(solution)/shard_map/ppermute | solution.py:821
  40.6 2.2 %collective-permute-start.3 = (f32[324,128]{1,0:T(8,128)S(1)}, f32[324,128]{1,0:T(8,128)S(1)}, u32[]{:S(2)}, u32[]{:S(2)}) collective-permute-start(f32[324,128]{1,0:T(8,128)S(1)} %get-tuple-element.22), channel_id=1, source_target_pairs={{1,0},{2,1},{3,2},{0,3},{5,4},{6,5},{7,6},{4,7},{9,8},{10,9},{11,1... | collective-permute-start | bytes 497672 | tf_op jit(solution)/shard_map/ppermute | solution.py:821
  42.9 8.6 %beside_gx.1.before_ref = f32[32,16,256]{2,1,0:T(8,128)S(1)} custom-call(s32[724]{0:T(1024)S(1)} %copy-done.4, f32[32,16,256]{2,1,0:T(8,128)S(1)} %own.1.before_ref, f32[6,4,8,256]{3,2,1,0:T(8,128)S(1)} %get-tuple-element.19.pack_ref, f32[264,128]{1,0:T(8,128)S(1)} %collective-permute-done.below_ref.rest_0_, ...), custom_call_target="tpu_custom_call" | custom-call | flops 10000000000 | bytes 1000000 | tf_op jit(solution)/shard_map/beside_gx/pallas_call | solution.py:975
  51.4 0.0 collective-permute-done.2.rest_2_.rest_0_
  51.5 0.0 collective-permute-done.3.rest_3_.rest_1_
  51.5 0.0 collective-permute-done.4
  51.5 0.1 collective-permute-start.6
  51.6 1.7 %collective-permute-start.5 = (f32[288,128]{1,0:T(8,128)S(1)}, f32[288,128]{1,0:T(8,128)S(1)}, u32[]{:S(2)}, u32[]{:S(2)}) collective-permute-start(f32[288,128]{1,0:T(8,128)S(1)} %pad_maximum_fusion), channel_id=1, source_target_pairs={{12,0},{16,4},{20,8},{24,12},{28,16},{0,20},{4,24},{8,28},{13,1},{... | collective-permute-start | bytes 442376 | tf_op jit(solution)/shard_map/ppermute | solution.py:821
  53.3 5.4 %beside_gy.1.near_ref = f32[32,16,256]{2,1,0:T(8,128)S(1)} custom-call(s32[724]{0:T(1024)S(1)} %copy-done.4, f32[32,16,256]{2,1,0:T(8,128)S(1)} %beside_gx.1.before_ref, f32[6,4,8,256]{3,2,1,0:T(8,128)S(1)} %get-tuple-element.19.pack_ref, f32[324,128]{1,0:T(8,128)S(1)} %collective-permute-done.2.rest_2_.rest_0_, ...), custom_call_target="tpu_custom_call" | custom-call | flops 10000000000 | bytes 1000000 | tf_op jit(solution)/shard_map/beside_gy/pallas_call | solution.py:975
  58.7 2.6 %leaf.1.down_ref = f32[96,256]{1,0:T(8,128)S(1)} custom-call(f32[2,3,4,8,128]{4,3,2,1,0:T(8,128)S(1)} %get-tuple-element.16.leaf_ref.own_ref, f32[8,128]{1,0:T(8,128)S(1)} %copy-done.3, f32[264,128]{1,0:T(8,128)S(1)} %collective-permute-done.below_ref.rest_0_, f32[264,128]{1,0:T(8,128)S(1)} %collective-permute-done.1.above_ref.rest_1_, ...), custom_call_target="tpu_custom_call" | custom-call | flops 6000000000 | bytes 1000000 | tf_op jit(solution)/shard_map/leaf/pallas_call | solution.py:995
  61.4 10.9 %far.1 = f32[12,4,8,256]{3,2,1,0:T(8,128)} custom-call(s32[724]{0:T(1024)S(1)} %copy-done.4, f32[4,8,256]{2,1,0:T(8,128)S(1)} %get-tuple-element.15.living_ref, f32[96,256]{1,0:T(8,128)S(1)} %leaf.1.down_ref, f32[36,24,128]{2,1,0:T(8,128)S(1)} %bitcast.1, f32[32,16,256]{2,1,0:T(8,128)S(1)} %beside_gy.1.near_ref, ...), custom_call_target="tpu_custom_call" | custom-call | flops 10000000000 | bytes 1000000 | tf_op jit(solution)/shard_map/far/pallas_call | solution.py:1016
  (15 shorter events, 0.1 us)
Async XLA Ops:
  0.0 0.8 %copy-start.3 = (f32[8,128]{1,0:T(8,128)S(1)}, f32[8,128]{1,0:T(8,128)}, u32[]{:S(2)}) copy-start(f32[8,128]{1,0:T(8,128)} %constant.4.clone.rows_ref) | copy-start | bytes 12292
  0.8 0.9 %copy-start = (f32[3,4,8,256]{3,2,1,0:T(8,128)S(1)}, f32[3,4,8,256]{3,2,1,0:T(8,128)}, u32[]{:S(2)}) copy-start(f32[3,4,8,256]{3,2,1,0:T(8,128)} %offsets_ref.1) | copy-start | bytes 294916
  1.7 0.9 %copy-start.1 = (f32[3,4,8,256]{3,2,1,0:T(8,128)S(1)}, f32[3,4,8,256]{3,2,1,0:T(8,128)}, u32[]{:S(2)}) copy-start(f32[3,4,8,256]{3,2,1,0:T(8,128)} %strengths_ref.1) | copy-start | bytes 294916
  2.6 0.8 %copy-start.2 = (f32[121,121]{1,0:T(8,128)S(1)}, f32[121,121]{1,0:T(8,128)}, u32[]{:S(2)}) copy-start(f32[121,121]{1,0:T(8,128)} %inverse_ref.1) | copy-start | bytes 175696
  7.5 3.5 %copy-start.4 = (s32[724]{0:T(1024)S(1)}, s32[724]{0:T(1024)}, u32[]{:S(2)}) copy-start(s32[724]{0:T(1024)} %constant.5.clone.table_ref.slot_ref) | copy-start | bytes 8692
  7.5 28.0 %collective-permute-start = (f32[264,128]{1,0:T(8,128)S(1)}, f32[264,128]{1,0:T(8,128)S(1)}, u32[]{:S(2)}, u32[]{:S(2)}) collective-permute-start(f32[264,128]{1,0:T(8,128)S(1)} %get-tuple-element.17), channel_id=1, source_target_pairs={{28,0},{0,4},{4,8},{8,12},{12,16},{16,20},{20,24},{24,28},{29,1},{... | collective-permute-start | bytes 405512 | tf_op jit(solution)/shard_map/ppermute | solution.py:821
  8.0 27.5 %collective-permute-start.1 = (f32[264,128]{1,0:T(8,128)S(1)}, f32[264,128]{1,0:T(8,128)S(1)}, u32[]{:S(2)}, u32[]{:S(2)}) collective-permute-start(f32[264,128]{1,0:T(8,128)S(1)} %get-tuple-element.18), channel_id=1, source_target_pairs={{4,0},{8,4},{12,8},{16,12},{20,16},{24,20},{28,24},{0,28},{5,1},{9... | collective-permute-start | bytes 405512 | tf_op jit(solution)/shard_map/ppermute | solution.py:821
  35.7 15.8 %collective-permute-start.4 = (f32[72,128]{1,0:T(8,128)S(1)}, f32[72,128]{1,0:T(8,128)S(1)}, u32[]{:S(2)}, u32[]{:S(2)}) collective-permute-start(f32[72,128]{1,0:T(8,128)S(1)} %get-tuple-element.23), channel_id=1, source_target_pairs={{2,0},{3,1},{0,2},{1,3},{6,4},{7,5},{4,6},{5,7},{10,8},{11,9},{8,1... | collective-permute-start | bytes 110600 | tf_op jit(solution)/shard_map/ppermute | solution.py:821
  39.0 12.4 %collective-permute-start.2 = (f32[324,128]{1,0:T(8,128)S(1)}, f32[324,128]{1,0:T(8,128)S(1)}, u32[]{:S(2)}, u32[]{:S(2)}) collective-permute-start(f32[324,128]{1,0:T(8,128)S(1)} %get-tuple-element.21), channel_id=1, source_target_pairs={{3,0},{0,1},{1,2},{2,3},{7,4},{4,5},{5,6},{6,7},{11,8},{8,9},{9,10... | collective-permute-start | bytes 497672 | tf_op jit(solution)/shard_map/ppermute | solution.py:821
  40.6 10.9 %collective-permute-start.3 = (f32[324,128]{1,0:T(8,128)S(1)}, f32[324,128]{1,0:T(8,128)S(1)}, u32[]{:S(2)}, u32[]{:S(2)}) collective-permute-start(f32[324,128]{1,0:T(8,128)S(1)} %get-tuple-element.22), channel_id=1, source_target_pairs={{1,0},{2,1},{3,2},{0,3},{5,4},{6,5},{7,6},{4,7},{9,8},{10,9},{11,1... | collective-permute-start | bytes 497672 | tf_op jit(solution)/shard_map/ppermute | solution.py:821
  51.5 9.8 %collective-permute-start.6 = (f32[288,128]{1,0:T(8,128)S(1)}, f32[288,128]{1,0:T(8,128)S(1)}, u32[]{:S(2)}, u32[]{:S(2)}) collective-permute-start(f32[288,128]{1,0:T(8,128)S(1)} %pad_maximum_fusion), channel_id=1, source_target_pairs={{20,0},{24,4},{28,8},{0,12},{4,16},{8,20},{12,24},{16,28},{21,1},{... | collective-permute-start | bytes 442376 | tf_op jit(solution)/shard_map/ppermute | solution.py:821
  51.6 9.8 %collective-permute-start.5 = (f32[288,128]{1,0:T(8,128)S(1)}, f32[288,128]{1,0:T(8,128)S(1)}, u32[]{:S(2)}, u32[]{:S(2)}) collective-permute-start(f32[288,128]{1,0:T(8,128)S(1)} %pad_maximum_fusion), channel_id=1, source_target_pairs={{12,0},{16,4},{20,8},{24,12},{28,16},{0,20},{4,24},{8,28},{13,1},{... | collective-permute-start | bytes 442376 | tf_op jit(solution)/shard_map/ppermute | solution.py:821

commit v7 on v6

--- a/solution.py
+++ b/solution.py
@@ -130,56 +130,29 @@
 def up_kernel(
     size_x,
     size_y,
-    counts_ref,
+    living_ref,
     offsets_ref,
     strengths_ref,
     rows_ref,
-    inverse_ref,
+    matrix_ref,
     pack_ref,
     leaf_ref,
     top_ref,
-    matrix_ref,
-    living_ref,
     *rest,
 ):
     parcels = rest[:2]
-    check, surface, cols_ref, strong, inverse, arrived = rest[2:]
-    copies = [
-        pltpu.make_async_copy(source, target, arrived.at[k])
-        for k, (source, target) in enumerate(
-            (
-                (offsets_ref, pack_ref.at[0:3]),
-                (strengths_ref, strong),
-                (inverse_ref, inverse),
-            )
-        )
-    ]
-    for copy in copies:
-        copy.start()
+    check, surface, cols_ref = rest[2:]
     lay_points(cols_ref, rows_ref)
     lay_surface(surface, cols_ref)
-    for copy in copies:
-        copy.wait()
     point = [rows_ref[j : j + 1, :] for j in range(3)]
-    lane = lax.broadcasted_iota(jnp.int32, (1, LANES), 1)
-    expansion = inverse_ref.shape[0]
-    matrix_ref[...] = jnp.zeros_like(matrix_ref)
-    matrix_ref[:expansion, :expansion] = inverse[...]
+    pack_ref[0:3] = offsets_ref[...]
 
     def one_column(i, j):
-        row = [pack_ref[c, i, pl.ds(j, 1), :] for c in range(3)]
-        count = counts_ref[i, pl.ds(j, 1), :]
-        living = jnp.concatenate(
-            [
-                jnp.where(lane < jnp.broadcast_to(count[:, k : k + 1], (1, LANES)), 1.0, 0.0)
-                for k in range(2)
-            ],
-            axis=1,
-        )
-        living_ref[i, pl.ds(j, 1), :] = living
+        row = [offsets_ref[c, i, pl.ds(j, 1), :] for c in range(3)]
+        living = living_ref[i, pl.ds(j, 1), :]
         charges = []
         for c in range(3):
-            value = STRENGTH_SCALE * strong[c, i, pl.ds(j, 1), :] * living
+            value = STRENGTH_SCALE * strengths_ref[c, i, pl.ds(j, 1), :] * living
             pack_ref[3 + c, i, pl.ds(j, 1), :] = value
             charges.append(value)
         charge = jnp.concatenate(charges + [jnp.zeros((5, 2 * LANES), F32)], axis=0)
@@ -387,7 +360,7 @@
 def run_tasks(size_y, tasks, table_ref, pack_ref, out_ref, lift, spread, moments, adds):
     for start, amount, sources in tasks:
         together = 1
-        while together * sources < 12 and amount % (2 * together) == 0:
+        while together * sources < 24 and amount % (2 * together) == 0:
             together *= 2
 
         def one(index, start, sources):
@@ -893,12 +866,15 @@
 
     smem = pl.BlockSpec(memory_space=pltpu.SMEM)
     vmem = pl.BlockSpec(memory_space=pltpu.VMEM)
-    hbm = pl.BlockSpec(memory_space=pltpu.HBM)
 
     def cost(flops):
         return pl.CostEstimate(flops=flops, bytes_accessed=10**6, transcendentals=0)
 
     top_rows = 3 * half_x * half_y
+    slot = jnp.arange(LANES)
+    living = (slot < counts[:, :, :, None]).astype(F32).reshape(size_x, size_y, depth * LANES)
+    pad = LANES - expansion
+    matrix = jnp.pad(check_inverse, ((0, pad), (0, pad)))
     (_, _, end_x), (_, near_y, end_y) = parcel_rows(size_x, size_y)
     made = pl.pallas_call(
         functools.partial(up_kernel, size_x, size_y),
@@ -906,25 +882,20 @@
             jax.ShapeDtypeStruct((6, size_x, size_y, depth * LANES), F32),
             jax.ShapeDtypeStruct((2, 3, size_x, size_y, LANES), F32),
             jax.ShapeDtypeStruct((top_rows, LANES), F32),
-            jax.ShapeDtypeStruct((LANES, LANES), F32),
-            jax.ShapeDtypeStruct((size_x, size_y, depth * LANES), F32),
             *[jax.ShapeDtypeStruct((end_x, LANES), F32)] * 2,
         ),
-        in_specs=[vmem, hbm, hbm, vmem, hbm],
-        out_specs=(vmem,) * 7,
+        in_specs=[vmem] * 5,
+        out_specs=(vmem,) * 5,
         scratch_shapes=[
             pltpu.VMEM((2, 3, size_x, size_y, LANES), F32),
             pltpu.VMEM((4, LANES, LANES), F32),
             pltpu.VMEM((3, LANES, LANES), F32),
-            pltpu.VMEM(strengths.shape, F32),
-            pltpu.VMEM(check_inverse.shape, F32),
-            pltpu.SemaphoreType.DMA((3,)),
         ],
         compiler_params=params(12),
         cost_estimate=cost(6 * 10**9),
         name="up",
-    )(counts, offsets, strengths, rows, check_inverse)
-    pack, leaf_charges, top_charges, matrix, living, to_below, to_above = made
+    )(living, offsets, strengths, rows, matrix)
+    pack, leaf_charges, top_charges, to_below, to_above = made
     below = moved(to_above, "gx", -1)
     above = moved(to_below, "gx", 1)
 

time: 72.6 us -> 70.9 us (0.977)
  local copies, waits for them, and re-layouts: 3.48 us -> 1.81 us
  other arithmetic: 0.01 us -> 0.81 us
    unnamed x14 -> x11, local copies, waits for them, and re-layouts: 3.45 us -> 0.92 us
    pad x0 -> x1, local copies, waits for them, and re-layouts: none -> 0.85 us  [body(): matrix = jnp.pad(check_inverse, ((0, pad), (0, pad)))]
    convert_element_type x0 -> x1, other arithmetic: none -> 0.79 us  [body(): (slot < counts[:, :, :, None]).astype(F32)]
  transfers between devices with their start and end apart: 7 -> 7, of which waited for: 0 -> 0; matrix products, arithmetic and copies ran while one was open for 0% -> 0% of each run, Pallas kernels for 57% -> 58%
where the time goes in v7:
time: 70.9 us; the launch traced here: 70.7 us
  Pallas kernels  55.5 us (78%)
  starting transfers between devices  12.4 us (17%)
  local copies, waits for them, and re-layouts  1.81 us (3%)
  other arithmetic  0.81 us (1%)
    pallas_call x1, Pallas kernels, body(): pl.pallas_call(functools.partial(own_kernel, size_x, size_y, own_tasks),...  24.5 us
    pallas_call x2, Pallas kernels, beside_near(): pl.pallas_call(functools.partial(halo_kernel, size_x, size_y, axis, tasks...  13.8 us
    ppermute x7, starting transfers between devices, moved(): lax.ppermute(array, axis, [((i + step) % count, i) for i in range(count)])  12.4 us
    pallas_call x1, Pallas kernels, body(): pl.pallas_call(functools.partial(far_kernel, size_x, size_y, tops_x, tops...  10.9 us
    pallas_call x1, Pallas kernels, body(): pl.pallas_call(functools.partial(up_kernel, size_x, size_y), out_shape=(j...  3.45 us
    pallas_call x1, Pallas kernels, body(): pl.pallas_call(functools.partial(leaf_kernel, size_x, size_y), out_shape=...  2.64 us
  transfers between devices with their start and end apart: 7, of which 0 were waited for; matrix products, arithmetic and copies ran while one was open for 0% of the time, Pallas kernels for 58%

profile of v7, /device:TPU:0, one launch (start us, length us, event | category | flops | bytes accessed | tf_op | source)
XLA Modules:
  0.0 70.7 jit_solution(4375477228725874618)
XLA Ops:
  0.0 0.8 %fusion.living_ref = f32[4,8,256]{2,1,0:T(8,128)S(1)} fusion(s32[4,8,2]{1,2,0:T(2,128)} %param.8, s32[256]{0:T(256)S(1)} %iota_bitcast_fusion), kind=kLoop, calls=%fused_computation.2 | loop fusion | flops 16384 | bytes 34048 | tf_op jit(solution)/shard_map/convert_element_type | solution.py:875
  0.8 0.0 copy-start.2
  0.8 0.9 %pad.4.matrix_ref.inverse_ref = f32[128,128]{1,0:T(8,128)S(1)} pad(f32[121,121]{1,0:T(8,128)} %param.9, f32[]{:T(128)} %constant.6.clone.1), padding=0_7x0_7 | pad | bytes 124104 | tf_op jit(solution)/shard_map/jit(_pad)/pad | solution.py:877
  1.7 0.0 copy-start.1
  1.7 0.9 %copy-done.1 = f32[3,4,8,256]{3,2,1,0:T(8,128)S(1)} copy-done((f32[3,4,8,256]{3,2,1,0:T(8,128)S(1)}, f32[3,4,8,256]{3,2,1,0:T(8,128)}, u32[]{:S(2)}) %copy-start.1) | copy-done | bytes 98328
  2.6 3.5 %up.1 = (f32[6,4,8,256]{3,2,1,0:T(8,128)S(1)}, f32[2,3,4,8,128]{4,3,2,1,0:T(8,128)S(1)}, f32[24,128]{1,0:T(8,128)S(1)}, f32[264,128]{1,0:T(8,128)S(1)}, f32[264,128]{1,0:T(8,128)S(1)}) custom-call(f32[4,8,256]{2,1,0:T(8,128)S(1)} %fusion.living_ref, f32[3,4,8,256]{3,2,1,0:T(8,128)S(1)} %copy-done, f32[3,4,8,256]{3,2,1,0:T(8,128)S(1)} %copy-done.1, ...), custom_call_target="tpu_custom_call" | custom-call | flops 6000000000 | bytes 1000000 | tf_op jit(solution)/shard_map/up/pallas_call | solution.py:879
  6.0 0.5 collective-permute-start
  6.5 2.9 %collective-permute-start.1 = (f32[264,128]{1,0:T(8,128)S(1)}, f32[264,128]{1,0:T(8,128)S(1)}, u32[]{:S(2)}, u32[]{:S(2)}) collective-permute-start(f32[264,128]{1,0:T(8,128)S(1)} %get-tuple-element.15), channel_id=1, source_target_pairs={{4,0},{8,4},{12,8},{16,12},{20,16},{24,20},{28,24},{0,28},{5,1},{9... | collective-permute-start | bytes 405512 | tf_op jit(solution)/shard_map/ppermute | solution.py:794
  9.4 24.5 %own.1.before_ref = f32[32,16,256]{2,1,0:T(8,128)S(1)} custom-call(s32[724]{0:T(1024)S(1)} %copy-done.3, f32[6,4,8,256]{3,2,1,0:T(8,128)S(1)} %get-tuple-element.16.pack_ref), custom_call_target="tpu_custom_call" | custom-call | flops 30000001024 | bytes 1000000 | tf_op jit(solution)/shard_map/own/pallas_call | solution.py:907
  34.0 0.0 collective-permute-done.below_ref.rest_0_
  34.0 0.0 collective-permute-done.1.above_ref.rest_1_
  34.0 0.1 turn.1
  34.1 3.4 %collective-permute-start.4 = (f32[72,128]{1,0:T(8,128)S(1)}, f32[72,128]{1,0:T(8,128)S(1)}, u32[]{:S(2)}, u32[]{:S(2)}) collective-permute-start(f32[72,128]{1,0:T(8,128)S(1)} %get-tuple-element.20), channel_id=1, source_target_pairs={{2,0},{3,1},{0,2},{1,3},{6,4},{7,5},{4,6},{5,7},{10,8},{11,9},{8,1... | collective-permute-start | bytes 110600 | tf_op jit(solution)/shard_map/ppermute | solution.py:794
  37.5 1.6 %collective-permute-start.2 = (f32[324,128]{1,0:T(8,128)S(1)}, f32[324,128]{1,0:T(8,128)S(1)}, u32[]{:S(2)}, u32[]{:S(2)}) collective-permute-start(f32[324,128]{1,0:T(8,128)S(1)} %get-tuple-element.18), channel_id=1, source_target_pairs={{3,0},{0,1},{1,2},{2,3},{7,4},{4,5},{5,6},{6,7},{11,8},{8,9},{9,10... | collective-permute-start | bytes 497672 | tf_op jit(solution)/shard_map/ppermute | solution.py:794
  39.1 2.2 %collective-permute-start.3 = (f32[324,128]{1,0:T(8,128)S(1)}, f32[324,128]{1,0:T(8,128)S(1)}, u32[]{:S(2)}, u32[]{:S(2)}) collective-permute-start(f32[324,128]{1,0:T(8,128)S(1)} %get-tuple-element.19), channel_id=1, source_target_pairs={{1,0},{2,1},{3,2},{0,3},{5,4},{6,5},{7,6},{4,7},{9,8},{10,9},{11,1... | collective-permute-start | bytes 497672 | tf_op jit(solution)/shard_map/ppermute | solution.py:794
  41.3 8.6 %beside_gx.1.before_ref = f32[32,16,256]{2,1,0:T(8,128)S(1)} custom-call(s32[724]{0:T(1024)S(1)} %copy-done.3, f32[32,16,256]{2,1,0:T(8,128)S(1)} %own.1.before_ref, f32[6,4,8,256]{3,2,1,0:T(8,128)S(1)} %get-tuple-element.16.pack_ref, f32[264,128]{1,0:T(8,128)S(1)} %collective-permute-done.below_ref.rest_0_, ...), custom_call_target="tpu_custom_call" | custom-call | flops 10000000000 | bytes 1000000 | tf_op jit(solution)/shard_map/beside_gx/pallas_call | solution.py:946
  49.9 0.0 collective-permute-done.2.rest_2_.rest_0_
  49.9 0.0 collective-permute-done.3.rest_3_.rest_1_
  50.0 0.1 collective-permute-start.6
  50.1 1.7 %collective-permute-start.5 = (f32[288,128]{1,0:T(8,128)S(1)}, f32[288,128]{1,0:T(8,128)S(1)}, u32[]{:S(2)}, u32[]{:S(2)}) collective-permute-start(f32[288,128]{1,0:T(8,128)S(1)} %pad_maximum_fusion), channel_id=1, source_target_pairs={{12,0},{16,4},{20,8},{24,12},{28,16},{0,20},{4,24},{8,28},{13,1},{... | collective-permute-start | bytes 442376 | tf_op jit(solution)/shard_map/ppermute | solution.py:794
  51.8 5.3 %beside_gy.1.near_ref = f32[32,16,256]{2,1,0:T(8,128)S(1)} custom-call(s32[724]{0:T(1024)S(1)} %copy-done.3, f32[32,16,256]{2,1,0:T(8,128)S(1)} %beside_gx.1.before_ref, f32[6,4,8,256]{3,2,1,0:T(8,128)S(1)} %get-tuple-element.16.pack_ref, f32[324,128]{1,0:T(8,128)S(1)} %collective-permute-done.2.rest_2_.rest_0_, ...), custom_call_target="tpu_custom_call" | custom-call | flops 10000000000 | bytes 1000000 | tf_op jit(solution)/shard_map/beside_gy/pallas_call | solution.py:946
  57.1 2.6 %leaf.1.down_ref = f32[96,256]{1,0:T(8,128)S(1)} custom-call(f32[2,3,4,8,128]{4,3,2,1,0:T(8,128)S(1)} %get-tuple-element.13.leaf_ref.own_ref, f32[8,128]{1,0:T(8,128)S(1)} %copy-done.2, f32[264,128]{1,0:T(8,128)S(1)} %collective-permute-done.below_ref.rest_0_, f32[264,128]{1,0:T(8,128)S(1)} %collective-permute-done.1.above_ref.rest_1_, ...), custom_call_target="tpu_custom_call" | custom-call | flops 6000000000 | bytes 1000000 | tf_op jit(solution)/shard_map/leaf/pallas_call | solution.py:966
  59.7 0.0 collective-permute-done.5
  59.8 10.9 %far.1 = f32[12,4,8,256]{3,2,1,0:T(8,128)} custom-call(s32[724]{0:T(1024)S(1)} %copy-done.3, f32[4,8,256]{2,1,0:T(8,128)S(1)} %fusion.living_ref, f32[96,256]{1,0:T(8,128)S(1)} %leaf.1.down_ref, f32[36,24,128]{2,1,0:T(8,128)S(1)} %bitcast.7, f32[32,16,256]{2,1,0:T(8,128)S(1)} %beside_gy.1.near_ref, f32[6,4,8,256]{3,2,1,0:T(8,128)S(1)} %get-tuple-element.16.pack_ref, ...), custom_call_target="tpu_custom_call" | custom-call | flops 10000000000 | bytes 1000000 | tf_op jit(solution)/shard_map/far/pallas_call | solution.py:987
  (15 shorter events, 0.1 us)
Async XLA Ops:
  0.0 1.7 %copy-start = (f32[3,4,8,256]{3,2,1,0:T(8,128)S(1)}, f32[3,4,8,256]{3,2,1,0:T(8,128)}, u32[]{:S(2)}) copy-start(f32[3,4,8,256]{3,2,1,0:T(8,128)} %offsets_ref.1) | copy-start | bytes 294916
  0.8 0.9 %copy-start.2 = (f32[8,128]{1,0:T(8,128)S(1)}, f32[8,128]{1,0:T(8,128)}, u32[]{:S(2)}) copy-start(f32[8,128]{1,0:T(8,128)} %constant.7.clone.rows_ref) | copy-start | bytes 12292
  1.7 0.9 %copy-start.1 = (f32[3,4,8,256]{3,2,1,0:T(8,128)S(1)}, f32[3,4,8,256]{3,2,1,0:T(8,128)}, u32[]{:S(2)}) copy-start(f32[3,4,8,256]{3,2,1,0:T(8,128)} %strengths_ref.1) | copy-start | bytes 294916
  6.0 3.4 %copy-start.3 = (s32[724]{0:T(1024)S(1)}, s32[724]{0:T(1024)}, u32[]{:S(2)}) copy-start(s32[724]{0:T(1024)} %constant.8.clone.table_ref.slot_ref) | copy-start | bytes 8692
  6.0 28.0 %collective-permute-start = (f32[264,128]{1,0:T(8,128)S(1)}, f32[264,128]{1,0:T(8,128)S(1)}, u32[]{:S(2)}, u32[]{:S(2)}) collective-permute-start(f32[264,128]{1,0:T(8,128)S(1)} %get-tuple-element.14), channel_id=1, source_target_pairs={{28,0},{0,4},{4,8},{8,12},{12,16},{16,20},{20,24},{24,28},{29,1},{... | collective-permute-start | bytes 405512 | tf_op jit(solution)/shard_map/ppermute | solution.py:794
  6.5 27.5 %collective-permute-start.1 = (f32[264,128]{1,0:T(8,128)S(1)}, f32[264,128]{1,0:T(8,128)S(1)}, u32[]{:S(2)}, u32[]{:S(2)}) collective-permute-start(f32[264,128]{1,0:T(8,128)S(1)} %get-tuple-element.15), channel_id=1, source_target_pairs={{4,0},{8,4},{12,8},{16,12},{20,16},{24,20},{28,24},{0,28},{5,1},{9... | collective-permute-start | bytes 405512 | tf_op jit(solution)/shard_map/ppermute | solution.py:794
  34.1 15.8 %collective-permute-start.4 = (f32[72,128]{1,0:T(8,128)S(1)}, f32[72,128]{1,0:T(8,128)S(1)}, u32[]{:S(2)}, u32[]{:S(2)}) collective-permute-start(f32[72,128]{1,0:T(8,128)S(1)} %get-tuple-element.20), channel_id=1, source_target_pairs={{2,0},{3,1},{0,2},{1,3},{6,4},{7,5},{4,6},{5,7},{10,8},{11,9},{8,1... | collective-permute-start | bytes 110600 | tf_op jit(solution)/shard_map/ppermute | solution.py:794
  37.5 12.4 %collective-permute-start.2 = (f32[324,128]{1,0:T(8,128)S(1)}, f32[324,128]{1,0:T(8,128)S(1)}, u32[]{:S(2)}, u32[]{:S(2)}) collective-permute-start(f32[324,128]{1,0:T(8,128)S(1)} %get-tuple-element.18), channel_id=1, source_target_pairs={{3,0},{0,1},{1,2},{2,3},{7,4},{4,5},{5,6},{6,7},{11,8},{8,9},{9,10... | collective-permute-start | bytes 497672 | tf_op jit(solution)/shard_map/ppermute | solution.py:794
  39.1 10.9 %collective-permute-start.3 = (f32[324,128]{1,0:T(8,128)S(1)}, f32[324,128]{1,0:T(8,128)S(1)}, u32[]{:S(2)}, u32[]{:S(2)}) collective-permute-start(f32[324,128]{1,0:T(8,128)S(1)} %get-tuple-element.19), channel_id=1, source_target_pairs={{1,0},{2,1},{3,2},{0,3},{5,4},{6,5},{7,6},{4,7},{9,8},{10,9},{11,1... | collective-permute-start | bytes 497672 | tf_op jit(solution)/shard_map/ppermute | solution.py:794
  50.0 9.7 %collective-permute-start.6 = (f32[288,128]{1,0:T(8,128)S(1)}, f32[288,128]{1,0:T(8,128)S(1)}, u32[]{:S(2)}, u32[]{:S(2)}) collective-permute-start(f32[288,128]{1,0:T(8,128)S(1)} %pad_maximum_fusion), channel_id=1, source_target_pairs={{20,0},{24,4},{28,8},{0,12},{4,16},{8,20},{12,24},{16,28},{21,1},{... | collective-permute-start | bytes 442376 | tf_op jit(solution)/shard_map/ppermute | solution.py:794
  50.1 9.6 %collective-permute-start.5 = (f32[288,128]{1,0:T(8,128)S(1)}, f32[288,128]{1,0:T(8,128)S(1)}, u32[]{:S(2)}, u32[]{:S(2)}) collective-permute-start(f32[288,128]{1,0:T(8,128)S(1)} %pad_maximum_fusion), channel_id=1, source_target_pairs={{12,0},{16,4},{20,8},{24,12},{28,16},{0,20},{4,24},{8,28},{13,1},{... | collective-permute-start | bytes 442376 | tf_op jit(solution)/shard_map/ppermute | solution.py:794

commit v8 on v7

--- a/solution.py
+++ b/solution.py
@@ -172,12 +172,12 @@
                 check[half, c, i, pl.ds(j, 1), :] = total[c : c + 1]
 
     def columns(index, carry):
-        for k in range(4):
-            step = index * 4 + k
+        for k in range(8):
+            step = index * 8 + k
             one_column(step // size_y, step % size_y)
         return carry
 
-    lax.fori_loop(0, size_x * size_y // 4, columns, 0)
+    lax.fori_loop(0, size_x * size_y // 8, columns, 0)
     matrix = matrix_ref[...]
     rows = 6 * size_x * size_y
     charges = 0.5 * dot_split_nt(check[...].reshape(rows, LANES), matrix)
@@ -654,7 +654,7 @@
                         ] = row
         return carry
 
-    lax.fori_loop(0, lanes_x * lanes_y, place, 0)
+    lax.fori_loop(0, lanes_x * lanes_y, place, 0, unroll=4)
     first_x = mine_x * half_x
     first_y = mine_y * half_y
     top_down[...] = jnp.zeros_like(top_down)
@@ -782,11 +782,11 @@
                 out_ref[3 + 3 * c + axis, i, pl.ds(j, 1), :] = slopes[axis][c : c + 1]
 
     def columns(index, carry):
-        for k in range(4):
-            one_column(index * 4 + k)
+        for k in range(8):
+            one_column(index * 8 + k)
         return carry
 
-    lax.fori_loop(0, size_x * size_y // 4, columns, 0)
+    lax.fori_loop(0, size_x * size_y // 8, columns, 0)
 
 
 def moved(array, axis, step):

time: 70.9 us -> 69.6 us (0.982)
  Pallas kernels: 55.5 us -> 54.2 us
    pallas_call x1, Pallas kernels: 10.9 us -> 10.1 us  [body(): pl.pallas_call(functools.partial(far_kernel, size_x, size_y, tops_x, tops...]
  transfers between devices with their start and end apart: 7 -> 7, of which waited for: 0 -> 0; matrix products, arithmetic and copies ran while one was open for 0% -> 0% of each run, Pallas kernels for 58% -> 59%
where the time goes in v8:
time: 69.6 us; the launch traced here: 69.4 us
  Pallas kernels  54.2 us (78%)
  starting transfers between devices  12.4 us (18%)
  local copies, waits for them, and re-layouts  1.81 us (3%)
  other arithmetic  0.81 us (1%)
    pallas_call x1, Pallas kernels, body(): pl.pallas_call(functools.partial(own_kernel, size_x, size_y, own_tasks),...  24.5 us
    pallas_call x2, Pallas kernels, beside_near(): pl.pallas_call(functools.partial(halo_kernel, size_x, size_y, axis, tasks...  13.8 us
    ppermute x7, starting transfers between devices, moved(): lax.ppermute(array, axis, [((i + step) % count, i) for i in range(count)])  12.4 us
    pallas_call x1, Pallas kernels, body(): pl.pallas_call(functools.partial(far_kernel, size_x, size_y, tops_x, tops...  10.1 us
    pallas_call x1, Pallas kernels, body(): pl.pallas_call(functools.partial(up_kernel, size_x, size_y), out_shape=(j...  2.94 us
    pallas_call x1, Pallas kernels, body(): pl.pallas_call(functools.partial(leaf_kernel, size_x, size_y), out_shape=...  2.64 us
  transfers between devices with their start and end apart: 7, of which 0 were waited for; matrix products, arithmetic and copies ran while one was open for 0% of the time, Pallas kernels for 59%

profile of v8, /device:TPU:0, one launch (start us, length us, event | category | flops | bytes accessed | tf_op | source)
XLA Modules:
  0.0 69.4 jit_solution(18143883850391364620)
XLA Ops:
  0.0 0.8 %fusion.living_ref = f32[4,8,256]{2,1,0:T(8,128)S(1)} fusion(s32[4,8,2]{1,2,0:T(2,128)} %param.8, s32[256]{0:T(256)S(1)} %iota_bitcast_fusion), kind=kLoop, calls=%fused_computation.2 | loop fusion | flops 16384 | bytes 34048 | tf_op jit(solution)/shard_map/convert_element_type | solution.py:875
  0.8 0.0 copy-start.2
  0.8 0.9 %pad.4.matrix_ref.inverse_ref = f32[128,128]{1,0:T(8,128)S(1)} pad(f32[121,121]{1,0:T(8,128)} %param.9, f32[]{:T(128)} %constant.6.clone.1), padding=0_7x0_7 | pad | bytes 124104 | tf_op jit(solution)/shard_map/jit(_pad)/pad | solution.py:877
  1.7 0.0 copy-start.1
  1.7 0.9 %copy-done.1 = f32[3,4,8,256]{3,2,1,0:T(8,128)S(1)} copy-done((f32[3,4,8,256]{3,2,1,0:T(8,128)S(1)}, f32[3,4,8,256]{3,2,1,0:T(8,128)}, u32[]{:S(2)}) %copy-start.1) | copy-done | bytes 98328
  2.6 2.9 %up.1 = (f32[6,4,8,256]{3,2,1,0:T(8,128)S(1)}, f32[2,3,4,8,128]{4,3,2,1,0:T(8,128)S(1)}, f32[24,128]{1,0:T(8,128)S(1)}, f32[264,128]{1,0:T(8,128)S(1)}, f32[264,128]{1,0:T(8,128)S(1)}) custom-call(f32[4,8,256]{2,1,0:T(8,128)S(1)} %fusion.living_ref, f32[3,4,8,256]{3,2,1,0:T(8,128)S(1)} %copy-done, f32[3,4,8,256]{3,2,1,0:T(8,128)S(1)} %copy-done.1, ...), custom_call_target="tpu_custom_call" | custom-call | flops 6000000000 | bytes 1000000 | tf_op jit(solution)/shard_map/up/pallas_call | solution.py:879
  5.5 0.5 collective-permute-start
  6.0 2.9 %collective-permute-start.1 = (f32[264,128]{1,0:T(8,128)S(1)}, f32[264,128]{1,0:T(8,128)S(1)}, u32[]{:S(2)}, u32[]{:S(2)}) collective-permute-start(f32[264,128]{1,0:T(8,128)S(1)} %get-tuple-element.15), channel_id=1, source_target_pairs={{4,0},{8,4},{12,8},{16,12},{20,16},{24,20},{28,24},{0,28},{5,1},{9... | collective-permute-start | bytes 405512 | tf_op jit(solution)/shard_map/ppermute | solution.py:794
  8.9 24.5 %own.1.before_ref = f32[32,16,256]{2,1,0:T(8,128)S(1)} custom-call(s32[724]{0:T(1024)S(1)} %copy-done.3, f32[6,4,8,256]{3,2,1,0:T(8,128)S(1)} %get-tuple-element.16.pack_ref), custom_call_target="tpu_custom_call" | custom-call | flops 30000001024 | bytes 1000000 | tf_op jit(solution)/shard_map/own/pallas_call | solution.py:907
  33.5 0.0 collective-permute-done.below_ref.rest_0_
  33.5 0.0 collective-permute-done.1.above_ref.rest_1_
  33.5 0.1 turn.1
  33.6 3.4 %collective-permute-start.4 = (f32[72,128]{1,0:T(8,128)S(1)}, f32[72,128]{1,0:T(8,128)S(1)}, u32[]{:S(2)}, u32[]{:S(2)}) collective-permute-start(f32[72,128]{1,0:T(8,128)S(1)} %get-tuple-element.20), channel_id=1, source_target_pairs={{2,0},{3,1},{0,2},{1,3},{6,4},{7,5},{4,6},{5,7},{10,8},{11,9},{8,1... | collective-permute-start | bytes 110600 | tf_op jit(solution)/shard_map/ppermute | solution.py:794
  37.0 1.6 %collective-permute-start.2 = (f32[324,128]{1,0:T(8,128)S(1)}, f32[324,128]{1,0:T(8,128)S(1)}, u32[]{:S(2)}, u32[]{:S(2)}) collective-permute-start(f32[324,128]{1,0:T(8,128)S(1)} %get-tuple-element.18), channel_id=1, source_target_pairs={{3,0},{0,1},{1,2},{2,3},{7,4},{4,5},{5,6},{6,7},{11,8},{8,9},{9,10... | collective-permute-start | bytes 497672 | tf_op jit(solution)/shard_map/ppermute | solution.py:794
  38.6 2.2 %collective-permute-start.3 = (f32[324,128]{1,0:T(8,128)S(1)}, f32[324,128]{1,0:T(8,128)S(1)}, u32[]{:S(2)}, u32[]{:S(2)}) collective-permute-start(f32[324,128]{1,0:T(8,128)S(1)} %get-tuple-element.19), channel_id=1, source_target_pairs={{1,0},{2,1},{3,2},{0,3},{5,4},{6,5},{7,6},{4,7},{9,8},{10,9},{11,1... | collective-permute-start | bytes 497672 | tf_op jit(solution)/shard_map/ppermute | solution.py:794
  40.8 8.6 %beside_gx.1.before_ref = f32[32,16,256]{2,1,0:T(8,128)S(1)} custom-call(s32[724]{0:T(1024)S(1)} %copy-done.3, f32[32,16,256]{2,1,0:T(8,128)S(1)} %own.1.before_ref, f32[6,4,8,256]{3,2,1,0:T(8,128)S(1)} %get-tuple-element.16.pack_ref, f32[264,128]{1,0:T(8,128)S(1)} %collective-permute-done.below_ref.rest_0_, ...), custom_call_target="tpu_custom_call" | custom-call | flops 10000000000 | bytes 1000000 | tf_op jit(solution)/shard_map/beside_gx/pallas_call | solution.py:946
  49.4 0.0 collective-permute-done.2.rest_2_.rest_0_
  49.4 0.0 collective-permute-done.3.rest_3_.rest_1_
  49.5 0.1 collective-permute-start.6
  49.5 1.7 %collective-permute-start.5 = (f32[288,128]{1,0:T(8,128)S(1)}, f32[288,128]{1,0:T(8,128)S(1)}, u32[]{:S(2)}, u32[]{:S(2)}) collective-permute-start(f32[288,128]{1,0:T(8,128)S(1)} %pad_maximum_fusion), channel_id=1, source_target_pairs={{12,0},{16,4},{20,8},{24,12},{28,16},{0,20},{4,24},{8,28},{13,1},{... | collective-permute-start | bytes 442376 | tf_op jit(solution)/shard_map/ppermute | solution.py:794
  51.3 5.3 %beside_gy.1.near_ref = f32[32,16,256]{2,1,0:T(8,128)S(1)} custom-call(s32[724]{0:T(1024)S(1)} %copy-done.3, f32[32,16,256]{2,1,0:T(8,128)S(1)} %beside_gx.1.before_ref, f32[6,4,8,256]{3,2,1,0:T(8,128)S(1)} %get-tuple-element.16.pack_ref, f32[324,128]{1,0:T(8,128)S(1)} %collective-permute-done.2.rest_2_.rest_0_, ...), custom_call_target="tpu_custom_call" | custom-call | flops 10000000000 | bytes 1000000 | tf_op jit(solution)/shard_map/beside_gy/pallas_call | solution.py:946
  56.5 2.6 %leaf.1.down_ref = f32[96,256]{1,0:T(8,128)S(1)} custom-call(f32[2,3,4,8,128]{4,3,2,1,0:T(8,128)S(1)} %get-tuple-element.13.leaf_ref.own_ref, f32[8,128]{1,0:T(8,128)S(1)} %copy-done.2, f32[264,128]{1,0:T(8,128)S(1)} %collective-permute-done.below_ref.rest_0_, f32[264,128]{1,0:T(8,128)S(1)} %collective-permute-done.1.above_ref.rest_1_, ...), custom_call_target="tpu_custom_call" | custom-call | flops 6000000000 | bytes 1000000 | tf_op jit(solution)/shard_map/leaf/pallas_call | solution.py:966
  59.2 0.0 collective-permute-done.6
  59.3 10.1 %far.1 = f32[12,4,8,256]{3,2,1,0:T(8,128)} custom-call(s32[724]{0:T(1024)S(1)} %copy-done.3, f32[4,8,256]{2,1,0:T(8,128)S(1)} %fusion.living_ref, f32[96,256]{1,0:T(8,128)S(1)} %leaf.1.down_ref, f32[36,24,128]{2,1,0:T(8,128)S(1)} %bitcast.7, f32[32,16,256]{2,1,0:T(8,128)S(1)} %beside_gy.1.near_ref, f32[6,4,8,256]{3,2,1,0:T(8,128)S(1)} %get-tuple-element.16.pack_ref, ...), custom_call_target="tpu_custom_call" | custom-call | flops 10000000000 | bytes 1000000 | tf_op jit(solution)/shard_map/far/pallas_call | solution.py:987
  (15 shorter events, 0.1 us)
Async XLA Ops:
  0.0 1.7 %copy-start = (f32[3,4,8,256]{3,2,1,0:T(8,128)S(1)}, f32[3,4,8,256]{3,2,1,0:T(8,128)}, u32[]{:S(2)}) copy-start(f32[3,4,8,256]{3,2,1,0:T(8,128)} %offsets_ref.1) | copy-start | bytes 294916
  0.8 0.9 %copy-start.2 = (f32[8,128]{1,0:T(8,128)S(1)}, f32[8,128]{1,0:T(8,128)}, u32[]{:S(2)}) copy-start(f32[8,128]{1,0:T(8,128)} %constant.7.clone.rows_ref) | copy-start | bytes 12292
  1.7 0.9 %copy-start.1 = (f32[3,4,8,256]{3,2,1,0:T(8,128)S(1)}, f32[3,4,8,256]{3,2,1,0:T(8,128)}, u32[]{:S(2)}) copy-start(f32[3,4,8,256]{3,2,1,0:T(8,128)} %strengths_ref.1) | copy-start | bytes 294916
  5.5 3.4 %copy-start.3 = (s32[724]{0:T(1024)S(1)}, s32[724]{0:T(1024)}, u32[]{:S(2)}) copy-start(s32[724]{0:T(1024)} %constant.8.clone.table_ref.slot_ref) | copy-start | bytes 8692
  5.5 28.0 %collective-permute-start = (f32[264,128]{1,0:T(8,128)S(1)}, f32[264,128]{1,0:T(8,128)S(1)}, u32[]{:S(2)}, u32[]{:S(2)}) collective-permute-start(f32[264,128]{1,0:T(8,128)S(1)} %get-tuple-element.14), channel_id=1, source_target_pairs={{28,0},{0,4},{4,8},{8,12},{12,16},{16,20},{20,24},{24,28},{29,1},{... | collective-permute-start | bytes 405512 | tf_op jit(solution)/shard_map/ppermute | solution.py:794
  6.0 27.5 %collective-permute-start.1 = (f32[264,128]{1,0:T(8,128)S(1)}, f32[264,128]{1,0:T(8,128)S(1)}, u32[]{:S(2)}, u32[]{:S(2)}) collective-permute-start(f32[264,128]{1,0:T(8,128)S(1)} %get-tuple-element.15), channel_id=1, source_target_pairs={{4,0},{8,4},{12,8},{16,12},{20,16},{24,20},{28,24},{0,28},{5,1},{9... | collective-permute-start | bytes 405512 | tf_op jit(solution)/shard_map/ppermute | solution.py:794
  33.6 15.8 %collective-permute-start.4 = (f32[72,128]{1,0:T(8,128)S(1)}, f32[72,128]{1,0:T(8,128)S(1)}, u32[]{:S(2)}, u32[]{:S(2)}) collective-permute-start(f32[72,128]{1,0:T(8,128)S(1)} %get-tuple-element.20), channel_id=1, source_target_pairs={{2,0},{3,1},{0,2},{1,3},{6,4},{7,5},{4,6},{5,7},{10,8},{11,9},{8,1... | collective-permute-start | bytes 110600 | tf_op jit(solution)/shard_map/ppermute | solution.py:794
  37.0 12.4 %collective-permute-start.2 = (f32[324,128]{1,0:T(8,128)S(1)}, f32[324,128]{1,0:T(8,128)S(1)}, u32[]{:S(2)}, u32[]{:S(2)}) collective-permute-start(f32[324,128]{1,0:T(8,128)S(1)} %get-tuple-element.18), channel_id=1, source_target_pairs={{3,0},{0,1},{1,2},{2,3},{7,4},{4,5},{5,6},{6,7},{11,8},{8,9},{9,10... | collective-permute-start | bytes 497672 | tf_op jit(solution)/shard_map/ppermute | solution.py:794
  38.6 10.9 %collective-permute-start.3 = (f32[324,128]{1,0:T(8,128)S(1)}, f32[324,128]{1,0:T(8,128)S(1)}, u32[]{:S(2)}, u32[]{:S(2)}) collective-permute-start(f32[324,128]{1,0:T(8,128)S(1)} %get-tuple-element.19), channel_id=1, source_target_pairs={{1,0},{2,1},{3,2},{0,3},{5,4},{6,5},{7,6},{4,7},{9,8},{10,9},{11,1... | collective-permute-start | bytes 497672 | tf_op jit(solution)/shard_map/ppermute | solution.py:794
  49.5 9.7 %collective-permute-start.6 = (f32[288,128]{1,0:T(8,128)S(1)}, f32[288,128]{1,0:T(8,128)S(1)}, u32[]{:S(2)}, u32[]{:S(2)}) collective-permute-start(f32[288,128]{1,0:T(8,128)S(1)} %pad_maximum_fusion), channel_id=1, source_target_pairs={{20,0},{24,4},{28,8},{0,12},{4,16},{8,20},{12,24},{16,28},{21,1},{... | collective-permute-start | bytes 442376 | tf_op jit(solution)/shard_map/ppermute | solution.py:794
  49.5 9.6 %collective-permute-start.5 = (f32[288,128]{1,0:T(8,128)S(1)}, f32[288,128]{1,0:T(8,128)S(1)}, u32[]{:S(2)}, u32[]{:S(2)}) collective-permute-start(f32[288,128]{1,0:T(8,128)S(1)} %pad_maximum_fusion), channel_id=1, source_target_pairs={{12,0},{16,4},{20,8},{24,12},{28,16},{0,20},{4,24},{8,28},{13,1},{... | collective-permute-start | bytes 442376 | tf_op jit(solution)/shard_map/ppermute | solution.py:794
